TPU v7x, 32 devices: a whole 2x2x4 slice. The times are simulated.
32 devices in a mesh: leaf: 8 (over z, core), vec: 4 (over y, x).
Axes of the slice: x: 2, y: 2, z: 4, core: 2. Of those that a mesh axis runs over, the one named last changes fastest.
Arguments:
- points: bfloat16 [128, 3, 256], P('leaf'), may hold values from 0 to 1
- probe_vectors: bfloat16 [128, 256, 256], P('leaf', 'vec'), may hold values from -6 to 6
- neighbours: int32 [128, 16], P('leaf'), may hold values from -1 to 127, as said below
- leaf_pivots: int32 [128, 64], P('leaf'), may hold values from 0 to 255, as said below
- leaf_inverse: float32 [128, 64, 64], P('leaf'), as said below
- local_pivots: int32 [120, 64], P('leaf'), may hold values from 0 to 127, as said below
- local_inverse: float32 [120, 64, 64], P('leaf'), as said below
- upper_pivots: int32 [7, 64], replicated, may hold values from 0 to 127, as said below
- upper_inverse: float32 [7, 64, 64], replicated, as said below
Outputs:
- leaf_interp: float32 [128, 256, 64], P('leaf')
- local_interp: float32 [120, 128, 64], P('leaf')
- upper_interp: float32 [8, 3, 128, 64], P('leaf')
- top_sketch: float32 [8, 256, 64], P('leaf', 'vec')
Inputs may be any that keep to these rules, and one draw needn't show every extreme that they name: Entry 0 of neighbours[i] is i; then come distinct clusters j != i with |j - i| <= 16, then -1 to the end. The first cluster of each group of 16 lists the cluster before it in entry 1, and the last one lists the cluster after it there, where those exist. A list holds at least 4 clusters, and some lists hold 16. `leaf_pivots`: each row holds 64 distinct row numbers. `local_pivots`: each row holds 64 distinct row numbers. `upper_pivots`: each row holds 64 distinct row numbers. `leaf_inverse`: diagonal entries lie in 0.5 to 1.5. `local_inverse`: diagonal entries lie in 0.5 to 1.5. `upper_inverse`: diagonal entries lie in 0.5 to 1.5.
All inputs are finite; a program needn't handle non-finite values.
Results may differ from a plain program's by a relative error of at most 0.0013.
Values may be sent and summed in bfloat16 or wider, within the bound.
No kernel may reach another device: no remote copies, remote signals or barrier semaphores. Data moves between devices by JAX's collectives and lax.ppermute only.
A program may use at most 64 MiB of HBM per device.

v0:
```python
import functools

import jax
import jax.numpy as jnp
from jax import lax
from jax.experimental import pallas as pl
from jax.experimental.pallas import tpu as pltpu
from jax.sharding import PartitionSpec as P

UPL = 3

SOFTEN = 0.0009
EPSILON = 1e-06
FLIGHT = 8
DEPTH = 128
CHUNK = 256
LATE = (2,)
ROUND_FLOPS = 400_000_000
VMEM_BYTES = 20 * 1024 * 1024
VMEM = pltpu.MemorySpace.VMEM
SMEM = pltpu.MemorySpace.SMEM


def nt(a, b):
    return lax.dot_general(a, b, (((1,), (1,)), ((), ())), preferred_element_type=jnp.float32)


def nn(a, b):
    return lax.dot_general(a, b, (((1,), (0,)), ((), ())), preferred_element_type=jnp.float32)


def split(a):
    high = a.astype(jnp.bfloat16)
    low = (a - high.astype(jnp.float32)).astype(jnp.bfloat16)
    return high, low


def stacked_split(a):
    high, low = split(a)
    return jnp.concatenate([high, low], axis=0)


def halves(a):
    rows = a.shape[0] // 2
    return a[:rows] + a[rows:]


def coordinates(points, extra):
    row = lax.broadcasted_iota(jnp.int32, (8, points.shape[1]), 0)
    padded = jnp.concatenate(
        [points, jnp.full((5, points.shape[1]), 0.5, jnp.float32)], axis=0
    )
    centred = padded - 0.5
    high, low = [part.astype(jnp.float32) for part in split(centred)]
    norm = jnp.sum(centred * centred, axis=0, keepdims=True) + extra
    first, rest = [part.astype(jnp.float32) for part in split(norm)]
    second, third = [part.astype(jnp.float32) for part in split(norm - first)]
    norms = jnp.where(row == 0, first, jnp.where(row == 1, second, jnp.where(row == 2, third, 0.0)))
    return high, low, norms, jnp.where(row < 3, 1.0, 0.0)


def far_features(points):
    high, low, norm, one = coordinates(points, SOFTEN)
    vacant = jnp.zeros((DEPTH - 48, points.shape[1]), jnp.float32)
    return jnp.concatenate(
        [-2.0 * high, -2.0 * low, -2.0 * high, -2.0 * low, one, norm, vacant], axis=0
    ).astype(jnp.bfloat16)


def near_features(points):
    high, low, norm, one = coordinates(points, 0.0)
    vacant = jnp.zeros((DEPTH - 48, points.shape[1]), jnp.float32)
    return jnp.transpose(
        jnp.concatenate([high, high, low, low, norm, one, vacant], axis=0)
    ).astype(jnp.bfloat16)


def add_blocks(share, tiers, base, wanted, nb_ref, far, vectors, near, total, tiles, codes):
    me = lax.axis_index("vec")
    count, slots = nb_ref.shape
    first = lax.axis_index("leaf") * count
    flight, size = tiles.shape[0], tiles.shape[1]
    idle = count * 64

    for way in range(flight):
        codes[way] = idle
    filled = jnp.int32(flight)
    for tier in tiers:
        for part in range(share):
            cluster = (me ^ tier) * share + part
            shift = cluster * 64 + count - base - first
            for slot in range(slots):
                listed = nb_ref[cluster, slot]
                codes[filled] = listed + shift
                filled += wanted(listed, first, count).astype(jnp.int32)
    for way in range(flight):
        codes[filled + way] = idle
    tiles[...] = jnp.zeros(tiles.shape, tiles.dtype)

    def multiply(code, tile):
        row = code // 64
        total[row] = total[row] + nt(vectors(code % 64), tile[...])

    def evaluate(code, tile):
        row = code // 64
        position = code % 64
        for top in range(0, size, CHUNK):
            distance = nn(near[row, top : top + CHUNK, :], far[position])
            tile[top : top + CHUNK, :] = lax.rsqrt(distance).astype(jnp.bfloat16)

    def step(index, carry):
        for way in range(flight):
            multiply(codes[index * flight + way], tiles.at[way])
            evaluate(codes[(index + 1) * flight + way], tiles.at[way])
        return carry

    steps = (filled - 1) // flight
    lax.fori_loop(0, steps, step, 0)
    for way in range(flight):
        multiply(codes[steps * flight + way], tiles.at[way])


def inside(listed, first, count):
    return (listed >= first) & (listed < first + count)


def outside(listed, first, count):
    return (listed >= 0) & ((listed < first) | (listed >= first + count))


def anywhere(listed, first, count):
    return listed >= 0


def joined_points(joined, count):
    points = joined[joined.shape[0] - 3 * count :, :].astype(jnp.float32)
    return [points[3 * cluster : 3 * cluster + 3] for cluster in range(count)]


def own_kernel(share, tiers, nb_ref, joined, total, far, near, tiles, codes):
    count, columns = far.shape[0], total.shape[1]
    for cluster, points in enumerate(joined_points(joined, count)):
        far[cluster] = far_features(points)
        near[cluster] = near_features(points)
    near[count] = near[0]
    total[...] = jnp.zeros(total.shape, total.dtype)

    def vectors(place):
        return joined[pl.ds(pl.multiple_of(place * columns, columns), columns), :]

    add_blocks(share, tiers, count, inside, nb_ref, far, vectors, near, total, tiles, codes)


def halo_kernel(share, tiers, nb_ref, joined, inner, outer, own_far, near, start, *refs):
    outs = refs[: len(tiers)]
    far, vectors, total, tiles, codes = refs[len(tiers) :]
    count, columns = own_far.shape[0], start.shape[1]
    me = lax.axis_index("vec")
    odd = lax.axis_index("leaf") & 1
    for place, source in ((2 * odd, outer), (2 - 2 * odd, inner), (1, joined)):
        for cluster in range(count):
            vectors[place * count + cluster] = source[cluster * columns : (cluster + 1) * columns, :]
        if source is joined:
            far[count : 2 * count] = own_far[...]
            continue
        for cluster, points in enumerate(joined_points(source, count)):
            far[place * count + cluster] = far_features(points)
    total[...] = start[...]

    def read(place):
        return vectors[place]

    add_blocks(share, tiers, 0, outside, nb_ref, far, read, near, total, tiles, codes)
    for tier, out in zip(tiers, outs):
        part = total[pl.ds((me ^ tier) * share, share)]
        out[...] = (part * 0.015625).astype(out.dtype)


def kept_kernel(share, nb_ref, far, vectors, near, out, total, tiles, codes):
    mine = pl.ds(lax.axis_index("vec") * share, share)
    total[mine] = jnp.zeros((share,) + total.shape[1:], total.dtype)

    def read(place):
        return vectors[place]

    add_blocks(share, (0,), 0, anywhere, nb_ref, far, read, near, total, tiles, codes)
    out[...] = (total[mine] * 0.015625).astype(out.dtype)


def join_kernel(points, probe, joined):
    count, columns, _ = probe.shape
    for cluster in range(count):
        joined[cluster * columns : (cluster + 1) * columns, :] = probe[cluster]
    joined[count * columns :, :] = jnp.concatenate(
        [points[cluster].astype(jnp.float32) for cluster in range(count)], axis=0
    ).astype(joined.dtype)


def near_call(body, outs, scratch, operands, rows, per_row):
    nb, size = operands[0], outs[0].shape[-1]
    blocks = rows * per_row
    return pl.pallas_call(
        body,
        out_shape=outs,
        in_specs=[pl.BlockSpec(memory_space=SMEM)]
        + [pl.BlockSpec(memory_space=VMEM)] * (len(operands) - 1),
        out_specs=[pl.BlockSpec(memory_space=VMEM)] * len(outs),
        scratch_shapes=scratch
        + [
            pltpu.VMEM((FLIGHT, size, size), jnp.bfloat16),
            pltpu.SMEM((rows * nb.shape[1] + 2 * FLIGHT,), jnp.int32),
        ],
        compiler_params=pltpu.CompilerParams(vmem_limit_bytes=VMEM_BYTES),
        cost_estimate=pl.CostEstimate(
            flops=blocks * size * size * 256,
            bytes_accessed=sum(o.size * o.dtype.itemsize for o in operands),
            transcendentals=blocks * size * size,
        ),
    )(*operands)


def pivot_factor(pivots, inverse, width):
    chosen = (
        lax.broadcasted_iota(jnp.int32, (width, pivots.shape[1]), 0) == pivots
    ).astype(jnp.bfloat16)
    return nt(stacked_split(jnp.transpose(inverse)), chosen).astype(jnp.bfloat16)


def leaf_node(sketch, factor):
    wide = sketch.astype(jnp.float32)
    mean_sq = jnp.sum(wide * wide, keepdims=True) / (sketch.shape[0] * sketch.shape[1]) + EPSILON
    scale = 1.0 / (sketch.shape[0] * mean_sq)
    picked = halves(nt(factor, sketch))
    raw = halves(nn(stacked_split(picked), sketch))
    interp = raw * scale
    upward = halves(nt(stacked_split(raw), sketch)) * (scale * lax.rsqrt(mean_sq))
    return interp, upward


def tree_node(sketch, factor):
    width, columns = sketch.shape
    mean_sq = jnp.sum(sketch * sketch, keepdims=True) / (width * columns) + EPSILON
    scale = 1.0 / (columns * mean_sq)
    parts = stacked_split(sketch)
    picked = halves(nn(jnp.concatenate([factor, factor], axis=1), parts))
    raw = halves(nt(stacked_split(picked), parts))
    raw = raw[:, :width] + raw[:, width:]
    interp = raw * scale
    both = stacked_split(raw)
    upward = halves(nn(jnp.concatenate([both, both], axis=1), parts)) * (scale * lax.rsqrt(mean_sq))
    return interp, upward


def own_nodes(share, group, me):
    rows, level_first, nodes = [], 0, share // 2
    while nodes >= 1:
        rows += [level_first + me * nodes + node for node in range(nodes)]
        level_first += (group // share) * nodes
        nodes //= 2
    return rows


def factor_kernel(
    share,
    leaf_total,
    leaf_pivots,
    leaf_inverse,
    local_pivots,
    local_inverse,
    upper_pivots,
    upper_inverse,
    _,
    leaf_out,
    own_out,
    group_out,
    upper_out,
):
    me = lax.axis_index("vec")
    group = leaf_pivots.shape[0]

    def put(out, index, pivots, inverse, row):
        out[index] = pivot_factor(pivots[pl.ds(row, 1), :], inverse[row], out.shape[2])

    for cluster in range(share):
        put(leaf_out, cluster, leaf_pivots, leaf_inverse, me * share + cluster)
    for index, row in enumerate(own_nodes(share, group, me)):
        put(own_out, index, local_pivots, local_inverse, row)
    for index in range(group // share - 1):
        put(group_out, index, local_pivots, local_inverse, group - group // share + index)
    heap_first = 0
    for tier in range(UPL):
        node = heap_first + (lax.axis_index("leaf") >> (tier + 1))
        put(upper_out, tier, upper_pivots, upper_inverse, node)
        heap_first += leaf_total >> (tier + 1)


def device_kernel(share, group, rank, own, *refs):
    parts = group // share
    arrived, refs = refs[: parts - 1], refs[parts - 1 :]
    leaf_factors, own_factors, pack, up_out, sketch, ups = refs
    me = lax.axis_index("vec")
    columns = own.shape[1]
    width = 2 * rank
    for tier, piece in enumerate((own,) + tuple(arrived)):
        place = pl.ds(pl.multiple_of((me ^ tier) * columns, columns), columns)
        for cluster in range(share):
            sketch[cluster, place, :] = piece[cluster]
    for cluster in range(share):
        interp, upward = leaf_node(sketch[cluster], leaf_factors[cluster])
        pack[cluster * rank : (cluster + 1) * rank, :] = interp
        ups[cluster * rank : (cluster + 1) * rank, :] = upward
    nodes, packed = share // 2, 0
    while nodes >= 1:
        results = []
        for node in range(nodes):
            interp, upward = tree_node(
                ups[2 * node * rank : 2 * (node + 1) * rank, :], own_factors[packed]
            )
            for lane, source, top, height in pack_places(packed, share, rank):
                pack[top : top + height, lane : lane + width] = interp[source : source + height]
            results.append(upward)
            packed += 1
        for node, upward in enumerate(results):
            ups[node * rank : (node + 1) * rank, :] = upward
        nodes //= 2
    up_out[...] = ups[0:rank, :]


def pack_places(index, share, rank):
    top = share * rank + index // 2 * rank
    if index < share - 2:
        return [(index % 2 * 2 * rank, 0, top, rank)]
    return [(0, 0, top, rank // 2), (2 * rank, rank // 2, top, rank // 2)]


def group_kernel(share, group, rank, own, *refs):
    parts = group // share
    arrived, refs = refs[: parts - 1], refs[parts - 1 :]
    factors, interps, up_out, ups = refs
    me = lax.axis_index("vec")
    for tier, piece in enumerate((own,) + tuple(arrived)):
        ups[pl.ds(pl.multiple_of((me ^ tier) * rank, rank), rank), :] = piece[...]
    done = 0
    nodes = parts // 2
    while nodes >= 1:
        results = []
        for node in range(nodes):
            interp, upward = tree_node(
                ups[2 * node * rank : 2 * (node + 1) * rank, :], factors[done]
            )
            interps[done * rank : (done + 1) * rank, :] = interp
            results.append(upward)
            done += 1
        for node, upward in enumerate(results):
            ups[node * rank : (node + 1) * rank, :] = upward
        nodes //= 2
    up_out[...] = ups[0:rank, :]


def upper_node(tier, rank, own, arrived, factors, ups):
    side = (lax.axis_index("leaf") >> tier) & 1
    ups[pl.ds(pl.multiple_of(side * rank, rank), rank), :] = own[...]
    ups[pl.ds(pl.multiple_of((1 - side) * rank, rank), rank), :] = arrived[...]
    return tree_node(ups[...], factors[tier])


def upper_kernel(tier, rank, own, arrived, factors, interp_out, up_out, ups):
    interp, upward = upper_node(tier, rank, own, arrived, factors, ups)
    interp_out[...] = interp
    up_out[...] = upward


def finish_kernel(tier, share, group, rank, own, arrived, factors, *refs):
    parts = group // share
    earlier, refs = refs[:tier], refs[tier:]
    packs, refs = refs[:parts], refs[parts:]
    joined, interps, top, leaf_out, local_out, ups, turned, sems = refs
    me = lax.axis_index("vec")
    copies = []

    def put(source, target):
        copies.append(pltpu.make_async_copy(source, target, sems.at[len(copies)]))
        copies[-1].start()

    def rows_at(start, height):
        return pl.ds(pl.multiple_of(start, height), height)

    for flip, piece in enumerate(packs):
        device = me ^ flip
        leaves = share * rank
        put(piece.at[0:leaves], leaf_out.at[rows_at(device * leaves, leaves)])
        for index, row in enumerate(own_nodes(share, group, device)):
            for lane, source, start, height in pack_places(index, share, rank):
                put(
                    piece.at[start : start + height, lane : lane + 2 * rank],
                    local_out.at[rows_at(row * rank + source, height)],
                )
    put(joined, local_out.at[(group - parts) * rank : (group - 1) * rank])

    interp, upward = upper_node(tier, rank, own, arrived, factors, ups)
    for index, ref in enumerate(earlier):
        interps[index] = ref[...]
    interps[tier] = interp
    turned[...] = jnp.transpose(upward)
    columns = top.shape[0]
    place = pl.multiple_of(me * columns, columns)
    top[...] = turned[pl.ds(place, columns), :]
    for copy in copies:
        copy.wait()


def call(body, outs, scratch, operands, flops=0, anywhere_in=0, anywhere_out=0):
    fixed = pl.BlockSpec(memory_space=VMEM)
    free = pl.BlockSpec(memory_space=pl.ANY)
    return pl.pallas_call(
        body,
        out_shape=outs,
        in_specs=[fixed] * (len(operands) - anywhere_in) + [free] * anywhere_in,
        out_specs=[fixed] * (len(outs) - anywhere_out) + [free] * anywhere_out,
        scratch_shapes=scratch,
        compiler_params=pltpu.CompilerParams(vmem_limit_bytes=VMEM_BYTES),
        cost_estimate=pl.CostEstimate(
            flops=flops, bytes_accessed=sum(o.size * o.dtype.itemsize for o in operands), transcendentals=0
        ),
    )(*operands)


def f32(*shape):
    return jax.ShapeDtypeStruct(shape, jnp.float32)


def on_device(
    points,
    probe_vectors,
    neighbours,
    leaf_pivots,
    leaf_inverse,
    local_pivots,
    local_inverse,
    upper_pivots,
    upper_inverse,
):
    group, columns, size = probe_vectors.shape
    rank = leaf_pivots.shape[1]
    leaf_total = lax.axis_size("leaf")
    parts = lax.axis_size("vec")
    share = group // parts
    total_columns = columns * parts

    joined = call(
        join_kernel,
        [jax.ShapeDtypeStruct((group * (columns + 3), size), jnp.bfloat16)],
        [],
        [points, probe_vectors],
    )[0]
    swaps = []
    for odd in (0, 1):
        pairs = [(i, i + 1) for i in range(odd, leaf_total - 1, 2)]
        swaps.append(lax.ppermute(joined, "leaf", pairs + [(j, i) for i, j in pairs]))
    inner, outer = swaps

    def vec_send(array, tier):
        return lax.ppermute(array, "vec", [(i, i ^ tier) for i in range(parts)])

    away = list(range(parts - 1, 0, -1))
    sent_rows = (parts - 1) * share

    def bf16(*shape):
        return jax.ShapeDtypeStruct(shape, jnp.bfloat16)

    started, own_far, near = near_call(
        functools.partial(own_kernel, share, away),
        [f32(group + 1, columns, size), bf16(group, DEPTH, size), bf16(group + 1, size, DEPTH)],
        [],
        [neighbours, joined],
        sent_rows,
        6,
    )
    *sent, far, vectors = near_call(
        functools.partial(halo_kernel, share, away),
        [bf16(share, columns, size)] * len(away)
        + [bf16(3 * group, DEPTH, size), bf16(3 * group, columns, size)],
        [pltpu.VMEM((group + 1, columns, size), jnp.float32)],
        [neighbours, joined, inner, outer, own_far, near, started],
        sent_rows,
        6,
    )
    arrived = {tier: vec_send(array, tier) for tier, array in zip(away, sent)}
    kept = near_call(
        functools.partial(kept_kernel, share),
        [bf16(share, columns, size)],
        [pltpu.VMEM((group + 1, columns, size), jnp.float32)],
        [neighbours, far, vectors, near],
        share,
        12,
    )[0]

    width = 2 * rank
    leaf_factors, own_factors, group_factors, upper_factors = call(
        functools.partial(factor_kernel, share, leaf_total),
        [
            bf16(share, width, size),
            bf16(max(1, share - 1), width, width),
            bf16(parts - 1, width, width),
            bf16(UPL, width, width),
        ],
        [],
        [
            leaf_pivots,
            leaf_inverse,
            local_pivots,
            local_inverse,
            upper_pivots,
            upper_inverse,
            kept,
        ],
        anywhere_in=1,
    )
    pack, own_up = call(
        functools.partial(device_kernel, share, group, rank),
        [f32((3 * share - 1) * rank // 2, size), f32(rank, total_columns)],
        [
            pltpu.VMEM((share, total_columns, size), jnp.bfloat16),
            pltpu.VMEM((share * rank, total_columns), jnp.float32),
        ],
        [kept] + [arrived[tier] for tier in range(1, parts)] + [leaf_factors, own_factors],
    )
    near_ups = [vec_send(own_up, tier) for tier in range(1, parts)]
    joined, own_up = call(
        functools.partial(group_kernel, share, group, rank),
        [f32((parts - 1) * rank, width), f32(rank, total_columns)],
        [pltpu.VMEM((parts * rank, total_columns), jnp.float32)],
        [own_up] + near_ups + [group_factors],
    )
    later, own_up = lax.optimization_barrier((pack, own_up))
    late = LATE if parts > max(LATE) else ()
    others = [vec_send(later if tier in late else pack, tier) for tier in range(1, parts)]

    maps = []
    for tier in range(UPL):
        partner = lax.ppermute(own_up, "leaf", [(i, i ^ (1 << tier)) for i in range(leaf_total)])
        operands = [own_up, partner, upper_factors]
        ups = pltpu.VMEM((width, total_columns), jnp.float32)
        if tier < UPL - 1:
            interp, own_up = call(
                functools.partial(upper_kernel, tier, rank),
                [f32(rank, width), f32(rank, total_columns)],
                [ups],
                operands,
                flops=ROUND_FLOPS,
            )
            maps.append(interp)
    upper_map, top, leaf_map, local_map = call(
        functools.partial(finish_kernel, UPL - 1, share, group, rank),
        [
            f32(UPL, rank, width),
            f32(columns, rank),
            f32(group * rank, size),
            f32((group - 1) * rank, width),
        ],
        [
            ups,
            pltpu.VMEM((total_columns, rank), jnp.float32),
            pltpu.SemaphoreType.DMA((parts * (share + 1) + 1,)),
        ],
        operands + maps + [pack] + others + [joined],
        flops=ROUND_FLOPS,
        anywhere_in=parts + 1,
        anywhere_out=2,
    )
    return (
        jnp.swapaxes(leaf_map.reshape(group, rank, size), 1, 2),
        jnp.swapaxes(local_map.reshape(group - 1, rank, width), 1, 2),
        jnp.swapaxes(upper_map, 1, 2)[None],
        top[None],
    )


def solution(mesh):
    placed = (
        P("leaf", None, None),
        P("leaf", "vec", None),
        P("leaf", None),
        P("leaf", None),
        P("leaf", None, None),
        P("leaf", None),
        P("leaf", None, None),
        P(),
        P(),
    )
    return jax.shard_map(
        on_device,
        mesh=mesh,
        in_specs=placed,
        out_specs=(
            P("leaf", None, None),
            P("leaf", None, None),
            P("leaf", None, None, None),
            P("leaf", "vec", None),
        ),
        check_vma=False,
    )
```

profile of v0, /device:TPU:0, one launch (start us, length us, event | category | flops | bytes accessed | tf_op | source)
XLA Modules:
  0.0 61.1 jit_solution(13999580248240677337)
XLA Ops:
  0.6 0.8 %copy.13.points = bf16[16,3,256]{2,1,0:T(4,128)(2,1)S(1)} copy(bf16[16,3,256]{2,0,1:T(8,128)(2,1)} %param.9) | data formatting | bytes 49152 | tf_op args[0]
  1.4 0.0 copy-start
  1.4 1.0 %copy-done = bf16[16,64,256]{2,1,0:T(8,128)(2,1)S(1)} copy-done((bf16[16,64,256]{2,1,0:T(8,128)(2,1)S(1)}, bf16[16,64,256]{2,1,0:T(8,128)(2,1)}, u32[]{:S(2)}) %copy-start) | copy-done | bytes 524312
  2.5 0.7 %collective-permute-start.1 = (bf16[1072,256]{1,0:T(8,128)(2,1)S(1)}, bf16[1072,256]{1,0:T(8,128)(2,1)S(1)}, u32[]{:S(2)}, u32[]{:S(2)}) collective-permute-start(bf16[1072,256]{1,0:T(8,128)(2,1)S(1)} %shard_map.120.joined), channel_id=1, source_target_pairs={{4,8},{12,16},{20,24},{8,4},{16,12},{24,20},{5,9},{13,17},{21,25},... | collective-permute-start | bytes 1646600 | tf_op jit(solution)/shard_map/ppermute | solution.py:459
  3.2 4.4 %collective-permute-start = (bf16[1072,256]{1,0:T(8,128)(2,1)S(1)}, bf16[1072,256]{1,0:T(8,128)(2,1)S(1)}, u32[]{:S(2)}, u32[]{:S(2)}) collective-permute-start(bf16[1072,256]{1,0:T(8,128)(2,1)S(1)} %shard_map.120.joined), channel_id=1, source_target_pairs={{0,4},{8,12},{16,20},{24,28},{4,0},{12,8},{20,16},{28,24},{1,5},{9... | collective-permute-start | bytes 1646600 | tf_op jit(solution)/shard_map/ppermute | solution.py:459
  7.6 0.0 copy-start.4
  7.6 0.7 %copy-done.4 = s32[16,16]{1,0:T(8,128)S(1)} copy-done((s32[16,16]{1,0:T(8,128)S(1)}, s32[16,16]{1,0:T(8,128)}, u32[]{:S(2)}) %copy-start.4) | copy-done | bytes 1048
  8.3 7.1 %shard_map.121 = (f32[17,64,256]{2,1,0:T(8,128)S(1)}, bf16[16,128,256]{2,1,0:T(8,128)(2,1)S(1)}, bf16[17,256,128]{2,1,0:T(8,128)(2,1)S(1)}) custom-call(s32[16,16]{1,0:T(8,128)S(1)} %copy-done.4, bf16[1072,256]{1,0:T(8,128)(2,1)S(1)} %shard_map.120.joined), custom_call_target="tpu_custom_call" | custom-call | flops 1207959552 | bytes 549888 | tf_op jit(solution)/shard_map/pallas_call | solution.py:202
  15.4 0.0 collective-permute-done.1.outer
  15.4 0.0 collective-permute-done.inner
  15.5 5.6 %shard_map.122 = (bf16[4,64,256]{2,1,0:T(8,128)(2,1)S(1)}, bf16[4,64,256]{2,1,0:T(8,128)(2,1)S(1)}, bf16[4,64,256]{2,1,0:T(8,128)(2,1)S(1)}, bf16[48,128,256]{2,1,0:T(8,128)(2,1)S(1)}, bf16[48,64,256]{2,1,0:T(8,128)(2,1)S(1)}) custom-call(s32[16,16]{1,0:T(8,128)S(1)} %copy-done.4, bf16[1072,256]{1,0:T(8,128)(2,1)S(1)} %shard_map.120.joined, ...), custom_call_target="tpu_custom_call" | custom-call | flops 1207959552 | bytes 4924416 | tf_op jit(solution)/shard_map/pallas_call | solution.py:202
  21.1 2.6 %collective-permute-start.2 = (bf16[4,64,256]{2,1,0:T(8,128)(2,1)S(1)}, bf16[4,64,256]{2,1,0:T(8,128)(2,1)S(1)}, u32[]{:S(2)}, u32[]{:S(2)}) collective-permute-start(bf16[4,64,256]{2,1,0:T(8,128)(2,1)S(1)} %get-tuple-element.35), channel_id=1, source_target_pairs={{0,1},{1,0},{2,3},{3,2},{4,5},{5,4},{6,7},{7,6},{8,9},{9,8},{10,11... | collective-permute-start | bytes 393224 | tf_op jit(solution)/shard_map/ppermute | solution.py:463
  23.7 1.5 %collective-permute-start.3 = (bf16[4,64,256]{2,1,0:T(8,128)(2,1)S(1)}, bf16[4,64,256]{2,1,0:T(8,128)(2,1)S(1)}, u32[]{:S(2)}, u32[]{:S(2)}) collective-permute-start(bf16[4,64,256]{2,1,0:T(8,128)(2,1)S(1)} %get-tuple-element.36), channel_id=1, source_target_pairs={{0,2},{1,3},{2,0},{3,1},{4,6},{5,7},{6,4},{7,5},{8,10},{9,11},{10,... | collective-permute-start | bytes 393224 | tf_op jit(solution)/shard_map/ppermute | solution.py:463
  25.2 0.0 collective-permute-start.4
  25.2 0.0 copy-start.1
  25.2 0.0 copy-start.2
  25.2 0.0 copy-start.3
  25.2 0.0 copy-start.5
  25.2 0.0 copy-start.6
  25.2 0.0 copy-start.7
  25.2 5.6 %shard_map.123._.own = bf16[4,64,256]{2,1,0:T(8,128)(2,1)S(1)} custom-call(s32[16,16]{1,0:T(8,128)S(1)} %copy-done.4, bf16[48,128,256]{2,1,0:T(8,128)(2,1)S(1)} %get-tuple-element.33.far, bf16[48,64,256]{2,1,0:T(8,128)(2,1)S(1)} %get-tuple-element.34.vectors, bf16[17,256,128]{2,1,0:T(8,128)(2,1)S(1)} %get-tuple-element.31.near), custom_call_target="tpu_custom_call" | custom-call | flops 805306368 | bytes 5833728 | tf_op jit(solution)/shard_map/pallas_call | solution.py:202
  30.9 0.0 copy-done.1
  30.9 0.0 copy-done.2
  30.9 0.0 copy-done.3
  30.9 0.0 copy-done.5
  30.9 0.0 copy-done.6
  30.9 0.0 copy-done.7
  30.9 0.5 shard_map.124
  31.4 0.0 collective-permute-done.2.refs_0_
  31.4 0.0 collective-permute-done.3.refs_1_
  31.4 0.0 collective-permute-done.4.refs_2_
  31.4 2.0 %shard_map.125 = (f32[352,256]{1,0:T(8,128)S(1)}, f32[64,256]{1,0:T(8,128)S(1)}) custom-call(bf16[4,64,256]{2,1,0:T(8,128)(2,1)S(1)} %shard_map.123._.own, bf16[4,64,256]{2,1,0:T(8,128)(2,1)S(1)} %collective-permute-done.2.refs_0_, bf16[4,64,256]{2,1,0:T(8,128)(2,1)S(1)} %collective-permute-done.3.refs_1_, ...), custom_call_target="tpu_custom_call" | custom-call | bytes 884736 | tf_op jit(solution)/shard_map/pallas_call | solution.py:415
  33.5 1.9 %collective-permute-start.7 = (f32[64,256]{1,0:T(8,128)S(1)}, f32[64,256]{1,0:T(8,128)S(1)}, u32[]{:S(2)}, u32[]{:S(2)}) collective-permute-start(f32[64,256]{1,0:T(8,128)S(1)} %get-tuple-element.41.own), channel_id=1, source_target_pairs={{0,3},{1,2},{2,1},{3,0},{4,7},{5,6},{6,5},{7,4},{8,11},{9,10},{10,... | collective-permute-start | bytes 196616 | tf_op jit(solution)/shard_map/ppermute | solution.py:463
  35.4 0.3 collective-permute-start.6
  35.7 1.4 %collective-permute-start.5 = (f32[64,256]{1,0:T(8,128)S(1)}, f32[64,256]{1,0:T(8,128)S(1)}, u32[]{:S(2)}, u32[]{:S(2)}) collective-permute-start(f32[64,256]{1,0:T(8,128)S(1)} %get-tuple-element.41.own), channel_id=1, source_target_pairs={{0,1},{1,0},{2,3},{3,2},{4,5},{5,4},{6,7},{7,6},{8,9},{9,8},{10,11... | collective-permute-start | bytes 196616 | tf_op jit(solution)/shard_map/ppermute | solution.py:463
  37.0 1.8 %collective-permute-start.13 = (f32[352,256]{1,0:T(8,128)S(1)}, f32[352,256]{1,0:T(8,128)S(1)}, u32[]{:S(2)}, u32[]{:S(2)}) collective-permute-start(f32[352,256]{1,0:T(8,128)S(1)} %get-tuple-element.50.refs_2_), channel_id=1, source_target_pairs={{0,3},{1,2},{2,1},{3,0},{4,7},{5,6},{6,5},{7,4},{8,11},{9,10},{10,... | collective-permute-start | bytes 1081352 | tf_op jit(solution)/shard_map/ppermute | solution.py:463
  38.9 0.9 %collective-permute-start.11 = (f32[352,256]{1,0:T(8,128)S(1)}, f32[352,256]{1,0:T(8,128)S(1)}, u32[]{:S(2)}, u32[]{:S(2)}) collective-permute-start(f32[352,256]{1,0:T(8,128)S(1)} %get-tuple-element.50.refs_2_), channel_id=1, source_target_pairs={{0,1},{1,0},{2,3},{3,2},{4,5},{5,4},{6,7},{7,6},{8,9},{9,8},{10,11... | collective-permute-start | bytes 1081352 | tf_op jit(solution)/shard_map/ppermute | solution.py:463
  39.7 0.0 collective-permute-done.7.refs_2_
  39.7 5.5 %collective-permute-done.6.refs_1_ = f32[64,256]{1,0:T(8,128)S(1)} collective-permute-done((f32[64,256]{1,0:T(8,128)S(1)}, f32[64,256]{1,0:T(8,128)S(1)}, u32[]{:S(2)}, u32[]{:S(2)}) %collective-permute-start.6) | collective-permute-done | bytes 65568 | tf_op jit(solution)/shard_map/ppermute | solution.py:463
  45.2 0.0 collective-permute-done.5.refs_0_
  45.2 1.2 %shard_map.126 = (f32[192,128]{1,0:T(8,128)S(1)}, f32[64,256]{1,0:T(8,128)S(1)}) custom-call(f32[64,256]{1,0:T(8,128)S(1)} %get-tuple-element.41.own, f32[64,256]{1,0:T(8,128)S(1)} %collective-permute-done.5.refs_0_, f32[64,256]{1,0:T(8,128)S(1)} %collective-permute-done.6.refs_1_, f32[64,256]{1,0:T(8,128)S(1)} %collective-permute-done.7.refs_2_, ...), custom_call_target="tpu_custom_call" | custom-call | bytes 360448 | tf_op jit(solution)/shard_map/pallas_call | solution.py:415
  46.4 0.1 collective-permute-start.12
  46.5 0.1 collective-permute-start.8
  46.6 1.2 %collective-permute-done.8.arrived = f32[64,256]{1,0:T(8,128)S(1)} collective-permute-done((f32[64,256]{1,0:T(8,128)S(1)}, f32[64,256]{1,0:T(8,128)S(1)}, u32[]{:S(2)}, u32[]{:S(2)}) %collective-permute-start.8) | collective-permute-done | bytes 65568 | tf_op jit(solution)/shard_map/ppermute | solution.py:541
  47.8 0.5 shard_map.127
  48.3 1.0 %collective-permute-start.9 = (f32[64,256]{1,0:T(8,128)S(1)}, f32[64,256]{1,0:T(8,128)S(1)}, u32[]{:S(2)}, u32[]{:S(2)}) collective-permute-start(f32[64,256]{1,0:T(8,128)S(1)} %get-tuple-element.46.own), channel_id=1, source_target_pairs={{0,8},{4,12},{8,0},{12,4},{16,24},{20,28},{24,16},{28,20},{1,9},{5... | collective-permute-start | bytes 196616 | tf_op jit(solution)/shard_map/ppermute | solution.py:541
  49.2 3.4 %collective-permute-done.9.arrived = f32[64,256]{1,0:T(8,128)S(1)} collective-permute-done((f32[64,256]{1,0:T(8,128)S(1)}, f32[64,256]{1,0:T(8,128)S(1)}, u32[]{:S(2)}, u32[]{:S(2)}) %collective-permute-start.9) | collective-permute-done | bytes 65568 | tf_op jit(solution)/shard_map/ppermute | solution.py:541
  52.6 0.5 shard_map.128
  53.1 0.1 collective-permute-start.10
  53.2 5.9 %collective-permute-done.10.arrived = f32[64,256]{1,0:T(8,128)S(1)} collective-permute-done((f32[64,256]{1,0:T(8,128)S(1)}, f32[64,256]{1,0:T(8,128)S(1)}, u32[]{:S(2)}, u32[]{:S(2)}) %collective-permute-start.10) | collective-permute-done | bytes 65568 | tf_op jit(solution)/shard_map/ppermute | solution.py:541
  59.0 0.0 collective-permute-done.13.refs_5_
  59.0 0.0 collective-permute-done.11.refs_3_
  59.0 0.0 collective-permute-done.12.refs_4_
  59.0 2.1 %shard_map.129 = (f32[3,64,128]{2,1,0:T(8,128)}, f32[64,64]{1,0:T(8,128)}, f32[1024,256]{1,0:T(8,128)}, f32[960,128]{1,0:T(8,128)}) custom-call(f32[64,256]{1,0:T(8,128)S(1)} %get-tuple-element.47.own, f32[64,256]{1,0:T(8,128)S(1)} %collective-permute-done.10.arrived, bf16[3,128,128]{2,1,0:T(8,128)(2,1)S(1)} %get-tuple-element.45.factors, ...), custom_call_target="tpu_custom_call" | custom-call | flops 400000000 | bytes 1835008 | tf_op jit(solution)/shard_map/pallas_call | solution.py:415
  (1 shorter events, 0.0 us)
Async XLA Ops:
  1.4 1.0 %copy-start = (bf16[16,64,256]{2,1,0:T(8,128)(2,1)S(1)}, bf16[16,64,256]{2,1,0:T(8,128)(2,1)}, u32[]{:S(2)}) copy-start(bf16[16,64,256]{2,1,0:T(8,128)(2,1)} %probe.1) | copy-start | bytes 1572868
  2.5 12.9 %collective-permute-start.1 = (bf16[1072,256]{1,0:T(8,128)(2,1)S(1)}, bf16[1072,256]{1,0:T(8,128)(2,1)S(1)}, u32[]{:S(2)}, u32[]{:S(2)}) collective-permute-start(bf16[1072,256]{1,0:T(8,128)(2,1)S(1)} %shard_map.120.joined), channel_id=1, source_target_pairs={{4,8},{12,16},{20,24},{8,4},{16,12},{24,20},{5,9},{13,17},{21,25},... | collective-permute-start | bytes 1646600 | tf_op jit(solution)/shard_map/ppermute | solution.py:459
  3.2 12.3 %collective-permute-start = (bf16[1072,256]{1,0:T(8,128)(2,1)S(1)}, bf16[1072,256]{1,0:T(8,128)(2,1)S(1)}, u32[]{:S(2)}, u32[]{:S(2)}) collective-permute-start(bf16[1072,256]{1,0:T(8,128)(2,1)S(1)} %shard_map.120.joined), channel_id=1, source_target_pairs={{0,4},{8,12},{16,20},{24,28},{4,0},{12,8},{20,16},{28,24},{1,5},{9... | collective-permute-start | bytes 1646600 | tf_op jit(solution)/shard_map/ppermute | solution.py:459
  7.6 0.7 %copy-start.4 = (s32[16,16]{1,0:T(8,128)S(1)}, s32[16,16]{1,0:T(8,128)}, u32[]{:S(2)}) copy-start(s32[16,16]{1,0:T(8,128)} %nb_ref.5) | copy-start | bytes 3076
  21.1 10.3 %collective-permute-start.2 = (bf16[4,64,256]{2,1,0:T(8,128)(2,1)S(1)}, bf16[4,64,256]{2,1,0:T(8,128)(2,1)S(1)}, u32[]{:S(2)}, u32[]{:S(2)}) collective-permute-start(bf16[4,64,256]{2,1,0:T(8,128)(2,1)S(1)} %get-tuple-element.35), channel_id=1, source_target_pairs={{0,1},{1,0},{2,3},{3,2},{4,5},{5,4},{6,7},{7,6},{8,9},{9,8},{10,11... | collective-permute-start | bytes 393224 | tf_op jit(solution)/shard_map/ppermute | solution.py:463
  23.7 7.7 %collective-permute-start.3 = (bf16[4,64,256]{2,1,0:T(8,128)(2,1)S(1)}, bf16[4,64,256]{2,1,0:T(8,128)(2,1)S(1)}, u32[]{:S(2)}, u32[]{:S(2)}) collective-permute-start(bf16[4,64,256]{2,1,0:T(8,128)(2,1)S(1)} %get-tuple-element.36), channel_id=1, source_target_pairs={{0,2},{1,3},{2,0},{3,1},{4,6},{5,7},{6,4},{7,5},{8,10},{9,11},{10,... | collective-permute-start | bytes 393224 | tf_op jit(solution)/shard_map/ppermute | solution.py:463
  25.2 6.2 %collective-permute-start.4 = (bf16[4,64,256]{2,1,0:T(8,128)(2,1)S(1)}, bf16[4,64,256]{2,1,0:T(8,128)(2,1)S(1)}, u32[]{:S(2)}, u32[]{:S(2)}) collective-permute-start(bf16[4,64,256]{2,1,0:T(8,128)(2,1)S(1)} %get-tuple-element.37), channel_id=1, source_target_pairs={{0,3},{1,2},{2,1},{3,0},{4,7},{5,6},{6,5},{7,4},{8,11},{9,10},{10,... | collective-permute-start | bytes 393224 | tf_op jit(solution)/shard_map/ppermute | solution.py:463
  25.2 5.7 %copy-start.1 = (f32[16,64,64]{2,1,0:T(8,128)S(1)}, f32[16,64,64]{2,1,0:T(8,128)}, u32[]{:S(2)}) copy-start(f32[16,64,64]{2,1,0:T(8,128)} %leaf_inverse.1) | copy-start | bytes 786436
  25.2 5.7 %copy-start.2 = (f32[15,64,64]{2,1,0:T(8,128)S(1)}, f32[15,64,64]{2,1,0:T(8,128)}, u32[]{:S(2)}) copy-start(f32[15,64,64]{2,1,0:T(8,128)} %local_inverse.1) | copy-start | bytes 737284
  25.2 5.7 %copy-start.3 = (f32[7,64,64]{2,1,0:T(8,128)S(1)}, f32[7,64,64]{2,1,0:T(8,128)}, u32[]{:S(2)}) copy-start(f32[7,64,64]{2,1,0:T(8,128)} %upper_inverse.1) | copy-start | bytes 344068
  25.2 5.7 %copy-start.5 = (s32[16,64]{1,0:T(8,128)S(1)}, s32[16,64]{1,0:T(8,128)}, u32[]{:S(2)}) copy-start(s32[16,64]{1,0:T(8,128)} %leaf_pivots.1) | copy-start | bytes 12292
  25.2 5.7 %copy-start.6 = (s32[15,64]{1,0:T(8,128)S(1)}, s32[15,64]{1,0:T(8,128)}, u32[]{:S(2)}) copy-start(s32[15,64]{1,0:T(8,128)} %local_pivots.1) | copy-start | bytes 11524
  25.2 5.7 %copy-start.7 = (s32[7,64]{1,0:T(8,128)S(1)}, s32[7,64]{1,0:T(8,128)}, u32[]{:S(2)}) copy-start(s32[7,64]{1,0:T(8,128)} %upper_pivots.1) | copy-start | bytes 5380
  33.5 6.3 %collective-permute-start.7 = (f32[64,256]{1,0:T(8,128)S(1)}, f32[64,256]{1,0:T(8,128)S(1)}, u32[]{:S(2)}, u32[]{:S(2)}) collective-permute-start(f32[64,256]{1,0:T(8,128)S(1)} %get-tuple-element.41.own), channel_id=1, source_target_pairs={{0,3},{1,2},{2,1},{3,0},{4,7},{5,6},{6,5},{7,4},{8,11},{9,10},{10,... | collective-permute-start | bytes 196616 | tf_op jit(solution)/shard_map/ppermute | solution.py:463
  35.4 9.8 %collective-permute-start.6 = (f32[64,256]{1,0:T(8,128)S(1)}, f32[64,256]{1,0:T(8,128)S(1)}, u32[]{:S(2)}, u32[]{:S(2)}) collective-permute-start(f32[64,256]{1,0:T(8,128)S(1)} %get-tuple-element.41.own), channel_id=1, source_target_pairs={{0,2},{1,3},{2,0},{3,1},{4,6},{5,7},{6,4},{7,5},{8,10},{9,11},{10,... | collective-permute-start | bytes 196616 | tf_op jit(solution)/shard_map/ppermute | solution.py:463
  35.7 9.5 %collective-permute-start.5 = (f32[64,256]{1,0:T(8,128)S(1)}, f32[64,256]{1,0:T(8,128)S(1)}, u32[]{:S(2)}, u32[]{:S(2)}) collective-permute-start(f32[64,256]{1,0:T(8,128)S(1)} %get-tuple-element.41.own), channel_id=1, source_target_pairs={{0,1},{1,0},{2,3},{3,2},{4,5},{5,4},{6,7},{7,6},{8,9},{9,8},{10,11... | collective-permute-start | bytes 196616 | tf_op jit(solution)/shard_map/ppermute | solution.py:463
  37.0 22.0 %collective-permute-start.13 = (f32[352,256]{1,0:T(8,128)S(1)}, f32[352,256]{1,0:T(8,128)S(1)}, u32[]{:S(2)}, u32[]{:S(2)}) collective-permute-start(f32[352,256]{1,0:T(8,128)S(1)} %get-tuple-element.50.refs_2_), channel_id=1, source_target_pairs={{0,3},{1,2},{2,1},{3,0},{4,7},{5,6},{6,5},{7,4},{8,11},{9,10},{10,... | collective-permute-start | bytes 1081352 | tf_op jit(solution)/shard_map/ppermute | solution.py:463
  38.9 20.2 %collective-permute-start.11 = (f32[352,256]{1,0:T(8,128)S(1)}, f32[352,256]{1,0:T(8,128)S(1)}, u32[]{:S(2)}, u32[]{:S(2)}) collective-permute-start(f32[352,256]{1,0:T(8,128)S(1)} %get-tuple-element.50.refs_2_), channel_id=1, source_target_pairs={{0,1},{1,0},{2,3},{3,2},{4,5},{5,4},{6,7},{7,6},{8,9},{9,8},{10,11... | collective-permute-start | bytes 1081352 | tf_op jit(solution)/shard_map/ppermute | solution.py:463
  46.4 12.6 %collective-permute-start.12 = (f32[352,256]{1,0:T(8,128)S(1)}, f32[352,256]{1,0:T(8,128)S(1)}, u32[]{:S(2)}, u32[]{:S(2)}) collective-permute-start(f32[352,256]{1,0:T(8,128)S(1)} %get-tuple-element.50.refs_2_), channel_id=1, source_target_pairs={{0,2},{1,3},{2,0},{3,1},{4,6},{5,7},{6,4},{7,5},{8,10},{9,11},{10,... | collective-permute-start | bytes 1081352 | tf_op jit(solution)/shard_map/ppermute | solution.py:463
  46.5 1.3 %collective-permute-start.8 = (f32[64,256]{1,0:T(8,128)S(1)}, f32[64,256]{1,0:T(8,128)S(1)}, u32[]{:S(2)}, u32[]{:S(2)}) collective-permute-start(f32[64,256]{1,0:T(8,128)S(1)} %get-tuple-element.44.own), channel_id=1, source_target_pairs={{0,4},{4,0},{8,12},{12,8},{16,20},{20,16},{24,28},{28,24},{1,5},{5... | collective-permute-start | bytes 196616 | tf_op jit(solution)/shard_map/ppermute | solution.py:541
  48.3 4.3 %collective-permute-start.9 = (f32[64,256]{1,0:T(8,128)S(1)}, f32[64,256]{1,0:T(8,128)S(1)}, u32[]{:S(2)}, u32[]{:S(2)}) collective-permute-start(f32[64,256]{1,0:T(8,128)S(1)} %get-tuple-element.46.own), channel_id=1, source_target_pairs={{0,8},{4,12},{8,0},{12,4},{16,24},{20,28},{24,16},{28,20},{1,9},{5... | collective-permute-start | bytes 196616 | tf_op jit(solution)/shard_map/ppermute | solution.py:541
  53.1 5.9 %collective-permute-start.10 = (f32[64,256]{1,0:T(8,128)S(1)}, f32[64,256]{1,0:T(8,128)S(1)}, u32[]{:S(2)}, u32[]{:S(2)}) collective-permute-start(f32[64,256]{1,0:T(8,128)S(1)} %get-tuple-element.47.own), channel_id=1, source_target_pairs={{0,16},{4,20},{8,24},{12,28},{16,0},{20,4},{24,8},{28,12},{1,17},{... | collective-permute-start | bytes 196616 | tf_op jit(solution)/shard_map/ppermute | solution.py:541
where the time goes:
time: 62.1 us; the launch traced here: 61.1 us
  Pallas kernels  25.1 us (40%)
  starting transfers between devices  16.7 us (27%)
  waiting for transfers between devices  15.9 us (26%)
  local copies, waits for them, and re-layouts  2.52 us (4%)
  between operations  0.85 us (1%)
    pallas_call x3, Pallas kernels, near_call(): pl.pallas_call(body, out_shape=outs, in_specs=[pl.BlockSpec(memory_space=...  18.3 us
    ppermute x9, starting transfers between devices, vec_send(): return lax.ppermute(array, 'vec', [(i, i ^ tier) for i in range(parts)])  10.5 us
    ppermute x3, waiting for transfers between devices, on_device(): lax.ppermute(own_up, 'leaf', [(i, i ^ 1 << tier) for i in range(leaf_tota...  10.5 us
    pallas_call x7, Pallas kernels, call(): pl.pallas_call(body, out_shape=outs, in_specs=[fixed] * (len(operands) -...  6.81 us
    ppermute x9, waiting for transfers between devices, vec_send(): return lax.ppermute(array, 'vec', [(i, i ^ tier) for i in range(parts)])  5.48 us
    ppermute x2, starting transfers between devices, on_device(): lax.ppermute(joined, 'leaf', pairs + [(j, i) for i, j in pairs])  5.11 us
    unnamed x17, local copies, waits for them, and re-layouts  2.52 us
  transfers between devices with their start and end apart: 14, of which 4 were waited for; matrix products, arithmetic and copies ran while one was open for 0% of the time, Pallas kernels for 25%

commit v1 on v0

--- a/solution.py
+++ b/solution.py
@@ -14,8 +14,7 @@
 FLIGHT = 8
 DEPTH = 128
 CHUNK = 256
-LATE = (2,)
-ROUND_FLOPS = 400_000_000
+ROUND_FLOPS = 1_150_000_000
 VMEM_BYTES = 20 * 1024 * 1024
 VMEM = pltpu.MemorySpace.VMEM
 SMEM = pltpu.MemorySpace.SMEM
@@ -532,9 +531,8 @@
         [pltpu.VMEM((parts * rank, total_columns), jnp.float32)],
         [own_up] + near_ups + [group_factors],
     )
-    later, own_up = lax.optimization_barrier((pack, own_up))
-    late = LATE if parts > max(LATE) else ()
-    others = [vec_send(later if tier in late else pack, tier) for tier in range(1, parts)]
+    pack, own_up = lax.optimization_barrier((pack, own_up))
+    others = [vec_send(pack, tier) for tier in range(1, parts)]
 
     maps = []
     for tier in range(UPL):

time: 62.1 us -> 64.7 us (1.042); the launches traced: 61.1 us -> 64.7 us
  Pallas kernels: 25.1 us -> 26.7 us
  waiting for transfers between devices: 15.9 us -> 17.2 us
  starting transfers between devices: 16.7 us -> 17.5 us
    ppermute x9, waiting for transfers between devices: 5.48 us -> 8.68 us  [vec_send(): return lax.ppermute(array, 'vec', [(i, i ^ tier) for i in range(parts)])]
    ppermute x3, waiting for transfers between devices: 10.5 us -> 8.48 us  [on_device(): lax.ppermute(own_up, 'leaf', [(i, i ^ 1 << tier) for i in range(leaf_tota...]
    pallas_call x3, Pallas kernels: 18.3 us -> 19.9 us  [near_call(): pl.pallas_call(body, out_shape=outs, in_specs=[pl.BlockSpec(memory_space=...]
  transfers between devices with their start and end apart: 14 -> 14, of which waited for: 4 -> 8; matrix products, arithmetic and copies ran while one was open for 0% -> 0% of each run, Pallas kernels for 25% -> 23%
where the time goes in v1:
time: 64.7 us
  Pallas kernels  26.7 us (41%)
  starting transfers between devices  17.5 us (27%)
  waiting for transfers between devices  17.2 us (27%)
  local copies, waits for them, and re-layouts  2.52 us (4%)
  between operations  0.82 us (1%)
    pallas_call x3, Pallas kernels, near_call(): pl.pallas_call(body, out_shape=outs, in_specs=[pl.BlockSpec(memory_space=...  19.9 us
    ppermute x9, starting transfers between devices, vec_send(): return lax.ppermute(array, 'vec', [(i, i ^ tier) for i in range(parts)])  10.7 us
    ppermute x9, waiting for transfers between devices, vec_send(): return lax.ppermute(array, 'vec', [(i, i ^ tier) for i in range(parts)])  8.68 us
    ppermute x3, waiting for transfers between devices, on_device(): lax.ppermute(own_up, 'leaf', [(i, i ^ 1 << tier) for i in range(leaf_tota...  8.48 us
    pallas_call x7, Pallas kernels, call(): pl.pallas_call(body, out_shape=outs, in_specs=[fixed] * (len(operands) -...  6.79 us
    ppermute x2, starting transfers between devices, on_device(): lax.ppermute(joined, 'leaf', pairs + [(j, i) for i, j in pairs])  5.11 us
    unnamed x17, local copies, waits for them, and re-layouts  2.52 us
    ppermute x3, starting transfers between devices, on_device(): lax.ppermute(own_up, 'leaf', [(i, i ^ 1 << tier) for i in range(leaf_tota...  1.69 us
  transfers between devices with their start and end apart: 14, of which 8 were waited for; matrix products, arithmetic and copies ran while one was open for 0% of the time, Pallas kernels for 23%

profile of v1, /device:TPU:0, one launch (start us, length us, event | category | flops | bytes accessed | tf_op | source)
XLA Modules:
  0.0 64.7 jit_solution(985749791222911095)
XLA Ops:
  0.6 0.8 %copy.13.points = bf16[16,3,256]{2,1,0:T(4,128)(2,1)S(1)} copy(bf16[16,3,256]{2,0,1:T(8,128)(2,1)} %param.9) | data formatting | bytes 49152 | tf_op args[0]
  1.4 0.0 copy-start
  1.4 1.0 %copy-done = bf16[16,64,256]{2,1,0:T(8,128)(2,1)S(1)} copy-done((bf16[16,64,256]{2,1,0:T(8,128)(2,1)S(1)}, bf16[16,64,256]{2,1,0:T(8,128)(2,1)}, u32[]{:S(2)}) %copy-start) | copy-done | bytes 524312
  2.5 0.7 %collective-permute-start.1 = (bf16[1072,256]{1,0:T(8,128)(2,1)S(1)}, bf16[1072,256]{1,0:T(8,128)(2,1)S(1)}, u32[]{:S(2)}, u32[]{:S(2)}) collective-permute-start(bf16[1072,256]{1,0:T(8,128)(2,1)S(1)} %shard_map.120.joined), channel_id=1, source_target_pairs={{4,8},{12,16},{20,24},{8,4},{16,12},{24,20},{5,9},{13,17},{21,25},... | collective-permute-start | bytes 1646600 | tf_op jit(solution)/shard_map/ppermute | solution.py:458
  3.2 4.4 %collective-permute-start = (bf16[1072,256]{1,0:T(8,128)(2,1)S(1)}, bf16[1072,256]{1,0:T(8,128)(2,1)S(1)}, u32[]{:S(2)}, u32[]{:S(2)}) collective-permute-start(bf16[1072,256]{1,0:T(8,128)(2,1)S(1)} %shard_map.120.joined), channel_id=1, source_target_pairs={{0,4},{8,12},{16,20},{24,28},{4,0},{12,8},{20,16},{28,24},{1,5},{9... | collective-permute-start | bytes 1646600 | tf_op jit(solution)/shard_map/ppermute | solution.py:458
  7.6 0.0 copy-start.4
  7.6 0.7 %copy-done.4 = s32[16,16]{1,0:T(8,128)S(1)} copy-done((s32[16,16]{1,0:T(8,128)S(1)}, s32[16,16]{1,0:T(8,128)}, u32[]{:S(2)}) %copy-start.4) | copy-done | bytes 1048
  8.3 8.2 %shard_map.121 = (f32[17,64,256]{2,1,0:T(8,128)S(1)}, bf16[16,128,256]{2,1,0:T(8,128)(2,1)S(1)}, bf16[17,256,128]{2,1,0:T(8,128)(2,1)S(1)}) custom-call(s32[16,16]{1,0:T(8,128)S(1)} %copy-done.4, bf16[1072,256]{1,0:T(8,128)(2,1)S(1)} %shard_map.120.joined), custom_call_target="tpu_custom_call" | custom-call | flops 1207959552 | bytes 549888 | tf_op jit(solution)/shard_map/pallas_call | solution.py:201
  16.5 0.0 collective-permute-done.1.outer
  16.5 0.0 collective-permute-done.inner
  16.5 6.7 %shard_map.122 = (bf16[4,64,256]{2,1,0:T(8,128)(2,1)S(1)}, bf16[4,64,256]{2,1,0:T(8,128)(2,1)S(1)}, bf16[4,64,256]{2,1,0:T(8,128)(2,1)S(1)}, bf16[48,128,256]{2,1,0:T(8,128)(2,1)S(1)}, bf16[48,64,256]{2,1,0:T(8,128)(2,1)S(1)}) custom-call(s32[16,16]{1,0:T(8,128)S(1)} %copy-done.4, bf16[1072,256]{1,0:T(8,128)(2,1)S(1)} %shard_map.120.joined, ...), custom_call_target="tpu_custom_call" | custom-call | flops 1207959552 | bytes 4924416 | tf_op jit(solution)/shard_map/pallas_call | solution.py:201
  23.2 1.5 %collective-permute-start.2 = (bf16[4,64,256]{2,1,0:T(8,128)(2,1)S(1)}, bf16[4,64,256]{2,1,0:T(8,128)(2,1)S(1)}, u32[]{:S(2)}, u32[]{:S(2)}) collective-permute-start(bf16[4,64,256]{2,1,0:T(8,128)(2,1)S(1)} %get-tuple-element.35), channel_id=1, source_target_pairs={{0,1},{1,0},{2,3},{3,2},{4,5},{5,4},{6,7},{7,6},{8,9},{9,8},{10,11... | collective-permute-start | bytes 393224 | tf_op jit(solution)/shard_map/ppermute | solution.py:462
  24.7 1.5 %collective-permute-start.3 = (bf16[4,64,256]{2,1,0:T(8,128)(2,1)S(1)}, bf16[4,64,256]{2,1,0:T(8,128)(2,1)S(1)}, u32[]{:S(2)}, u32[]{:S(2)}) collective-permute-start(bf16[4,64,256]{2,1,0:T(8,128)(2,1)S(1)} %get-tuple-element.36), channel_id=1, source_target_pairs={{0,2},{1,3},{2,0},{3,1},{4,6},{5,7},{6,4},{7,5},{8,10},{9,11},{10,... | collective-permute-start | bytes 393224 | tf_op jit(solution)/shard_map/ppermute | solution.py:462
  26.2 0.5 collective-permute-start.4
  26.8 0.0 copy-start.1
  26.8 0.0 copy-start.2
  26.8 0.0 copy-start.3
  26.8 0.0 copy-start.5
  26.8 0.0 copy-start.6
  26.8 0.0 copy-start.7
  26.8 5.1 %shard_map.123._.own = bf16[4,64,256]{2,1,0:T(8,128)(2,1)S(1)} custom-call(s32[16,16]{1,0:T(8,128)S(1)} %copy-done.4, bf16[48,128,256]{2,1,0:T(8,128)(2,1)S(1)} %get-tuple-element.33.far, bf16[48,64,256]{2,1,0:T(8,128)(2,1)S(1)} %get-tuple-element.34.vectors, bf16[17,256,128]{2,1,0:T(8,128)(2,1)S(1)} %get-tuple-element.31.near), custom_call_target="tpu_custom_call" | custom-call | flops 805306368 | bytes 5833728 | tf_op jit(solution)/shard_map/pallas_call | solution.py:201
  31.9 0.0 copy-done.1
  31.9 0.0 copy-done.2
  31.9 0.0 copy-done.3
  31.9 0.0 copy-done.5
  31.9 0.0 copy-done.6
  31.9 0.0 copy-done.7
  31.9 0.5 shard_map.124
  32.4 0.0 collective-permute-done.2.refs_0_
  32.4 0.0 collective-permute-done.3.refs_1_
  32.4 0.1 collective-permute-done.4.refs_2_
  32.5 2.0 %shard_map.125 = (f32[352,256]{1,0:T(8,128)S(1)}, f32[64,256]{1,0:T(8,128)S(1)}) custom-call(bf16[4,64,256]{2,1,0:T(8,128)(2,1)S(1)} %shard_map.123._.own, bf16[4,64,256]{2,1,0:T(8,128)(2,1)S(1)} %collective-permute-done.2.refs_0_, bf16[4,64,256]{2,1,0:T(8,128)(2,1)S(1)} %collective-permute-done.3.refs_1_, ...), custom_call_target="tpu_custom_call" | custom-call | bytes 884736 | tf_op jit(solution)/shard_map/pallas_call | solution.py:414
  34.6 2.4 %collective-permute-start.7 = (f32[64,256]{1,0:T(8,128)S(1)}, f32[64,256]{1,0:T(8,128)S(1)}, u32[]{:S(2)}, u32[]{:S(2)}) collective-permute-start(f32[64,256]{1,0:T(8,128)S(1)} %get-tuple-element.41.own), channel_id=1, source_target_pairs={{0,3},{1,2},{2,1},{3,0},{4,7},{5,6},{6,5},{7,4},{8,11},{9,10},{10,... | collective-permute-start | bytes 196616 | tf_op jit(solution)/shard_map/ppermute | solution.py:462
  37.0 0.5 collective-permute-start.6
  37.5 0.6 collective-permute-start.5
  38.1 1.9 %collective-permute-done.7.refs_2_ = f32[64,256]{1,0:T(8,128)S(1)} collective-permute-done((f32[64,256]{1,0:T(8,128)S(1)}, f32[64,256]{1,0:T(8,128)S(1)}, u32[]{:S(2)}, u32[]{:S(2)}) %collective-permute-start.7) | collective-permute-done | bytes 65568 | tf_op jit(solution)/shard_map/ppermute | solution.py:462
  40.0 1.2 %collective-permute-done.6.refs_1_ = f32[64,256]{1,0:T(8,128)S(1)} collective-permute-done((f32[64,256]{1,0:T(8,128)S(1)}, f32[64,256]{1,0:T(8,128)S(1)}, u32[]{:S(2)}, u32[]{:S(2)}) %collective-permute-start.6) | collective-permute-done | bytes 65568 | tf_op jit(solution)/shard_map/ppermute | solution.py:462
  41.2 0.5 collective-permute-done.5.refs_0_
  41.8 1.2 %shard_map.126 = (f32[192,128]{1,0:T(8,128)S(1)}, f32[64,256]{1,0:T(8,128)S(1)}) custom-call(f32[64,256]{1,0:T(8,128)S(1)} %get-tuple-element.41.own, f32[64,256]{1,0:T(8,128)S(1)} %collective-permute-done.5.refs_0_, f32[64,256]{1,0:T(8,128)S(1)} %collective-permute-done.6.refs_1_, f32[64,256]{1,0:T(8,128)S(1)} %collective-permute-done.7.refs_2_, ...), custom_call_target="tpu_custom_call" | custom-call | bytes 360448 | tf_op jit(solution)/shard_map/pallas_call | solution.py:414
  43.0 0.1 collective-permute-start.8
  43.1 1.6 %collective-permute-start.13 = (f32[352,256]{1,0:T(8,128)S(1)}, f32[352,256]{1,0:T(8,128)S(1)}, u32[]{:S(2)}, u32[]{:S(2)}) collective-permute-start(f32[352,256]{1,0:T(8,128)S(1)} %get-tuple-element.50.refs_2_), channel_id=1, source_target_pairs={{0,3},{1,2},{2,1},{3,0},{4,7},{5,6},{6,5},{7,4},{8,11},{9,10},{10,... | collective-permute-start | bytes 1081352 | tf_op jit(solution)/shard_map/ppermute | solution.py:462
  44.6 0.6 collective-permute-start.12
  45.2 1.4 %collective-permute-start.11 = (f32[352,256]{1,0:T(8,128)S(1)}, f32[352,256]{1,0:T(8,128)S(1)}, u32[]{:S(2)}, u32[]{:S(2)}) collective-permute-start(f32[352,256]{1,0:T(8,128)S(1)} %get-tuple-element.50.refs_2_), channel_id=1, source_target_pairs={{0,1},{1,0},{2,3},{3,2},{4,5},{5,4},{6,7},{7,6},{8,9},{9,8},{10,11... | collective-permute-start | bytes 1081352 | tf_op jit(solution)/shard_map/ppermute | solution.py:462
  46.6 0.0 collective-permute-done.8.arrived
  46.6 0.5 shard_map.127
  47.1 0.5 collective-permute-start.9
  47.5 3.9 %collective-permute-done.9.arrived = f32[64,256]{1,0:T(8,128)S(1)} collective-permute-done((f32[64,256]{1,0:T(8,128)S(1)}, f32[64,256]{1,0:T(8,128)S(1)}, u32[]{:S(2)}, u32[]{:S(2)}) %collective-permute-start.9) | collective-permute-done | bytes 65568 | tf_op jit(solution)/shard_map/ppermute | solution.py:539
  51.4 0.5 shard_map.128
  51.9 1.2 %collective-permute-start.10 = (f32[64,256]{1,0:T(8,128)S(1)}, f32[64,256]{1,0:T(8,128)S(1)}, u32[]{:S(2)}, u32[]{:S(2)}) collective-permute-start(f32[64,256]{1,0:T(8,128)S(1)} %get-tuple-element.47.own), channel_id=1, source_target_pairs={{0,16},{4,20},{8,24},{12,28},{16,0},{20,4},{24,8},{28,12},{1,17},{... | collective-permute-start | bytes 196616 | tf_op jit(solution)/shard_map/ppermute | solution.py:539
  53.1 4.6 %collective-permute-done.10.arrived = f32[64,256]{1,0:T(8,128)S(1)} collective-permute-done((f32[64,256]{1,0:T(8,128)S(1)}, f32[64,256]{1,0:T(8,128)S(1)}, u32[]{:S(2)}, u32[]{:S(2)}) %collective-permute-start.10) | collective-permute-done | bytes 65568 | tf_op jit(solution)/shard_map/ppermute | solution.py:539
  57.7 0.0 collective-permute-done.13.refs_5_
  57.7 4.9 %collective-permute-done.12.refs_4_ = f32[352,256]{1,0:T(8,128)S(1)} collective-permute-done((f32[352,256]{1,0:T(8,128)S(1)}, f32[352,256]{1,0:T(8,128)S(1)}, u32[]{:S(2)}, u32[]{:S(2)}) %collective-permute-start.12) | collective-permute-done | bytes 360480 | tf_op jit(solution)/shard_map/ppermute | solution.py:462
  62.5 0.1 collective-permute-done.11.refs_3_
  62.6 2.1 %shard_map.129 = (f32[3,64,128]{2,1,0:T(8,128)}, f32[64,64]{1,0:T(8,128)}, f32[1024,256]{1,0:T(8,128)}, f32[960,128]{1,0:T(8,128)}) custom-call(f32[64,256]{1,0:T(8,128)S(1)} %get-tuple-element.47.own, f32[64,256]{1,0:T(8,128)S(1)} %collective-permute-done.10.arrived, bf16[3,128,128]{2,1,0:T(8,128)(2,1)S(1)} %get-tuple-element.45.factors, ...), custom_call_target="tpu_custom_call" | custom-call | flops 1150000000 | bytes 1835008 | tf_op jit(solution)/shard_map/pallas_call | solution.py:414
  (1 shorter events, 0.0 us)
Async XLA Ops:
  1.4 1.0 %copy-start = (bf16[16,64,256]{2,1,0:T(8,128)(2,1)S(1)}, bf16[16,64,256]{2,1,0:T(8,128)(2,1)}, u32[]{:S(2)}) copy-start(bf16[16,64,256]{2,1,0:T(8,128)(2,1)} %probe.1) | copy-start | bytes 1572868
  2.5 14.0 %collective-permute-start.1 = (bf16[1072,256]{1,0:T(8,128)(2,1)S(1)}, bf16[1072,256]{1,0:T(8,128)(2,1)S(1)}, u32[]{:S(2)}, u32[]{:S(2)}) collective-permute-start(bf16[1072,256]{1,0:T(8,128)(2,1)S(1)} %shard_map.120.joined), channel_id=1, source_target_pairs={{4,8},{12,16},{20,24},{8,4},{16,12},{24,20},{5,9},{13,17},{21,25},... | collective-permute-start | bytes 1646600 | tf_op jit(solution)/shard_map/ppermute | solution.py:458
  3.2 13.3 %collective-permute-start = (bf16[1072,256]{1,0:T(8,128)(2,1)S(1)}, bf16[1072,256]{1,0:T(8,128)(2,1)S(1)}, u32[]{:S(2)}, u32[]{:S(2)}) collective-permute-start(bf16[1072,256]{1,0:T(8,128)(2,1)S(1)} %shard_map.120.joined), channel_id=1, source_target_pairs={{0,4},{8,12},{16,20},{24,28},{4,0},{12,8},{20,16},{28,24},{1,5},{9... | collective-permute-start | bytes 1646600 | tf_op jit(solution)/shard_map/ppermute | solution.py:458
  7.6 0.7 %copy-start.4 = (s32[16,16]{1,0:T(8,128)S(1)}, s32[16,16]{1,0:T(8,128)}, u32[]{:S(2)}) copy-start(s32[16,16]{1,0:T(8,128)} %nb_ref.5) | copy-start | bytes 3076
  23.2 9.2 %collective-permute-start.2 = (bf16[4,64,256]{2,1,0:T(8,128)(2,1)S(1)}, bf16[4,64,256]{2,1,0:T(8,128)(2,1)S(1)}, u32[]{:S(2)}, u32[]{:S(2)}) collective-permute-start(bf16[4,64,256]{2,1,0:T(8,128)(2,1)S(1)} %get-tuple-element.35), channel_id=1, source_target_pairs={{0,1},{1,0},{2,3},{3,2},{4,5},{5,4},{6,7},{7,6},{8,9},{9,8},{10,11... | collective-permute-start | bytes 393224 | tf_op jit(solution)/shard_map/ppermute | solution.py:462
  24.7 7.7 %collective-permute-start.3 = (bf16[4,64,256]{2,1,0:T(8,128)(2,1)S(1)}, bf16[4,64,256]{2,1,0:T(8,128)(2,1)S(1)}, u32[]{:S(2)}, u32[]{:S(2)}) collective-permute-start(bf16[4,64,256]{2,1,0:T(8,128)(2,1)S(1)} %get-tuple-element.36), channel_id=1, source_target_pairs={{0,2},{1,3},{2,0},{3,1},{4,6},{5,7},{6,4},{7,5},{8,10},{9,11},{10,... | collective-permute-start | bytes 393224 | tf_op jit(solution)/shard_map/ppermute | solution.py:462
  26.2 6.3 %collective-permute-start.4 = (bf16[4,64,256]{2,1,0:T(8,128)(2,1)S(1)}, bf16[4,64,256]{2,1,0:T(8,128)(2,1)S(1)}, u32[]{:S(2)}, u32[]{:S(2)}) collective-permute-start(bf16[4,64,256]{2,1,0:T(8,128)(2,1)S(1)} %get-tuple-element.37), channel_id=1, source_target_pairs={{0,3},{1,2},{2,1},{3,0},{4,7},{5,6},{6,5},{7,4},{8,11},{9,10},{10,... | collective-permute-start | bytes 393224 | tf_op jit(solution)/shard_map/ppermute | solution.py:462
  26.8 5.1 %copy-start.1 = (f32[16,64,64]{2,1,0:T(8,128)S(1)}, f32[16,64,64]{2,1,0:T(8,128)}, u32[]{:S(2)}) copy-start(f32[16,64,64]{2,1,0:T(8,128)} %leaf_inverse.1) | copy-start | bytes 786436
  26.8 5.1 %copy-start.2 = (f32[15,64,64]{2,1,0:T(8,128)S(1)}, f32[15,64,64]{2,1,0:T(8,128)}, u32[]{:S(2)}) copy-start(f32[15,64,64]{2,1,0:T(8,128)} %local_inverse.1) | copy-start | bytes 737284
  26.8 5.1 %copy-start.3 = (f32[7,64,64]{2,1,0:T(8,128)S(1)}, f32[7,64,64]{2,1,0:T(8,128)}, u32[]{:S(2)}) copy-start(f32[7,64,64]{2,1,0:T(8,128)} %upper_inverse.1) | copy-start | bytes 344068
  26.8 5.2 %copy-start.5 = (s32[16,64]{1,0:T(8,128)S(1)}, s32[16,64]{1,0:T(8,128)}, u32[]{:S(2)}) copy-start(s32[16,64]{1,0:T(8,128)} %leaf_pivots.1) | copy-start | bytes 12292
  26.8 5.2 %copy-start.6 = (s32[15,64]{1,0:T(8,128)S(1)}, s32[15,64]{1,0:T(8,128)}, u32[]{:S(2)}) copy-start(s32[15,64]{1,0:T(8,128)} %local_pivots.1) | copy-start | bytes 11524
  26.8 5.2 %copy-start.7 = (s32[7,64]{1,0:T(8,128)S(1)}, s32[7,64]{1,0:T(8,128)}, u32[]{:S(2)}) copy-start(s32[7,64]{1,0:T(8,128)} %upper_pivots.1) | copy-start | bytes 5380
  34.6 5.4 %collective-permute-start.7 = (f32[64,256]{1,0:T(8,128)S(1)}, f32[64,256]{1,0:T(8,128)S(1)}, u32[]{:S(2)}, u32[]{:S(2)}) collective-permute-start(f32[64,256]{1,0:T(8,128)S(1)} %get-tuple-element.41.own), channel_id=1, source_target_pairs={{0,3},{1,2},{2,1},{3,0},{4,7},{5,6},{6,5},{7,4},{8,11},{9,10},{10,... | collective-permute-start | bytes 196616 | tf_op jit(solution)/shard_map/ppermute | solution.py:462
  37.0 4.3 %collective-permute-start.6 = (f32[64,256]{1,0:T(8,128)S(1)}, f32[64,256]{1,0:T(8,128)S(1)}, u32[]{:S(2)}, u32[]{:S(2)}) collective-permute-start(f32[64,256]{1,0:T(8,128)S(1)} %get-tuple-element.41.own), channel_id=1, source_target_pairs={{0,2},{1,3},{2,0},{3,1},{4,6},{5,7},{6,4},{7,5},{8,10},{9,11},{10,... | collective-permute-start | bytes 196616 | tf_op jit(solution)/shard_map/ppermute | solution.py:462
  37.5 4.3 %collective-permute-start.5 = (f32[64,256]{1,0:T(8,128)S(1)}, f32[64,256]{1,0:T(8,128)S(1)}, u32[]{:S(2)}, u32[]{:S(2)}) collective-permute-start(f32[64,256]{1,0:T(8,128)S(1)} %get-tuple-element.41.own), channel_id=1, source_target_pairs={{0,1},{1,0},{2,3},{3,2},{4,5},{5,4},{6,7},{7,6},{8,9},{9,8},{10,11... | collective-permute-start | bytes 196616 | tf_op jit(solution)/shard_map/ppermute | solution.py:462
  43.0 3.6 %collective-permute-start.8 = (f32[64,256]{1,0:T(8,128)S(1)}, f32[64,256]{1,0:T(8,128)S(1)}, u32[]{:S(2)}, u32[]{:S(2)}) collective-permute-start(f32[64,256]{1,0:T(8,128)S(1)} %get-tuple-element.44.own), channel_id=1, source_target_pairs={{0,4},{4,0},{8,12},{12,8},{16,20},{20,16},{24,28},{28,24},{1,5},{5... | collective-permute-start | bytes 196616 | tf_op jit(solution)/shard_map/ppermute | solution.py:539
  43.1 14.6 %collective-permute-start.13 = (f32[352,256]{1,0:T(8,128)S(1)}, f32[352,256]{1,0:T(8,128)S(1)}, u32[]{:S(2)}, u32[]{:S(2)}) collective-permute-start(f32[352,256]{1,0:T(8,128)S(1)} %get-tuple-element.50.refs_2_), channel_id=1, source_target_pairs={{0,3},{1,2},{2,1},{3,0},{4,7},{5,6},{6,5},{7,4},{8,11},{9,10},{10,... | collective-permute-start | bytes 1081352 | tf_op jit(solution)/shard_map/ppermute | solution.py:462
  44.6 17.9 %collective-permute-start.12 = (f32[352,256]{1,0:T(8,128)S(1)}, f32[352,256]{1,0:T(8,128)S(1)}, u32[]{:S(2)}, u32[]{:S(2)}) collective-permute-start(f32[352,256]{1,0:T(8,128)S(1)} %get-tuple-element.50.refs_2_), channel_id=1, source_target_pairs={{0,2},{1,3},{2,0},{3,1},{4,6},{5,7},{6,4},{7,5},{8,10},{9,11},{10,... | collective-permute-start | bytes 1081352 | tf_op jit(solution)/shard_map/ppermute | solution.py:462
  45.2 17.4 %collective-permute-start.11 = (f32[352,256]{1,0:T(8,128)S(1)}, f32[352,256]{1,0:T(8,128)S(1)}, u32[]{:S(2)}, u32[]{:S(2)}) collective-permute-start(f32[352,256]{1,0:T(8,128)S(1)} %get-tuple-element.50.refs_2_), channel_id=1, source_target_pairs={{0,1},{1,0},{2,3},{3,2},{4,5},{5,4},{6,7},{7,6},{8,9},{9,8},{10,11... | collective-permute-start | bytes 1081352 | tf_op jit(solution)/shard_map/ppermute | solution.py:462
  47.1 4.3 %collective-permute-start.9 = (f32[64,256]{1,0:T(8,128)S(1)}, f32[64,256]{1,0:T(8,128)S(1)}, u32[]{:S(2)}, u32[]{:S(2)}) collective-permute-start(f32[64,256]{1,0:T(8,128)S(1)} %get-tuple-element.46.own), channel_id=1, source_target_pairs={{0,8},{4,12},{8,0},{12,4},{16,24},{20,28},{24,16},{28,20},{1,9},{5... | collective-permute-start | bytes 196616 | tf_op jit(solution)/shard_map/ppermute | solution.py:539
  51.9 5.8 %collective-permute-start.10 = (f32[64,256]{1,0:T(8,128)S(1)}, f32[64,256]{1,0:T(8,128)S(1)}, u32[]{:S(2)}, u32[]{:S(2)}) collective-permute-start(f32[64,256]{1,0:T(8,128)S(1)} %get-tuple-element.47.own), channel_id=1, source_target_pairs={{0,16},{4,20},{8,24},{12,28},{16,0},{20,4},{24,8},{28,12},{1,17},{... | collective-permute-start | bytes 196616 | tf_op jit(solution)/shard_map/ppermute | solution.py:539

commit v2 on v1

--- a/solution.py
+++ b/solution.py
@@ -14,7 +14,7 @@
 FLIGHT = 8
 DEPTH = 128
 CHUNK = 256
-ROUND_FLOPS = 1_150_000_000
+ROUND_FLOPS = 950_000_000
 VMEM_BYTES = 20 * 1024 * 1024
 VMEM = pltpu.MemorySpace.VMEM
 SMEM = pltpu.MemorySpace.SMEM
@@ -369,12 +369,7 @@
     up_out[...] = upward
 
 
-def finish_kernel(tier, share, group, rank, own, arrived, factors, *refs):
-    parts = group // share
-    earlier, refs = refs[:tier], refs[tier:]
-    packs, refs = refs[:parts], refs[parts:]
-    joined, interps, top, leaf_out, local_out, ups, turned, sems = refs
-    me = lax.axis_index("vec")
+def start_copies(pieces, share, group, rank, leaf_out, local_out, sems):
     copies = []
 
     def put(source, target):
@@ -384,31 +379,64 @@
     def rows_at(start, height):
         return pl.ds(pl.multiple_of(start, height), height)
 
-    for flip, piece in enumerate(packs):
-        device = me ^ flip
-        leaves = share * rank
-        put(piece.at[0:leaves], leaf_out.at[rows_at(device * leaves, leaves)])
-        for index, row in enumerate(own_nodes(share, group, device)):
+    leaves = share * rank
+    for flip, first, piece in pieces:
+        device = lax.axis_index("vec") ^ flip
+        end = first + piece.shape[0]
+        if first < leaves:
+            height = min(end, leaves) - first
+            step = height if height == leaves else rank
+            for row in range(0, height, step):
+                put(
+                    piece.at[row : row + step],
+                    leaf_out.at[rows_at(device * leaves + first + row, step)],
+                )
+        for index, node in enumerate(own_nodes(share, group, device)):
             for lane, source, start, height in pack_places(index, share, rank):
-                put(
-                    piece.at[start : start + height, lane : lane + 2 * rank],
-                    local_out.at[rows_at(row * rank + source, height)],
-                )
-    put(joined, local_out.at[(group - parts) * rank : (group - 1) * rank])
-
+                if first <= start < end:
+                    put(
+                        piece.at[start - first : start - first + height, lane : lane + 2 * rank],
+                        local_out.at[rows_at(node * rank + source, height)],
+                    )
+    return copies
+
+
+def place_kernel(flips, share, group, rank, *refs):
+    packs, (joined, leaf_out, local_out, sems) = refs[: len(flips)], refs[len(flips) :]
+    pieces = [(flip, 0, piece) for flip, piece in zip(flips, packs)]
+    copies = start_copies(pieces, share, group, rank, leaf_out, local_out, sems)
+    rows = joined.shape[0]
+    target = local_out.at[local_out.shape[0] - rows :]
+    copies.append(pltpu.make_async_copy(joined, target, sems.at[len(copies)]))
+    copies[-1].start()
+    for copy in copies:
+        copy.wait()
+
+
+def forward_kernel(here, there, _, upper, lower):
+    upper[...] = here[0 : upper.shape[0], :]
+    lower[...] = there[upper.shape[0] :, :]
+
+
+def finish_kernel(tier, tails, share, group, rank, own, arrived, factors, *refs):
+    earlier, refs = refs[:tier], refs[tier:]
+    packs, refs = refs[: len(tails)], refs[len(tails) :]
+    _, _, interps, top, leaf_out, local_out, ups, turned, sems = refs
+    pieces = [(flip, first, piece) for (flip, first), piece in zip(tails, packs)]
+    copies = start_copies(pieces, share, group, rank, leaf_out, local_out, sems)
     interp, upward = upper_node(tier, rank, own, arrived, factors, ups)
     for index, ref in enumerate(earlier):
         interps[index] = ref[...]
     interps[tier] = interp
     turned[...] = jnp.transpose(upward)
     columns = top.shape[0]
-    place = pl.multiple_of(me * columns, columns)
+    place = pl.multiple_of(lax.axis_index("vec") * columns, columns)
     top[...] = turned[pl.ds(place, columns), :]
     for copy in copies:
         copy.wait()
 
 
-def call(body, outs, scratch, operands, flops=0, anywhere_in=0, anywhere_out=0):
+def call(body, outs, scratch, operands, flops=0, anywhere_in=0, anywhere_out=0, aliases=None):
     fixed = pl.BlockSpec(memory_space=VMEM)
     free = pl.BlockSpec(memory_space=pl.ANY)
     return pl.pallas_call(
@@ -417,6 +445,7 @@
         in_specs=[fixed] * (len(operands) - anywhere_in) + [free] * anywhere_in,
         out_specs=[fixed] * (len(outs) - anywhere_out) + [free] * anywhere_out,
         scratch_shapes=scratch,
+        input_output_aliases=aliases or {},
         compiler_params=pltpu.CompilerParams(vmem_limit_bytes=VMEM_BYTES),
         cost_estimate=pl.CostEstimate(
             flops=flops, bytes_accessed=sum(o.size * o.dtype.itemsize for o in operands), transcendentals=0
@@ -531,8 +560,10 @@
         [pltpu.VMEM((parts * rank, total_columns), jnp.float32)],
         [own_up] + near_ups + [group_factors],
     )
-    pack, own_up = lax.optimization_barrier((pack, own_up))
-    others = [vec_send(pack, tier) for tier in range(1, parts)]
+    passing = parts == 4
+    flips = [0] + [tier for tier in range(1, parts) if not (passing and tier == 3)]
+    packs = [pack] + [vec_send(pack, tier) for tier in flips[1:]]
+    tails, tail_packs = [], []
 
     maps = []
     for tier in range(UPL):
@@ -548,8 +579,29 @@
                 flops=ROUND_FLOPS,
             )
             maps.append(interp)
+    if passing:
+        upper_rows = (share - 1) * rank
+        upper, lower = call(
+            forward_kernel,
+            [f32(upper_rows, size), f32(pack.shape[0] - upper_rows, size)],
+            [],
+            [packs[1], packs[2], own_up],
+            anywhere_in=1,
+        )
+        tails = [(3, 0), (3, upper_rows)]
+        tail_packs = [vec_send(upper, 2), vec_send(lower, 1)]
+    leaf_map, local_map = call(
+        functools.partial(place_kernel, flips, share, group, rank),
+        [f32(group * rank, size), f32((group - 1) * rank, width)],
+        [pltpu.SemaphoreType.DMA((len(flips) * (share + 1) + 1,))],
+        packs + [joined],
+        flops=ROUND_FLOPS,
+        anywhere_in=len(flips) + 1,
+        anywhere_out=2,
+    )
+    operands += maps + tail_packs + [leaf_map, local_map]
     upper_map, top, leaf_map, local_map = call(
-        functools.partial(finish_kernel, UPL - 1, share, group, rank),
+        functools.partial(finish_kernel, UPL - 1, tails, share, group, rank),
         [
             f32(UPL, rank, width),
             f32(columns, rank),
@@ -559,12 +611,13 @@
         [
             ups,
             pltpu.VMEM((total_columns, rank), jnp.float32),
-            pltpu.SemaphoreType.DMA((parts * (share + 1) + 1,)),
+            pltpu.SemaphoreType.DMA((2 * share + 1,)),
         ],
-        operands + maps + [pack] + others + [joined],
+        operands,
         flops=ROUND_FLOPS,
-        anywhere_in=parts + 1,
+        anywhere_in=len(tails) + 2,
         anywhere_out=2,
+        aliases={len(operands) - 2: 2, len(operands) - 1: 3},
     )
     return (
         jnp.swapaxes(leaf_map.reshape(group, rank, size), 1, 2),

time: 64.7 us -> 59.4 us (0.918)
  waiting for transfers between devices: 17.2 us -> 9.72 us
  starting transfers between devices: 17.5 us -> 20 us
    ppermute x9 -> x10, waiting for transfers between devices: 8.68 us -> 2.96 us  [vec_send(): return lax.ppermute(array, 'vec', [(i, i ^ tier) for i in range(parts)])]
    ppermute x3, starting transfers between devices: 1.69 us -> 3.56 us  [on_device(): lax.ppermute(own_up, 'leaf', [(i, i ^ 1 << tier) for i in range(leaf_tota...]
    ppermute x3, waiting for transfers between devices: 8.48 us -> 6.75 us  [on_device(): lax.ppermute(own_up, 'leaf', [(i, i ^ 1 << tier) for i in range(leaf_tota...]
    pallas_call x3, Pallas kernels: 19.9 us -> 18.9 us  [near_call(): pl.pallas_call(body, out_shape=outs, in_specs=[pl.BlockSpec(memory_space=...]
    pallas_call x7 -> x9, Pallas kernels: 6.79 us -> 7.57 us  [call(): pl.pallas_call(body, out_shape=outs, in_specs=[fixed] * (len(operands) -...]
    ppermute x9 -> x10, starting transfers between devices: 10.7 us -> 11.3 us  [vec_send(): return lax.ppermute(array, 'vec', [(i, i ^ tier) for i in range(parts)])]
  transfers between devices with their start and end apart: 14 -> 15, of which waited for: 8 -> 7; matrix products, arithmetic and copies ran while one was open for 0% -> 0% of each run, Pallas kernels for 23% -> 29%
where the time goes in v2:
time: 59.4 us; the launch traced here: 59.5 us
  Pallas kernels  26.4 us (44%)
  starting transfers between devices  20 us (34%)
  waiting for transfers between devices  9.72 us (16%)
  local copies, waits for them, and re-layouts  2.52 us (4%)
  between operations  0.84 us (1%)
    pallas_call x3, Pallas kernels, near_call(): pl.pallas_call(body, out_shape=outs, in_specs=[pl.BlockSpec(memory_space=...  18.9 us
    ppermute x10, starting transfers between devices, vec_send(): return lax.ppermute(array, 'vec', [(i, i ^ tier) for i in range(parts)])  11.3 us
    pallas_call x9, Pallas kernels, call(): pl.pallas_call(body, out_shape=outs, in_specs=[fixed] * (len(operands) -...  7.57 us
    ppermute x3, waiting for transfers between devices, on_device(): lax.ppermute(own_up, 'leaf', [(i, i ^ 1 << tier) for i in range(leaf_tota...  6.75 us
    ppermute x2, starting transfers between devices, on_device(): lax.ppermute(joined, 'leaf', pairs + [(j, i) for i, j in pairs])  5.11 us
    ppermute x3, starting transfers between devices, on_device(): lax.ppermute(own_up, 'leaf', [(i, i ^ 1 << tier) for i in range(leaf_tota...  3.56 us
    ppermute x10, waiting for transfers between devices, vec_send(): return lax.ppermute(array, 'vec', [(i, i ^ tier) for i in range(parts)])  2.96 us
    unnamed x17, local copies, waits for them, and re-layouts  2.52 us
  transfers between devices with their start and end apart: 15, of which 7 were waited for; matrix products, arithmetic and copies ran while one was open for 0% of the time, Pallas kernels for 29%

profile of v2, /device:TPU:0, one launch (start us, length us, event | category | flops | bytes accessed | tf_op | source)
XLA Modules:
  0.0 59.5 jit_solution(1538929333827530525)
XLA Ops:
  0.6 0.8 %copy.15.points = bf16[16,3,256]{2,1,0:T(4,128)(2,1)S(1)} copy(bf16[16,3,256]{2,0,1:T(8,128)(2,1)} %param.9) | data formatting | bytes 49152 | tf_op args[0]
  1.4 0.0 copy-start
  1.4 1.0 %copy-done = bf16[16,64,256]{2,1,0:T(8,128)(2,1)S(1)} copy-done((bf16[16,64,256]{2,1,0:T(8,128)(2,1)S(1)}, bf16[16,64,256]{2,1,0:T(8,128)(2,1)}, u32[]{:S(2)}) %copy-start) | copy-done | bytes 524312
  2.5 0.7 %collective-permute-start.1 = (bf16[1072,256]{1,0:T(8,128)(2,1)S(1)}, bf16[1072,256]{1,0:T(8,128)(2,1)S(1)}, u32[]{:S(2)}, u32[]{:S(2)}) collective-permute-start(bf16[1072,256]{1,0:T(8,128)(2,1)S(1)} %shard_map.120.joined), channel_id=1, source_target_pairs={{4,8},{12,16},{20,24},{8,4},{16,12},{24,20},{5,9},{13,17},{21,25},... | collective-permute-start | bytes 1646600 | tf_op jit(solution)/shard_map/ppermute | solution.py:487
  3.2 4.4 %collective-permute-start = (bf16[1072,256]{1,0:T(8,128)(2,1)S(1)}, bf16[1072,256]{1,0:T(8,128)(2,1)S(1)}, u32[]{:S(2)}, u32[]{:S(2)}) collective-permute-start(bf16[1072,256]{1,0:T(8,128)(2,1)S(1)} %shard_map.120.joined), channel_id=1, source_target_pairs={{0,4},{8,12},{16,20},{24,28},{4,0},{12,8},{20,16},{28,24},{1,5},{9... | collective-permute-start | bytes 1646600 | tf_op jit(solution)/shard_map/ppermute | solution.py:487
  7.6 0.0 copy-start.4
  7.6 0.7 %copy-done.4 = s32[16,16]{1,0:T(8,128)S(1)} copy-done((s32[16,16]{1,0:T(8,128)S(1)}, s32[16,16]{1,0:T(8,128)}, u32[]{:S(2)}) %copy-start.4) | copy-done | bytes 1048
  8.3 8.2 %shard_map.121 = (f32[17,64,256]{2,1,0:T(8,128)S(1)}, bf16[16,128,256]{2,1,0:T(8,128)(2,1)S(1)}, bf16[17,256,128]{2,1,0:T(8,128)(2,1)S(1)}) custom-call(s32[16,16]{1,0:T(8,128)S(1)} %copy-done.4, bf16[1072,256]{1,0:T(8,128)(2,1)S(1)} %shard_map.120.joined), custom_call_target="tpu_custom_call" | custom-call | flops 1207959552 | bytes 549888 | tf_op jit(solution)/shard_map/pallas_call | solution.py:201
  16.5 0.0 collective-permute-done.1.outer
  16.5 0.0 collective-permute-done.inner
  16.5 5.6 %shard_map.122 = (bf16[4,64,256]{2,1,0:T(8,128)(2,1)S(1)}, bf16[4,64,256]{2,1,0:T(8,128)(2,1)S(1)}, bf16[4,64,256]{2,1,0:T(8,128)(2,1)S(1)}, bf16[48,128,256]{2,1,0:T(8,128)(2,1)S(1)}, bf16[48,64,256]{2,1,0:T(8,128)(2,1)S(1)}) custom-call(s32[16,16]{1,0:T(8,128)S(1)} %copy-done.4, bf16[1072,256]{1,0:T(8,128)(2,1)S(1)} %shard_map.120.joined, ...), custom_call_target="tpu_custom_call" | custom-call | flops 1207959552 | bytes 4924416 | tf_op jit(solution)/shard_map/pallas_call | solution.py:201
  22.1 2.1 %collective-permute-start.2 = (bf16[4,64,256]{2,1,0:T(8,128)(2,1)S(1)}, bf16[4,64,256]{2,1,0:T(8,128)(2,1)S(1)}, u32[]{:S(2)}, u32[]{:S(2)}) collective-permute-start(bf16[4,64,256]{2,1,0:T(8,128)(2,1)S(1)} %get-tuple-element.37), channel_id=1, source_target_pairs={{0,1},{1,0},{2,3},{3,2},{4,5},{5,4},{6,7},{7,6},{8,9},{9,8},{10,11... | collective-permute-start | bytes 393224 | tf_op jit(solution)/shard_map/ppermute | solution.py:491
  24.2 1.5 %collective-permute-start.3 = (bf16[4,64,256]{2,1,0:T(8,128)(2,1)S(1)}, bf16[4,64,256]{2,1,0:T(8,128)(2,1)S(1)}, u32[]{:S(2)}, u32[]{:S(2)}) collective-permute-start(bf16[4,64,256]{2,1,0:T(8,128)(2,1)S(1)} %get-tuple-element.38), channel_id=1, source_target_pairs={{0,2},{1,3},{2,0},{3,1},{4,6},{5,7},{6,4},{7,5},{8,10},{9,11},{10,... | collective-permute-start | bytes 393224 | tf_op jit(solution)/shard_map/ppermute | solution.py:491
  25.7 0.0 collective-permute-start.4
  25.7 0.0 copy-start.1
  25.7 0.0 copy-start.2
  25.7 0.0 copy-start.3
  25.7 0.0 copy-start.5
  25.7 0.0 copy-start.6
  25.8 0.0 copy-start.7
  25.8 5.1 %shard_map.123._.own = bf16[4,64,256]{2,1,0:T(8,128)(2,1)S(1)} custom-call(s32[16,16]{1,0:T(8,128)S(1)} %copy-done.4, bf16[48,128,256]{2,1,0:T(8,128)(2,1)S(1)} %get-tuple-element.35.far, bf16[48,64,256]{2,1,0:T(8,128)(2,1)S(1)} %get-tuple-element.36.vectors, bf16[17,256,128]{2,1,0:T(8,128)(2,1)S(1)} %get-tuple-element.33.near), custom_call_target="tpu_custom_call" | custom-call | flops 805306368 | bytes 5833728 | tf_op jit(solution)/shard_map/pallas_call | solution.py:201
  30.9 0.0 copy-done.1
  30.9 0.0 copy-done.2
  30.9 0.0 copy-done.3
  30.9 0.0 copy-done.5
  30.9 0.0 copy-done.6
  30.9 0.0 copy-done.7
  30.9 0.5 shard_map.124
  31.4 0.0 collective-permute-done.2.refs_0_
  31.4 1.3 %collective-permute-done.3.refs_1_ = bf16[4,64,256]{2,1,0:T(8,128)(2,1)S(1)} collective-permute-done((bf16[4,64,256]{2,1,0:T(8,128)(2,1)S(1)}, bf16[4,64,256]{2,1,0:T(8,128)(2,1)S(1)}, u32[]{:S(2)}, u32[]{:S(2)}) %collective-permute-start.3) | collective-permute-done | bytes 131104 | tf_op jit(solution)/shard_map/ppermute | solution.py:491
  32.7 0.0 collective-permute-done.4.refs_2_
  32.7 2.0 %shard_map.125 = (f32[352,256]{1,0:T(8,128)S(1)}, f32[64,256]{1,0:T(8,128)S(1)}) custom-call(bf16[4,64,256]{2,1,0:T(8,128)(2,1)S(1)} %shard_map.123._.own, bf16[4,64,256]{2,1,0:T(8,128)(2,1)S(1)} %collective-permute-done.2.refs_0_, bf16[4,64,256]{2,1,0:T(8,128)(2,1)S(1)} %collective-permute-done.3.refs_1_, ...), custom_call_target="tpu_custom_call" | custom-call | bytes 884736 | tf_op jit(solution)/shard_map/pallas_call | solution.py:442
  34.7 1.2 %collective-permute-start.7 = (f32[64,256]{1,0:T(8,128)S(1)}, f32[64,256]{1,0:T(8,128)S(1)}, u32[]{:S(2)}, u32[]{:S(2)}) collective-permute-start(f32[64,256]{1,0:T(8,128)S(1)} %get-tuple-element.42.own), channel_id=1, source_target_pairs={{0,3},{1,2},{2,1},{3,0},{4,7},{5,6},{6,5},{7,4},{8,11},{9,10},{10,... | collective-permute-start | bytes 196616 | tf_op jit(solution)/shard_map/ppermute | solution.py:491
  36.0 0.8 %collective-permute-start.6 = (f32[64,256]{1,0:T(8,128)S(1)}, f32[64,256]{1,0:T(8,128)S(1)}, u32[]{:S(2)}, u32[]{:S(2)}) collective-permute-start(f32[64,256]{1,0:T(8,128)S(1)} %get-tuple-element.42.own), channel_id=1, source_target_pairs={{0,2},{1,3},{2,0},{3,1},{4,6},{5,7},{6,4},{7,5},{8,10},{9,11},{10,... | collective-permute-start | bytes 196616 | tf_op jit(solution)/shard_map/ppermute | solution.py:491
  36.7 1.6 %collective-permute-start.5 = (f32[64,256]{1,0:T(8,128)S(1)}, f32[64,256]{1,0:T(8,128)S(1)}, u32[]{:S(2)}, u32[]{:S(2)}) collective-permute-start(f32[64,256]{1,0:T(8,128)S(1)} %get-tuple-element.42.own), channel_id=1, source_target_pairs={{0,1},{1,0},{2,3},{3,2},{4,5},{5,4},{6,7},{7,6},{8,9},{9,8},{10,11... | collective-permute-start | bytes 196616 | tf_op jit(solution)/shard_map/ppermute | solution.py:491
  38.3 0.8 %collective-permute-start.12 = (f32[352,256]{1,0:T(8,128)S(1)}, f32[352,256]{1,0:T(8,128)S(1)}, u32[]{:S(2)}, u32[]{:S(2)}) collective-permute-start(f32[352,256]{1,0:T(8,128)S(1)} %get-tuple-element.50.refs_0_), channel_id=1, source_target_pairs={{0,2},{1,3},{2,0},{3,1},{4,6},{5,7},{6,4},{7,5},{8,10},{9,11},{10,... | collective-permute-start | bytes 1081352 | tf_op jit(solution)/shard_map/ppermute | solution.py:491
  39.1 0.9 %collective-permute-start.11 = (f32[352,256]{1,0:T(8,128)S(1)}, f32[352,256]{1,0:T(8,128)S(1)}, u32[]{:S(2)}, u32[]{:S(2)}) collective-permute-start(f32[352,256]{1,0:T(8,128)S(1)} %get-tuple-element.50.refs_0_), channel_id=1, source_target_pairs={{0,1},{1,0},{2,3},{3,2},{4,5},{5,4},{6,7},{7,6},{8,9},{9,8},{10,11... | collective-permute-start | bytes 1081352 | tf_op jit(solution)/shard_map/ppermute | solution.py:491
  40.0 0.7 %collective-permute-done.7.refs_2_ = f32[64,256]{1,0:T(8,128)S(1)} collective-permute-done((f32[64,256]{1,0:T(8,128)S(1)}, f32[64,256]{1,0:T(8,128)S(1)}, u32[]{:S(2)}, u32[]{:S(2)}) %collective-permute-start.7) | collective-permute-done | bytes 65568 | tf_op jit(solution)/shard_map/ppermute | solution.py:491
  40.8 0.7 %collective-permute-done.6.refs_1_ = f32[64,256]{1,0:T(8,128)S(1)} collective-permute-done((f32[64,256]{1,0:T(8,128)S(1)}, f32[64,256]{1,0:T(8,128)S(1)}, u32[]{:S(2)}, u32[]{:S(2)}) %collective-permute-start.6) | collective-permute-done | bytes 65568 | tf_op jit(solution)/shard_map/ppermute | solution.py:491
  41.5 0.2 collective-permute-done.5.refs_0_
  41.7 1.2 %shard_map.126 = (f32[192,128]{1,0:T(8,128)S(1)}, f32[64,256]{1,0:T(8,128)S(1)}) custom-call(f32[64,256]{1,0:T(8,128)S(1)} %get-tuple-element.42.own, f32[64,256]{1,0:T(8,128)S(1)} %collective-permute-done.5.refs_0_, f32[64,256]{1,0:T(8,128)S(1)} %collective-permute-done.6.refs_1_, f32[64,256]{1,0:T(8,128)S(1)} %collective-permute-done.7.refs_2_, ...), custom_call_target="tpu_custom_call" | custom-call | bytes 360448 | tf_op jit(solution)/shard_map/pallas_call | solution.py:442
  42.9 0.1 collective-permute-start.8
  43.0 1.2 %collective-permute-done.8.arrived = f32[64,256]{1,0:T(8,128)S(1)} collective-permute-done((f32[64,256]{1,0:T(8,128)S(1)}, f32[64,256]{1,0:T(8,128)S(1)}, u32[]{:S(2)}, u32[]{:S(2)}) %collective-permute-start.8) | collective-permute-done | bytes 65568 | tf_op jit(solution)/shard_map/ppermute | solution.py:570
  44.2 0.5 shard_map.127
  44.7 0.9 %collective-permute-start.9 = (f32[64,256]{1,0:T(8,128)S(1)}, f32[64,256]{1,0:T(8,128)S(1)}, u32[]{:S(2)}, u32[]{:S(2)}) collective-permute-start(f32[64,256]{1,0:T(8,128)S(1)} %get-tuple-element.46.own), channel_id=1, source_target_pairs={{0,8},{4,12},{8,0},{12,4},{16,24},{20,28},{24,16},{28,20},{1,9},{5... | collective-permute-start | bytes 196616 | tf_op jit(solution)/shard_map/ppermute | solution.py:570
  45.6 3.5 %collective-permute-done.9.arrived = f32[64,256]{1,0:T(8,128)S(1)} collective-permute-done((f32[64,256]{1,0:T(8,128)S(1)}, f32[64,256]{1,0:T(8,128)S(1)}, u32[]{:S(2)}, u32[]{:S(2)}) %collective-permute-start.9) | collective-permute-done | bytes 65568 | tf_op jit(solution)/shard_map/ppermute | solution.py:570
  49.0 0.5 shard_map.128
  49.5 0.0 collective-permute-done.12.there.refs_2_
  49.5 0.0 collective-permute-done.11.here.refs_1_
  49.6 1.3 %collective-permute-start.13 = (f32[192,256]{1,0:T(8,128)S(1)}, f32[192,256]{1,0:T(8,128)S(1)}, u32[]{:S(2)}, u32[]{:S(2)}) collective-permute-start(f32[192,256]{1,0:T(8,128)S(1)} %get-tuple-element.51), channel_id=1, source_target_pairs={{0,2},{1,3},{2,0},{3,1},{4,6},{5,7},{6,4},{7,5},{8,10},{9,11},{10,... | collective-permute-start | bytes 589832 | tf_op jit(solution)/shard_map/ppermute | solution.py:491
  50.9 1.1 %collective-permute-start.14 = (f32[160,256]{1,0:T(8,128)S(1)}, f32[160,256]{1,0:T(8,128)S(1)}, u32[]{:S(2)}, u32[]{:S(2)}) collective-permute-start(f32[160,256]{1,0:T(8,128)S(1)} %get-tuple-element.52), channel_id=1, source_target_pairs={{0,1},{1,0},{2,3},{3,2},{4,5},{5,4},{6,7},{7,6},{8,9},{9,8},{10,11... | collective-permute-start | bytes 491528 | tf_op jit(solution)/shard_map/ppermute | solution.py:491
  52.0 2.6 %collective-permute-start.10 = (f32[64,256]{1,0:T(8,128)S(1)}, f32[64,256]{1,0:T(8,128)S(1)}, u32[]{:S(2)}, u32[]{:S(2)}) collective-permute-start(f32[64,256]{1,0:T(8,128)S(1)} %get-tuple-element.47._.own), channel_id=1, source_target_pairs={{0,16},{4,20},{8,24},{12,28},{16,0},{20,4},{24,8},{28,12},{1,17},{... | collective-permute-start | bytes 196616 | tf_op jit(solution)/shard_map/ppermute | solution.py:570
  54.6 1.1 %shard_map.130 = (f32[1024,256]{1,0:T(8,128)}, f32[960,128]{1,0:T(8,128)}) custom-call(f32[352,256]{1,0:T(8,128)S(1)} %get-tuple-element.50.refs_0_, f32[352,256]{1,0:T(8,128)S(1)} %collective-permute-done.11.here.refs_1_, f32[352,256]{1,0:T(8,128)S(1)} %collective-permute-done.12.there.refs_2_, f32[192,128]{1,0:T(8,128)S(1)} %get-tuple-element.53.refs_3_), custom_call_target="tpu_custom_call" | custom-call | flops 950000000 | bytes 1179648 | tf_op jit(solution)/shard_map/pallas_call | solution.py:442
  55.8 2.0 %collective-permute-done.10.arrived = f32[64,256]{1,0:T(8,128)S(1)} collective-permute-done((f32[64,256]{1,0:T(8,128)S(1)}, f32[64,256]{1,0:T(8,128)S(1)}, u32[]{:S(2)}, u32[]{:S(2)}) %collective-permute-start.10) | collective-permute-done | bytes 65568 | tf_op jit(solution)/shard_map/ppermute | solution.py:570
  57.8 0.0 collective-permute-done.14.refs_3_
  57.8 0.0 collective-permute-done.13.refs_2_
  57.8 1.7 %shard_map.131 = (f32[3,64,128]{2,1,0:T(8,128)}, f32[64,64]{1,0:T(8,128)}, f32[1024,256]{1,0:T(8,128)}, f32[960,128]{1,0:T(8,128)}) custom-call(f32[64,256]{1,0:T(8,128)S(1)} %get-tuple-element.47._.own, f32[64,256]{1,0:T(8,128)S(1)} %collective-permute-done.10.arrived, ...), custom_call_target="tpu_custom_call", output_to_operand_aliasing={{2}: (7, {}), {3}: (8, {})} | custom-call | flops 950000000 | bytes 2195456 | tf_op jit(solution)/shard_map/pallas_call | solution.py:442
  (2 shorter events, 0.1 us)
Async XLA Ops:
  1.4 1.0 %copy-start = (bf16[16,64,256]{2,1,0:T(8,128)(2,1)S(1)}, bf16[16,64,256]{2,1,0:T(8,128)(2,1)}, u32[]{:S(2)}) copy-start(bf16[16,64,256]{2,1,0:T(8,128)(2,1)} %probe.1) | copy-start | bytes 1572868
  2.5 14.0 %collective-permute-start.1 = (bf16[1072,256]{1,0:T(8,128)(2,1)S(1)}, bf16[1072,256]{1,0:T(8,128)(2,1)S(1)}, u32[]{:S(2)}, u32[]{:S(2)}) collective-permute-start(bf16[1072,256]{1,0:T(8,128)(2,1)S(1)} %shard_map.120.joined), channel_id=1, source_target_pairs={{4,8},{12,16},{20,24},{8,4},{16,12},{24,20},{5,9},{13,17},{21,25},... | collective-permute-start | bytes 1646600 | tf_op jit(solution)/shard_map/ppermute | solution.py:487
  3.2 13.3 %collective-permute-start = (bf16[1072,256]{1,0:T(8,128)(2,1)S(1)}, bf16[1072,256]{1,0:T(8,128)(2,1)S(1)}, u32[]{:S(2)}, u32[]{:S(2)}) collective-permute-start(bf16[1072,256]{1,0:T(8,128)(2,1)S(1)} %shard_map.120.joined), channel_id=1, source_target_pairs={{0,4},{8,12},{16,20},{24,28},{4,0},{12,8},{20,16},{28,24},{1,5},{9... | collective-permute-start | bytes 1646600 | tf_op jit(solution)/shard_map/ppermute | solution.py:487
  7.6 0.7 %copy-start.4 = (s32[16,16]{1,0:T(8,128)S(1)}, s32[16,16]{1,0:T(8,128)}, u32[]{:S(2)}) copy-start(s32[16,16]{1,0:T(8,128)} %nb_ref.5) | copy-start | bytes 3076
  22.1 9.3 %collective-permute-start.2 = (bf16[4,64,256]{2,1,0:T(8,128)(2,1)S(1)}, bf16[4,64,256]{2,1,0:T(8,128)(2,1)S(1)}, u32[]{:S(2)}, u32[]{:S(2)}) collective-permute-start(bf16[4,64,256]{2,1,0:T(8,128)(2,1)S(1)} %get-tuple-element.37), channel_id=1, source_target_pairs={{0,1},{1,0},{2,3},{3,2},{4,5},{5,4},{6,7},{7,6},{8,9},{9,8},{10,11... | collective-permute-start | bytes 393224 | tf_op jit(solution)/shard_map/ppermute | solution.py:491
  24.2 8.5 %collective-permute-start.3 = (bf16[4,64,256]{2,1,0:T(8,128)(2,1)S(1)}, bf16[4,64,256]{2,1,0:T(8,128)(2,1)S(1)}, u32[]{:S(2)}, u32[]{:S(2)}) collective-permute-start(bf16[4,64,256]{2,1,0:T(8,128)(2,1)S(1)} %get-tuple-element.38), channel_id=1, source_target_pairs={{0,2},{1,3},{2,0},{3,1},{4,6},{5,7},{6,4},{7,5},{8,10},{9,11},{10,... | collective-permute-start | bytes 393224 | tf_op jit(solution)/shard_map/ppermute | solution.py:491
  25.7 7.0 %collective-permute-start.4 = (bf16[4,64,256]{2,1,0:T(8,128)(2,1)S(1)}, bf16[4,64,256]{2,1,0:T(8,128)(2,1)S(1)}, u32[]{:S(2)}, u32[]{:S(2)}) collective-permute-start(bf16[4,64,256]{2,1,0:T(8,128)(2,1)S(1)} %get-tuple-element.39), channel_id=1, source_target_pairs={{0,3},{1,2},{2,1},{3,0},{4,7},{5,6},{6,5},{7,4},{8,11},{9,10},{10,... | collective-permute-start | bytes 393224 | tf_op jit(solution)/shard_map/ppermute | solution.py:491
  25.7 5.1 %copy-start.1 = (f32[16,64,64]{2,1,0:T(8,128)S(1)}, f32[16,64,64]{2,1,0:T(8,128)}, u32[]{:S(2)}) copy-start(f32[16,64,64]{2,1,0:T(8,128)} %leaf_inverse.1) | copy-start | bytes 786436
  25.7 5.1 %copy-start.2 = (f32[15,64,64]{2,1,0:T(8,128)S(1)}, f32[15,64,64]{2,1,0:T(8,128)}, u32[]{:S(2)}) copy-start(f32[15,64,64]{2,1,0:T(8,128)} %local_inverse.1) | copy-start | bytes 737284
  25.7 5.1 %copy-start.3 = (f32[7,64,64]{2,1,0:T(8,128)S(1)}, f32[7,64,64]{2,1,0:T(8,128)}, u32[]{:S(2)}) copy-start(f32[7,64,64]{2,1,0:T(8,128)} %upper_inverse.1) | copy-start | bytes 344068
  25.7 5.2 %copy-start.5 = (s32[16,64]{1,0:T(8,128)S(1)}, s32[16,64]{1,0:T(8,128)}, u32[]{:S(2)}) copy-start(s32[16,64]{1,0:T(8,128)} %leaf_pivots.1) | copy-start | bytes 12292
  25.7 5.2 %copy-start.6 = (s32[15,64]{1,0:T(8,128)S(1)}, s32[15,64]{1,0:T(8,128)}, u32[]{:S(2)}) copy-start(s32[15,64]{1,0:T(8,128)} %local_pivots.1) | copy-start | bytes 11524
  25.8 5.2 %copy-start.7 = (s32[7,64]{1,0:T(8,128)S(1)}, s32[7,64]{1,0:T(8,128)}, u32[]{:S(2)}) copy-start(s32[7,64]{1,0:T(8,128)} %upper_pivots.1) | copy-start | bytes 5380
  34.7 6.0 %collective-permute-start.7 = (f32[64,256]{1,0:T(8,128)S(1)}, f32[64,256]{1,0:T(8,128)S(1)}, u32[]{:S(2)}, u32[]{:S(2)}) collective-permute-start(f32[64,256]{1,0:T(8,128)S(1)} %get-tuple-element.42.own), channel_id=1, source_target_pairs={{0,3},{1,2},{2,1},{3,0},{4,7},{5,6},{6,5},{7,4},{8,11},{9,10},{10,... | collective-permute-start | bytes 196616 | tf_op jit(solution)/shard_map/ppermute | solution.py:491
  36.0 5.5 %collective-permute-start.6 = (f32[64,256]{1,0:T(8,128)S(1)}, f32[64,256]{1,0:T(8,128)S(1)}, u32[]{:S(2)}, u32[]{:S(2)}) collective-permute-start(f32[64,256]{1,0:T(8,128)S(1)} %get-tuple-element.42.own), channel_id=1, source_target_pairs={{0,2},{1,3},{2,0},{3,1},{4,6},{5,7},{6,4},{7,5},{8,10},{9,11},{10,... | collective-permute-start | bytes 196616 | tf_op jit(solution)/shard_map/ppermute | solution.py:491
  36.7 5.0 %collective-permute-start.5 = (f32[64,256]{1,0:T(8,128)S(1)}, f32[64,256]{1,0:T(8,128)S(1)}, u32[]{:S(2)}, u32[]{:S(2)}) collective-permute-start(f32[64,256]{1,0:T(8,128)S(1)} %get-tuple-element.42.own), channel_id=1, source_target_pairs={{0,1},{1,0},{2,3},{3,2},{4,5},{5,4},{6,7},{7,6},{8,9},{9,8},{10,11... | collective-permute-start | bytes 196616 | tf_op jit(solution)/shard_map/ppermute | solution.py:491
  38.3 11.2 %collective-permute-start.12 = (f32[352,256]{1,0:T(8,128)S(1)}, f32[352,256]{1,0:T(8,128)S(1)}, u32[]{:S(2)}, u32[]{:S(2)}) collective-permute-start(f32[352,256]{1,0:T(8,128)S(1)} %get-tuple-element.50.refs_0_), channel_id=1, source_target_pairs={{0,2},{1,3},{2,0},{3,1},{4,6},{5,7},{6,4},{7,5},{8,10},{9,11},{10,... | collective-permute-start | bytes 1081352 | tf_op jit(solution)/shard_map/ppermute | solution.py:491
  39.1 10.4 %collective-permute-start.11 = (f32[352,256]{1,0:T(8,128)S(1)}, f32[352,256]{1,0:T(8,128)S(1)}, u32[]{:S(2)}, u32[]{:S(2)}) collective-permute-start(f32[352,256]{1,0:T(8,128)S(1)} %get-tuple-element.50.refs_0_), channel_id=1, source_target_pairs={{0,1},{1,0},{2,3},{3,2},{4,5},{5,4},{6,7},{7,6},{8,9},{9,8},{10,11... | collective-permute-start | bytes 1081352 | tf_op jit(solution)/shard_map/ppermute | solution.py:491
  42.9 1.3 %collective-permute-start.8 = (f32[64,256]{1,0:T(8,128)S(1)}, f32[64,256]{1,0:T(8,128)S(1)}, u32[]{:S(2)}, u32[]{:S(2)}) collective-permute-start(f32[64,256]{1,0:T(8,128)S(1)} %get-tuple-element.44.own), channel_id=1, source_target_pairs={{0,4},{4,0},{8,12},{12,8},{16,20},{20,16},{24,28},{28,24},{1,5},{5... | collective-permute-start | bytes 196616 | tf_op jit(solution)/shard_map/ppermute | solution.py:570
  44.7 4.3 %collective-permute-start.9 = (f32[64,256]{1,0:T(8,128)S(1)}, f32[64,256]{1,0:T(8,128)S(1)}, u32[]{:S(2)}, u32[]{:S(2)}) collective-permute-start(f32[64,256]{1,0:T(8,128)S(1)} %get-tuple-element.46.own), channel_id=1, source_target_pairs={{0,8},{4,12},{8,0},{12,4},{16,24},{20,28},{24,16},{28,20},{1,9},{5... | collective-permute-start | bytes 196616 | tf_op jit(solution)/shard_map/ppermute | solution.py:570
  49.6 8.2 %collective-permute-start.13 = (f32[192,256]{1,0:T(8,128)S(1)}, f32[192,256]{1,0:T(8,128)S(1)}, u32[]{:S(2)}, u32[]{:S(2)}) collective-permute-start(f32[192,256]{1,0:T(8,128)S(1)} %get-tuple-element.51), channel_id=1, source_target_pairs={{0,2},{1,3},{2,0},{3,1},{4,6},{5,7},{6,4},{7,5},{8,10},{9,11},{10,... | collective-permute-start | bytes 589832 | tf_op jit(solution)/shard_map/ppermute | solution.py:491
  50.9 6.9 %collective-permute-start.14 = (f32[160,256]{1,0:T(8,128)S(1)}, f32[160,256]{1,0:T(8,128)S(1)}, u32[]{:S(2)}, u32[]{:S(2)}) collective-permute-start(f32[160,256]{1,0:T(8,128)S(1)} %get-tuple-element.52), channel_id=1, source_target_pairs={{0,1},{1,0},{2,3},{3,2},{4,5},{5,4},{6,7},{7,6},{8,9},{9,8},{10,11... | collective-permute-start | bytes 491528 | tf_op jit(solution)/shard_map/ppermute | solution.py:491
  52.0 5.8 %collective-permute-start.10 = (f32[64,256]{1,0:T(8,128)S(1)}, f32[64,256]{1,0:T(8,128)S(1)}, u32[]{:S(2)}, u32[]{:S(2)}) collective-permute-start(f32[64,256]{1,0:T(8,128)S(1)} %get-tuple-element.47._.own), channel_id=1, source_target_pairs={{0,16},{4,20},{8,24},{12,28},{16,0},{20,4},{24,8},{28,12},{1,17},{... | collective-permute-start | bytes 196616 | tf_op jit(solution)/shard_map/ppermute | solution.py:570

commit v3 on v2

--- a/solution.py
+++ b/solution.py
@@ -113,8 +113,12 @@
             evaluate(codes[(index + 1) * flight + way], tiles.at[way])
         return carry
 
+    def two_steps(index, carry):
+        return step(2 * index + 1, step(2 * index, carry))
+
     steps = (filled - 1) // flight
-    lax.fori_loop(0, steps, step, 0)
+    lax.fori_loop(0, steps // 2, two_steps, 0)
+    lax.fori_loop(steps // 2 * 2, steps, step, 0)
     for way in range(flight):
         multiply(codes[steps * flight + way], tiles.at[way])
 

time: 59.4 us -> 58.4 us (0.983); the launches traced: 59.5 us -> 57.6 us
  Pallas kernels: 26.4 us -> 24.5 us
  waiting for transfers between devices: 9.72 us -> 9.1 us
  starting transfers between devices: 20 us -> 20.6 us
    pallas_call x3, Pallas kernels: 18.9 us -> 17 us  [near_call(): pl.pallas_call(body, out_shape=outs, in_specs=[pl.BlockSpec(memory_space=...]
    ppermute x3, waiting for transfers between devices: 6.75 us -> 5.72 us  [on_device(): lax.ppermute(own_up, 'leaf', [(i, i ^ 1 << tier) for i in range(leaf_tota...]
  transfers between devices with their start and end apart: 15 -> 15, of which waited for: 7 -> 6; matrix products, arithmetic and copies ran while one was open for 0% -> 0% of each run, Pallas kernels for 29% -> 26%
where the time goes in v3:
time: 58.4 us; the launch traced here: 57.6 us
  Pallas kernels  24.5 us (42%)
  starting transfers between devices  20.6 us (35%)
  waiting for transfers between devices  9.1 us (16%)
  local copies, waits for them, and re-layouts  2.52 us (4%)
  between operations  0.84 us (1%)
    pallas_call x3, Pallas kernels, near_call(): pl.pallas_call(body, out_shape=outs, in_specs=[pl.BlockSpec(memory_space=...  17 us
    ppermute x10, starting transfers between devices, vec_send(): return lax.ppermute(array, 'vec', [(i, i ^ tier) for i in range(parts)])  11.5 us
    pallas_call x9, Pallas kernels, call(): pl.pallas_call(body, out_shape=outs, in_specs=[fixed] * (len(operands) -...  7.57 us
    ppermute x3, waiting for transfers between devices, on_device(): lax.ppermute(own_up, 'leaf', [(i, i ^ 1 << tier) for i in range(leaf_tota...  5.72 us
    ppermute x2, starting transfers between devices, on_device(): lax.ppermute(joined, 'leaf', pairs + [(j, i) for i, j in pairs])  5.11 us
    ppermute x3, starting transfers between devices, on_device(): lax.ppermute(own_up, 'leaf', [(i, i ^ 1 << tier) for i in range(leaf_tota...  3.94 us
    ppermute x10, waiting for transfers between devices, vec_send(): return lax.ppermute(array, 'vec', [(i, i ^ tier) for i in range(parts)])  3.37 us
    unnamed x17, local copies, waits for them, and re-layouts  2.52 us
  transfers between devices with their start and end apart: 15, of which 6 were waited for; matrix products, arithmetic and copies ran while one was open for 0% of the time, Pallas kernels for 26%

profile of v3, /device:TPU:0, one launch (start us, length us, event | category | flops | bytes accessed | tf_op | source)
XLA Modules:
  0.0 57.6 jit_solution(10103050167205962786)
XLA Ops:
  0.6 0.8 %copy.15.points = bf16[16,3,256]{2,1,0:T(4,128)(2,1)S(1)} copy(bf16[16,3,256]{2,0,1:T(8,128)(2,1)} %param.9) | data formatting | bytes 49152 | tf_op args[0]
  1.4 0.0 copy-start
  1.4 1.0 %copy-done = bf16[16,64,256]{2,1,0:T(8,128)(2,1)S(1)} copy-done((bf16[16,64,256]{2,1,0:T(8,128)(2,1)S(1)}, bf16[16,64,256]{2,1,0:T(8,128)(2,1)}, u32[]{:S(2)}) %copy-start) | copy-done | bytes 524312
  2.5 0.7 %collective-permute-start.1 = (bf16[1072,256]{1,0:T(8,128)(2,1)S(1)}, bf16[1072,256]{1,0:T(8,128)(2,1)S(1)}, u32[]{:S(2)}, u32[]{:S(2)}) collective-permute-start(bf16[1072,256]{1,0:T(8,128)(2,1)S(1)} %shard_map.120.joined), channel_id=1, source_target_pairs={{4,8},{12,16},{20,24},{8,4},{16,12},{24,20},{5,9},{13,17},{21,25},... | collective-permute-start | bytes 1646600 | tf_op jit(solution)/shard_map/ppermute | solution.py:491
  3.2 4.4 %collective-permute-start = (bf16[1072,256]{1,0:T(8,128)(2,1)S(1)}, bf16[1072,256]{1,0:T(8,128)(2,1)S(1)}, u32[]{:S(2)}, u32[]{:S(2)}) collective-permute-start(bf16[1072,256]{1,0:T(8,128)(2,1)S(1)} %shard_map.120.joined), channel_id=1, source_target_pairs={{0,4},{8,12},{16,20},{24,28},{4,0},{12,8},{20,16},{28,24},{1,5},{9... | collective-permute-start | bytes 1646600 | tf_op jit(solution)/shard_map/ppermute | solution.py:491
  7.6 0.0 copy-start.4
  7.6 0.7 %copy-done.4 = s32[16,16]{1,0:T(8,128)S(1)} copy-done((s32[16,16]{1,0:T(8,128)S(1)}, s32[16,16]{1,0:T(8,128)}, u32[]{:S(2)}) %copy-start.4) | copy-done | bytes 1048
  8.3 7.4 %shard_map.121 = (f32[17,64,256]{2,1,0:T(8,128)S(1)}, bf16[16,128,256]{2,1,0:T(8,128)(2,1)S(1)}, bf16[17,256,128]{2,1,0:T(8,128)(2,1)S(1)}) custom-call(s32[16,16]{1,0:T(8,128)S(1)} %copy-done.4, bf16[1072,256]{1,0:T(8,128)(2,1)S(1)} %shard_map.120.joined), custom_call_target="tpu_custom_call" | custom-call | flops 1207959552 | bytes 549888 | tf_op jit(solution)/shard_map/pallas_call | solution.py:205
  15.7 0.0 collective-permute-done.1.outer
  15.7 0.0 collective-permute-done.inner
  15.7 5.6 %shard_map.122 = (bf16[4,64,256]{2,1,0:T(8,128)(2,1)S(1)}, bf16[4,64,256]{2,1,0:T(8,128)(2,1)S(1)}, bf16[4,64,256]{2,1,0:T(8,128)(2,1)S(1)}, bf16[48,128,256]{2,1,0:T(8,128)(2,1)S(1)}, bf16[48,64,256]{2,1,0:T(8,128)(2,1)S(1)}) custom-call(s32[16,16]{1,0:T(8,128)S(1)} %copy-done.4, bf16[1072,256]{1,0:T(8,128)(2,1)S(1)} %shard_map.120.joined, ...), custom_call_target="tpu_custom_call" | custom-call | flops 1207959552 | bytes 4924416 | tf_op jit(solution)/shard_map/pallas_call | solution.py:205
  21.3 1.6 %collective-permute-start.2 = (bf16[4,64,256]{2,1,0:T(8,128)(2,1)S(1)}, bf16[4,64,256]{2,1,0:T(8,128)(2,1)S(1)}, u32[]{:S(2)}, u32[]{:S(2)}) collective-permute-start(bf16[4,64,256]{2,1,0:T(8,128)(2,1)S(1)} %get-tuple-element.37), channel_id=1, source_target_pairs={{0,1},{1,0},{2,3},{3,2},{4,5},{5,4},{6,7},{7,6},{8,9},{9,8},{10,11... | collective-permute-start | bytes 393224 | tf_op jit(solution)/shard_map/ppermute | solution.py:495
  22.8 1.5 %collective-permute-start.3 = (bf16[4,64,256]{2,1,0:T(8,128)(2,1)S(1)}, bf16[4,64,256]{2,1,0:T(8,128)(2,1)S(1)}, u32[]{:S(2)}, u32[]{:S(2)}) collective-permute-start(bf16[4,64,256]{2,1,0:T(8,128)(2,1)S(1)} %get-tuple-element.38), channel_id=1, source_target_pairs={{0,2},{1,3},{2,0},{3,1},{4,6},{5,7},{6,4},{7,5},{8,10},{9,11},{10,... | collective-permute-start | bytes 393224 | tf_op jit(solution)/shard_map/ppermute | solution.py:495
  24.4 0.5 collective-permute-start.4
  24.8 0.0 copy-start.1
  24.8 0.0 copy-start.2
  24.8 0.0 copy-start.3
  24.8 0.0 copy-start.5
  24.9 0.0 copy-start.6
  24.9 0.0 copy-start.7
  24.9 4.0 %shard_map.123._.own = bf16[4,64,256]{2,1,0:T(8,128)(2,1)S(1)} custom-call(s32[16,16]{1,0:T(8,128)S(1)} %copy-done.4, bf16[48,128,256]{2,1,0:T(8,128)(2,1)S(1)} %get-tuple-element.35.far, bf16[48,64,256]{2,1,0:T(8,128)(2,1)S(1)} %get-tuple-element.36.vectors, bf16[17,256,128]{2,1,0:T(8,128)(2,1)S(1)} %get-tuple-element.33.near), custom_call_target="tpu_custom_call" | custom-call | flops 805306368 | bytes 5833728 | tf_op jit(solution)/shard_map/pallas_call | solution.py:205
  28.9 0.0 copy-done.1
  28.9 0.0 copy-done.2
  28.9 0.0 copy-done.3
  28.9 0.0 copy-done.5
  29.0 0.0 copy-done.6
  29.0 0.0 copy-done.7
  29.0 0.5 shard_map.124
  29.4 0.0 collective-permute-done.2.refs_0_
  29.5 1.2 %collective-permute-done.3.refs_1_ = bf16[4,64,256]{2,1,0:T(8,128)(2,1)S(1)} collective-permute-done((bf16[4,64,256]{2,1,0:T(8,128)(2,1)S(1)}, bf16[4,64,256]{2,1,0:T(8,128)(2,1)S(1)}, u32[]{:S(2)}, u32[]{:S(2)}) %collective-permute-start.3) | collective-permute-done | bytes 131104 | tf_op jit(solution)/shard_map/ppermute | solution.py:495
  30.6 0.0 collective-permute-done.4.refs_2_
  30.6 2.0 %shard_map.125 = (f32[352,256]{1,0:T(8,128)S(1)}, f32[64,256]{1,0:T(8,128)S(1)}) custom-call(bf16[4,64,256]{2,1,0:T(8,128)(2,1)S(1)} %shard_map.123._.own, bf16[4,64,256]{2,1,0:T(8,128)(2,1)S(1)} %collective-permute-done.2.refs_0_, bf16[4,64,256]{2,1,0:T(8,128)(2,1)S(1)} %collective-permute-done.3.refs_1_, ...), custom_call_target="tpu_custom_call" | custom-call | bytes 884736 | tf_op jit(solution)/shard_map/pallas_call | solution.py:446
  32.7 1.6 %collective-permute-start.7 = (f32[64,256]{1,0:T(8,128)S(1)}, f32[64,256]{1,0:T(8,128)S(1)}, u32[]{:S(2)}, u32[]{:S(2)}) collective-permute-start(f32[64,256]{1,0:T(8,128)S(1)} %get-tuple-element.42.own), channel_id=1, source_target_pairs={{0,3},{1,2},{2,1},{3,0},{4,7},{5,6},{6,5},{7,4},{8,11},{9,10},{10,... | collective-permute-start | bytes 196616 | tf_op jit(solution)/shard_map/ppermute | solution.py:495
  34.3 1.2 %collective-permute-start.6 = (f32[64,256]{1,0:T(8,128)S(1)}, f32[64,256]{1,0:T(8,128)S(1)}, u32[]{:S(2)}, u32[]{:S(2)}) collective-permute-start(f32[64,256]{1,0:T(8,128)S(1)} %get-tuple-element.42.own), channel_id=1, source_target_pairs={{0,2},{1,3},{2,0},{3,1},{4,6},{5,7},{6,4},{7,5},{8,10},{9,11},{10,... | collective-permute-start | bytes 196616 | tf_op jit(solution)/shard_map/ppermute | solution.py:495
  35.5 0.8 %collective-permute-start.5 = (f32[64,256]{1,0:T(8,128)S(1)}, f32[64,256]{1,0:T(8,128)S(1)}, u32[]{:S(2)}, u32[]{:S(2)}) collective-permute-start(f32[64,256]{1,0:T(8,128)S(1)} %get-tuple-element.42.own), channel_id=1, source_target_pairs={{0,1},{1,0},{2,3},{3,2},{4,5},{5,4},{6,7},{7,6},{8,9},{9,8},{10,11... | collective-permute-start | bytes 196616 | tf_op jit(solution)/shard_map/ppermute | solution.py:495
  36.3 1.5 %collective-permute-start.12 = (f32[352,256]{1,0:T(8,128)S(1)}, f32[352,256]{1,0:T(8,128)S(1)}, u32[]{:S(2)}, u32[]{:S(2)}) collective-permute-start(f32[352,256]{1,0:T(8,128)S(1)} %get-tuple-element.50.refs_0_), channel_id=1, source_target_pairs={{0,2},{1,3},{2,0},{3,1},{4,6},{5,7},{6,4},{7,5},{8,10},{9,11},{10,... | collective-permute-start | bytes 1081352 | tf_op jit(solution)/shard_map/ppermute | solution.py:495
  37.8 0.5 collective-permute-start.11
  38.3 0.0 collective-permute-done.7.refs_2_
  38.3 1.1 %collective-permute-done.6.refs_1_ = f32[64,256]{1,0:T(8,128)S(1)} collective-permute-done((f32[64,256]{1,0:T(8,128)S(1)}, f32[64,256]{1,0:T(8,128)S(1)}, u32[]{:S(2)}, u32[]{:S(2)}) %collective-permute-start.6) | collective-permute-done | bytes 65568 | tf_op jit(solution)/shard_map/ppermute | solution.py:495
  39.5 1.0 %collective-permute-done.5.refs_0_ = f32[64,256]{1,0:T(8,128)S(1)} collective-permute-done((f32[64,256]{1,0:T(8,128)S(1)}, f32[64,256]{1,0:T(8,128)S(1)}, u32[]{:S(2)}, u32[]{:S(2)}) %collective-permute-start.5) | collective-permute-done | bytes 65568 | tf_op jit(solution)/shard_map/ppermute | solution.py:495
  40.5 1.2 %shard_map.126 = (f32[192,128]{1,0:T(8,128)S(1)}, f32[64,256]{1,0:T(8,128)S(1)}) custom-call(f32[64,256]{1,0:T(8,128)S(1)} %get-tuple-element.42.own, f32[64,256]{1,0:T(8,128)S(1)} %collective-permute-done.5.refs_0_, f32[64,256]{1,0:T(8,128)S(1)} %collective-permute-done.6.refs_1_, f32[64,256]{1,0:T(8,128)S(1)} %collective-permute-done.7.refs_2_, ...), custom_call_target="tpu_custom_call" | custom-call | bytes 360448 | tf_op jit(solution)/shard_map/pallas_call | solution.py:446
  41.7 0.1 collective-permute-start.8
  41.8 1.2 %collective-permute-done.8.arrived = f32[64,256]{1,0:T(8,128)S(1)} collective-permute-done((f32[64,256]{1,0:T(8,128)S(1)}, f32[64,256]{1,0:T(8,128)S(1)}, u32[]{:S(2)}, u32[]{:S(2)}) %collective-permute-start.8) | collective-permute-done | bytes 65568 | tf_op jit(solution)/shard_map/ppermute | solution.py:574
  43.0 0.5 shard_map.127
  43.5 1.7 %collective-permute-start.9 = (f32[64,256]{1,0:T(8,128)S(1)}, f32[64,256]{1,0:T(8,128)S(1)}, u32[]{:S(2)}, u32[]{:S(2)}) collective-permute-start(f32[64,256]{1,0:T(8,128)S(1)} %get-tuple-element.46.own), channel_id=1, source_target_pairs={{0,8},{4,12},{8,0},{12,4},{16,24},{20,28},{24,16},{28,20},{1,9},{5... | collective-permute-start | bytes 196616 | tf_op jit(solution)/shard_map/ppermute | solution.py:574
  45.2 2.6 %collective-permute-done.9.arrived = f32[64,256]{1,0:T(8,128)S(1)} collective-permute-done((f32[64,256]{1,0:T(8,128)S(1)}, f32[64,256]{1,0:T(8,128)S(1)}, u32[]{:S(2)}, u32[]{:S(2)}) %collective-permute-start.9) | collective-permute-done | bytes 65568 | tf_op jit(solution)/shard_map/ppermute | solution.py:574
  47.8 0.5 shard_map.128
  48.3 0.0 collective-permute-done.12.there.refs_2_
  48.3 0.0 collective-permute-done.11.here.refs_1_
  48.3 1.2 %collective-permute-start.13 = (f32[192,256]{1,0:T(8,128)S(1)}, f32[192,256]{1,0:T(8,128)S(1)}, u32[]{:S(2)}, u32[]{:S(2)}) collective-permute-start(f32[192,256]{1,0:T(8,128)S(1)} %get-tuple-element.51), channel_id=1, source_target_pairs={{0,2},{1,3},{2,0},{3,1},{4,6},{5,7},{6,4},{7,5},{8,10},{9,11},{10,... | collective-permute-start | bytes 589832 | tf_op jit(solution)/shard_map/ppermute | solution.py:495
  49.5 1.2 %collective-permute-start.14 = (f32[160,256]{1,0:T(8,128)S(1)}, f32[160,256]{1,0:T(8,128)S(1)}, u32[]{:S(2)}, u32[]{:S(2)}) collective-permute-start(f32[160,256]{1,0:T(8,128)S(1)} %get-tuple-element.52), channel_id=1, source_target_pairs={{0,1},{1,0},{2,3},{3,2},{4,5},{5,4},{6,7},{7,6},{8,9},{9,8},{10,11... | collective-permute-start | bytes 491528 | tf_op jit(solution)/shard_map/ppermute | solution.py:495
  50.7 2.1 %collective-permute-start.10 = (f32[64,256]{1,0:T(8,128)S(1)}, f32[64,256]{1,0:T(8,128)S(1)}, u32[]{:S(2)}, u32[]{:S(2)}) collective-permute-start(f32[64,256]{1,0:T(8,128)S(1)} %get-tuple-element.47._.own), channel_id=1, source_target_pairs={{0,16},{4,20},{8,24},{12,28},{16,0},{20,4},{24,8},{28,12},{1,17},{... | collective-permute-start | bytes 196616 | tf_op jit(solution)/shard_map/ppermute | solution.py:574
  52.9 1.1 %shard_map.130 = (f32[1024,256]{1,0:T(8,128)}, f32[960,128]{1,0:T(8,128)}) custom-call(f32[352,256]{1,0:T(8,128)S(1)} %get-tuple-element.50.refs_0_, f32[352,256]{1,0:T(8,128)S(1)} %collective-permute-done.11.here.refs_1_, f32[352,256]{1,0:T(8,128)S(1)} %collective-permute-done.12.there.refs_2_, f32[192,128]{1,0:T(8,128)S(1)} %get-tuple-element.53.refs_3_), custom_call_target="tpu_custom_call" | custom-call | flops 950000000 | bytes 1179648 | tf_op jit(solution)/shard_map/pallas_call | solution.py:446
  54.0 1.9 %collective-permute-done.10.arrived = f32[64,256]{1,0:T(8,128)S(1)} collective-permute-done((f32[64,256]{1,0:T(8,128)S(1)}, f32[64,256]{1,0:T(8,128)S(1)}, u32[]{:S(2)}, u32[]{:S(2)}) %collective-permute-start.10) | collective-permute-done | bytes 65568 | tf_op jit(solution)/shard_map/ppermute | solution.py:574
  55.9 0.0 collective-permute-done.14.refs_3_
  55.9 0.0 collective-permute-done.13.refs_2_
  55.9 1.7 %shard_map.131 = (f32[3,64,128]{2,1,0:T(8,128)}, f32[64,64]{1,0:T(8,128)}, f32[1024,256]{1,0:T(8,128)}, f32[960,128]{1,0:T(8,128)}) custom-call(f32[64,256]{1,0:T(8,128)S(1)} %get-tuple-element.47._.own, f32[64,256]{1,0:T(8,128)S(1)} %collective-permute-done.10.arrived, ...), custom_call_target="tpu_custom_call", output_to_operand_aliasing={{2}: (7, {}), {3}: (8, {})} | custom-call | flops 950000000 | bytes 2195456 | tf_op jit(solution)/shard_map/pallas_call | solution.py:446
  (2 shorter events, 0.1 us)
Async XLA Ops:
  1.4 1.0 %copy-start = (bf16[16,64,256]{2,1,0:T(8,128)(2,1)S(1)}, bf16[16,64,256]{2,1,0:T(8,128)(2,1)}, u32[]{:S(2)}) copy-start(bf16[16,64,256]{2,1,0:T(8,128)(2,1)} %probe.1) | copy-start | bytes 1572868
  2.5 13.2 %collective-permute-start.1 = (bf16[1072,256]{1,0:T(8,128)(2,1)S(1)}, bf16[1072,256]{1,0:T(8,128)(2,1)S(1)}, u32[]{:S(2)}, u32[]{:S(2)}) collective-permute-start(bf16[1072,256]{1,0:T(8,128)(2,1)S(1)} %shard_map.120.joined), channel_id=1, source_target_pairs={{4,8},{12,16},{20,24},{8,4},{16,12},{24,20},{5,9},{13,17},{21,25},... | collective-permute-start | bytes 1646600 | tf_op jit(solution)/shard_map/ppermute | solution.py:491
  3.2 12.5 %collective-permute-start = (bf16[1072,256]{1,0:T(8,128)(2,1)S(1)}, bf16[1072,256]{1,0:T(8,128)(2,1)S(1)}, u32[]{:S(2)}, u32[]{:S(2)}) collective-permute-start(bf16[1072,256]{1,0:T(8,128)(2,1)S(1)} %shard_map.120.joined), channel_id=1, source_target_pairs={{0,4},{8,12},{16,20},{24,28},{4,0},{12,8},{20,16},{28,24},{1,5},{9... | collective-permute-start | bytes 1646600 | tf_op jit(solution)/shard_map/ppermute | solution.py:491
  7.6 0.7 %copy-start.4 = (s32[16,16]{1,0:T(8,128)S(1)}, s32[16,16]{1,0:T(8,128)}, u32[]{:S(2)}) copy-start(s32[16,16]{1,0:T(8,128)} %nb_ref.5) | copy-start | bytes 3076
  21.3 8.2 %collective-permute-start.2 = (bf16[4,64,256]{2,1,0:T(8,128)(2,1)S(1)}, bf16[4,64,256]{2,1,0:T(8,128)(2,1)S(1)}, u32[]{:S(2)}, u32[]{:S(2)}) collective-permute-start(bf16[4,64,256]{2,1,0:T(8,128)(2,1)S(1)} %get-tuple-element.37), channel_id=1, source_target_pairs={{0,1},{1,0},{2,3},{3,2},{4,5},{5,4},{6,7},{7,6},{8,9},{9,8},{10,11... | collective-permute-start | bytes 393224 | tf_op jit(solution)/shard_map/ppermute | solution.py:495
  22.8 7.8 %collective-permute-start.3 = (bf16[4,64,256]{2,1,0:T(8,128)(2,1)S(1)}, bf16[4,64,256]{2,1,0:T(8,128)(2,1)S(1)}, u32[]{:S(2)}, u32[]{:S(2)}) collective-permute-start(bf16[4,64,256]{2,1,0:T(8,128)(2,1)S(1)} %get-tuple-element.38), channel_id=1, source_target_pairs={{0,2},{1,3},{2,0},{3,1},{4,6},{5,7},{6,4},{7,5},{8,10},{9,11},{10,... | collective-permute-start | bytes 393224 | tf_op jit(solution)/shard_map/ppermute | solution.py:495
  24.4 6.3 %collective-permute-start.4 = (bf16[4,64,256]{2,1,0:T(8,128)(2,1)S(1)}, bf16[4,64,256]{2,1,0:T(8,128)(2,1)S(1)}, u32[]{:S(2)}, u32[]{:S(2)}) collective-permute-start(bf16[4,64,256]{2,1,0:T(8,128)(2,1)S(1)} %get-tuple-element.39), channel_id=1, source_target_pairs={{0,3},{1,2},{2,1},{3,0},{4,7},{5,6},{6,5},{7,4},{8,11},{9,10},{10,... | collective-permute-start | bytes 393224 | tf_op jit(solution)/shard_map/ppermute | solution.py:495
  24.8 4.1 %copy-start.1 = (f32[16,64,64]{2,1,0:T(8,128)S(1)}, f32[16,64,64]{2,1,0:T(8,128)}, u32[]{:S(2)}) copy-start(f32[16,64,64]{2,1,0:T(8,128)} %leaf_inverse.1) | copy-start | bytes 786436
  24.8 4.1 %copy-start.2 = (f32[15,64,64]{2,1,0:T(8,128)S(1)}, f32[15,64,64]{2,1,0:T(8,128)}, u32[]{:S(2)}) copy-start(f32[15,64,64]{2,1,0:T(8,128)} %local_inverse.1) | copy-start | bytes 737284
  24.8 4.1 %copy-start.3 = (f32[7,64,64]{2,1,0:T(8,128)S(1)}, f32[7,64,64]{2,1,0:T(8,128)}, u32[]{:S(2)}) copy-start(f32[7,64,64]{2,1,0:T(8,128)} %upper_inverse.1) | copy-start | bytes 344068
  24.8 4.1 %copy-start.5 = (s32[16,64]{1,0:T(8,128)S(1)}, s32[16,64]{1,0:T(8,128)}, u32[]{:S(2)}) copy-start(s32[16,64]{1,0:T(8,128)} %leaf_pivots.1) | copy-start | bytes 12292
  24.9 4.1 %copy-start.6 = (s32[15,64]{1,0:T(8,128)S(1)}, s32[15,64]{1,0:T(8,128)}, u32[]{:S(2)}) copy-start(s32[15,64]{1,0:T(8,128)} %local_pivots.1) | copy-start | bytes 11524
  24.9 4.1 %copy-start.7 = (s32[7,64]{1,0:T(8,128)S(1)}, s32[7,64]{1,0:T(8,128)}, u32[]{:S(2)}) copy-start(s32[7,64]{1,0:T(8,128)} %upper_pivots.1) | copy-start | bytes 5380
  32.7 5.6 %collective-permute-start.7 = (f32[64,256]{1,0:T(8,128)S(1)}, f32[64,256]{1,0:T(8,128)S(1)}, u32[]{:S(2)}, u32[]{:S(2)}) collective-permute-start(f32[64,256]{1,0:T(8,128)S(1)} %get-tuple-element.42.own), channel_id=1, source_target_pairs={{0,3},{1,2},{2,1},{3,0},{4,7},{5,6},{6,5},{7,4},{8,11},{9,10},{10,... | collective-permute-start | bytes 196616 | tf_op jit(solution)/shard_map/ppermute | solution.py:495
  34.3 5.2 %collective-permute-start.6 = (f32[64,256]{1,0:T(8,128)S(1)}, f32[64,256]{1,0:T(8,128)S(1)}, u32[]{:S(2)}, u32[]{:S(2)}) collective-permute-start(f32[64,256]{1,0:T(8,128)S(1)} %get-tuple-element.42.own), channel_id=1, source_target_pairs={{0,2},{1,3},{2,0},{3,1},{4,6},{5,7},{6,4},{7,5},{8,10},{9,11},{10,... | collective-permute-start | bytes 196616 | tf_op jit(solution)/shard_map/ppermute | solution.py:495
  35.5 5.0 %collective-permute-start.5 = (f32[64,256]{1,0:T(8,128)S(1)}, f32[64,256]{1,0:T(8,128)S(1)}, u32[]{:S(2)}, u32[]{:S(2)}) collective-permute-start(f32[64,256]{1,0:T(8,128)S(1)} %get-tuple-element.42.own), channel_id=1, source_target_pairs={{0,1},{1,0},{2,3},{3,2},{4,5},{5,4},{6,7},{7,6},{8,9},{9,8},{10,11... | collective-permute-start | bytes 196616 | tf_op jit(solution)/shard_map/ppermute | solution.py:495
  36.3 12.0 %collective-permute-start.12 = (f32[352,256]{1,0:T(8,128)S(1)}, f32[352,256]{1,0:T(8,128)S(1)}, u32[]{:S(2)}, u32[]{:S(2)}) collective-permute-start(f32[352,256]{1,0:T(8,128)S(1)} %get-tuple-element.50.refs_0_), channel_id=1, source_target_pairs={{0,2},{1,3},{2,0},{3,1},{4,6},{5,7},{6,4},{7,5},{8,10},{9,11},{10,... | collective-permute-start | bytes 1081352 | tf_op jit(solution)/shard_map/ppermute | solution.py:495
  37.8 10.5 %collective-permute-start.11 = (f32[352,256]{1,0:T(8,128)S(1)}, f32[352,256]{1,0:T(8,128)S(1)}, u32[]{:S(2)}, u32[]{:S(2)}) collective-permute-start(f32[352,256]{1,0:T(8,128)S(1)} %get-tuple-element.50.refs_0_), channel_id=1, source_target_pairs={{0,1},{1,0},{2,3},{3,2},{4,5},{5,4},{6,7},{7,6},{8,9},{9,8},{10,11... | collective-permute-start | bytes 1081352 | tf_op jit(solution)/shard_map/ppermute | solution.py:495
  41.7 1.3 %collective-permute-start.8 = (f32[64,256]{1,0:T(8,128)S(1)}, f32[64,256]{1,0:T(8,128)S(1)}, u32[]{:S(2)}, u32[]{:S(2)}) collective-permute-start(f32[64,256]{1,0:T(8,128)S(1)} %get-tuple-element.44.own), channel_id=1, source_target_pairs={{0,4},{4,0},{8,12},{12,8},{16,20},{20,16},{24,28},{28,24},{1,5},{5... | collective-permute-start | bytes 196616 | tf_op jit(solution)/shard_map/ppermute | solution.py:574
  43.5 4.3 %collective-permute-start.9 = (f32[64,256]{1,0:T(8,128)S(1)}, f32[64,256]{1,0:T(8,128)S(1)}, u32[]{:S(2)}, u32[]{:S(2)}) collective-permute-start(f32[64,256]{1,0:T(8,128)S(1)} %get-tuple-element.46.own), channel_id=1, source_target_pairs={{0,8},{4,12},{8,0},{12,4},{16,24},{20,28},{24,16},{28,20},{1,9},{5... | collective-permute-start | bytes 196616 | tf_op jit(solution)/shard_map/ppermute | solution.py:574
  48.3 7.6 %collective-permute-start.13 = (f32[192,256]{1,0:T(8,128)S(1)}, f32[192,256]{1,0:T(8,128)S(1)}, u32[]{:S(2)}, u32[]{:S(2)}) collective-permute-start(f32[192,256]{1,0:T(8,128)S(1)} %get-tuple-element.51), channel_id=1, source_target_pairs={{0,2},{1,3},{2,0},{3,1},{4,6},{5,7},{6,4},{7,5},{8,10},{9,11},{10,... | collective-permute-start | bytes 589832 | tf_op jit(solution)/shard_map/ppermute | solution.py:495
  49.5 6.4 %collective-permute-start.14 = (f32[160,256]{1,0:T(8,128)S(1)}, f32[160,256]{1,0:T(8,128)S(1)}, u32[]{:S(2)}, u32[]{:S(2)}) collective-permute-start(f32[160,256]{1,0:T(8,128)S(1)} %get-tuple-element.52), channel_id=1, source_target_pairs={{0,1},{1,0},{2,3},{3,2},{4,5},{5,4},{6,7},{7,6},{8,9},{9,8},{10,11... | collective-permute-start | bytes 491528 | tf_op jit(solution)/shard_map/ppermute | solution.py:495
  50.7 5.2 %collective-permute-start.10 = (f32[64,256]{1,0:T(8,128)S(1)}, f32[64,256]{1,0:T(8,128)S(1)}, u32[]{:S(2)}, u32[]{:S(2)}) collective-permute-start(f32[64,256]{1,0:T(8,128)S(1)} %get-tuple-element.47._.own), channel_id=1, source_target_pairs={{0,16},{4,20},{8,24},{12,28},{16,0},{20,4},{24,8},{28,12},{1,17},{... | collective-permute-start | bytes 196616 | tf_op jit(solution)/shard_map/ppermute | solution.py:574

commit v4 on v2

--- a/solution.py
+++ b/solution.py
@@ -114,7 +114,17 @@
         return carry
 
     steps = (filled - 1) // flight
-    lax.fori_loop(0, steps, step, 0)
+    done = jnp.int32(0)
+    for width in (4, 2, 1):
+        rounds = (steps - done) // width
+
+        def several(index, carry, width=width, done=done):
+            for offset in range(width):
+                carry = step(done + index * width + offset, carry)
+            return carry
+
+        lax.fori_loop(0, rounds, several, 0)
+        done = done + rounds * width
     for way in range(flight):
         multiply(codes[steps * flight + way], tiles.at[way])
 

time: 59.4 us -> 57.7 us (0.971)
  Pallas kernels: 26.4 us -> 22.3 us
  starting transfers between devices: 20 us -> 23.1 us
  waiting for transfers between devices: 9.72 us -> 8.65 us
    pallas_call x3, Pallas kernels: 18.9 us -> 14.7 us  [near_call(): pl.pallas_call(body, out_shape=outs, in_specs=[pl.BlockSpec(memory_space=...]
    ppermute x3, starting transfers between devices: 3.56 us -> 6.06 us  [on_device(): lax.ppermute(own_up, 'leaf', [(i, i ^ 1 << tier) for i in range(leaf_tota...]
    ppermute x3, waiting for transfers between devices: 6.75 us -> 4.98 us  [on_device(): lax.ppermute(own_up, 'leaf', [(i, i ^ 1 << tier) for i in range(leaf_tota...]
    ppermute x10, waiting for transfers between devices: 2.96 us -> 3.66 us  [vec_send(): return lax.ppermute(array, 'vec', [(i, i ^ tier) for i in range(parts)])]
    ppermute x10, starting transfers between devices: 11.3 us -> 12 us  [vec_send(): return lax.ppermute(array, 'vec', [(i, i ^ tier) for i in range(parts)])]
  transfers between devices with their start and end apart: 15 -> 15, of which waited for: 7 -> 5; matrix products, arithmetic and copies ran while one was open for 0% -> 0% of each run, Pallas kernels for 29% -> 24%
where the time goes in v4:
time: 57.7 us; the launch traced here: 57.6 us
  starting transfers between devices  23.1 us (40%)
  Pallas kernels  22.3 us (39%)
  waiting for transfers between devices  8.65 us (15%)
  local copies, waits for them, and re-layouts  2.52 us (4%)
  between operations  1 us (2%)
    pallas_call x3, Pallas kernels, near_call(): pl.pallas_call(body, out_shape=outs, in_specs=[pl.BlockSpec(memory_space=...  14.7 us
    ppermute x10, starting transfers between devices, vec_send(): return lax.ppermute(array, 'vec', [(i, i ^ tier) for i in range(parts)])  12 us
    pallas_call x9, Pallas kernels, call(): pl.pallas_call(body, out_shape=outs, in_specs=[fixed] * (len(operands) -...  7.56 us
    ppermute x3, starting transfers between devices, on_device(): lax.ppermute(own_up, 'leaf', [(i, i ^ 1 << tier) for i in range(leaf_tota...  6.06 us
    ppermute x2, starting transfers between devices, on_device(): lax.ppermute(joined, 'leaf', pairs + [(j, i) for i, j in pairs])  5.11 us
    ppermute x3, waiting for transfers between devices, on_device(): lax.ppermute(own_up, 'leaf', [(i, i ^ 1 << tier) for i in range(leaf_tota...  4.98 us
    ppermute x10, waiting for transfers between devices, vec_send(): return lax.ppermute(array, 'vec', [(i, i ^ tier) for i in range(parts)])  3.66 us
    unnamed x17, local copies, waits for them, and re-layouts  2.52 us
  transfers between devices with their start and end apart: 15, of which 5 were waited for; matrix products, arithmetic and copies ran while one was open for 0% of the time, Pallas kernels for 24%

profile of v4, /device:TPU:0, one launch (start us, length us, event | category | flops | bytes accessed | tf_op | source)
XLA Modules:
  0.0 57.6 jit_solution(5126472125638409169)
XLA Ops:
  0.6 0.8 %copy.15.points = bf16[16,3,256]{2,1,0:T(4,128)(2,1)S(1)} copy(bf16[16,3,256]{2,0,1:T(8,128)(2,1)} %param.9) | data formatting | bytes 49152 | tf_op args[0]
  1.4 0.0 copy-start
  1.4 1.0 %copy-done = bf16[16,64,256]{2,1,0:T(8,128)(2,1)S(1)} copy-done((bf16[16,64,256]{2,1,0:T(8,128)(2,1)S(1)}, bf16[16,64,256]{2,1,0:T(8,128)(2,1)}, u32[]{:S(2)}) %copy-start) | copy-done | bytes 524312
  2.5 0.7 %collective-permute-start.1 = (bf16[1072,256]{1,0:T(8,128)(2,1)S(1)}, bf16[1072,256]{1,0:T(8,128)(2,1)S(1)}, u32[]{:S(2)}, u32[]{:S(2)}) collective-permute-start(bf16[1072,256]{1,0:T(8,128)(2,1)S(1)} %shard_map.120.joined), channel_id=1, source_target_pairs={{4,8},{12,16},{20,24},{8,4},{16,12},{24,20},{5,9},{13,17},{21,25},... | collective-permute-start | bytes 1646600 | tf_op jit(solution)/shard_map/ppermute | solution.py:497
  3.2 4.4 %collective-permute-start = (bf16[1072,256]{1,0:T(8,128)(2,1)S(1)}, bf16[1072,256]{1,0:T(8,128)(2,1)S(1)}, u32[]{:S(2)}, u32[]{:S(2)}) collective-permute-start(bf16[1072,256]{1,0:T(8,128)(2,1)S(1)} %shard_map.120.joined), channel_id=1, source_target_pairs={{0,4},{8,12},{16,20},{24,28},{4,0},{12,8},{20,16},{28,24},{1,5},{9... | collective-permute-start | bytes 1646600 | tf_op jit(solution)/shard_map/ppermute | solution.py:497
  7.6 0.0 copy-start.4
  7.6 0.7 %copy-done.4 = s32[16,16]{1,0:T(8,128)S(1)} copy-done((s32[16,16]{1,0:T(8,128)S(1)}, s32[16,16]{1,0:T(8,128)}, u32[]{:S(2)}) %copy-start.4) | copy-done | bytes 1048
  8.3 6.1 %shard_map.121 = (f32[17,64,256]{2,1,0:T(8,128)S(1)}, bf16[16,128,256]{2,1,0:T(8,128)(2,1)S(1)}, bf16[17,256,128]{2,1,0:T(8,128)(2,1)S(1)}) custom-call(s32[16,16]{1,0:T(8,128)S(1)} %copy-done.4, bf16[1072,256]{1,0:T(8,128)(2,1)S(1)} %shard_map.120.joined), custom_call_target="tpu_custom_call" | custom-call | flops 1207959552 | bytes 549888 | tf_op jit(solution)/shard_map/pallas_call | solution.py:211
  14.4 0.0 collective-permute-done.1.outer
  14.4 0.0 collective-permute-done.inner
  14.4 4.9 %shard_map.122 = (bf16[4,64,256]{2,1,0:T(8,128)(2,1)S(1)}, bf16[4,64,256]{2,1,0:T(8,128)(2,1)S(1)}, bf16[4,64,256]{2,1,0:T(8,128)(2,1)S(1)}, bf16[48,128,256]{2,1,0:T(8,128)(2,1)S(1)}, bf16[48,64,256]{2,1,0:T(8,128)(2,1)S(1)}) custom-call(s32[16,16]{1,0:T(8,128)S(1)} %copy-done.4, bf16[1072,256]{1,0:T(8,128)(2,1)S(1)} %shard_map.120.joined, ...), custom_call_target="tpu_custom_call" | custom-call | flops 1207959552 | bytes 4924416 | tf_op jit(solution)/shard_map/pallas_call | solution.py:211
  19.4 1.6 %collective-permute-start.2 = (bf16[4,64,256]{2,1,0:T(8,128)(2,1)S(1)}, bf16[4,64,256]{2,1,0:T(8,128)(2,1)S(1)}, u32[]{:S(2)}, u32[]{:S(2)}) collective-permute-start(bf16[4,64,256]{2,1,0:T(8,128)(2,1)S(1)} %get-tuple-element.37), channel_id=1, source_target_pairs={{0,1},{1,0},{2,3},{3,2},{4,5},{5,4},{6,7},{7,6},{8,9},{9,8},{10,11... | collective-permute-start | bytes 393224 | tf_op jit(solution)/shard_map/ppermute | solution.py:501
  20.9 1.3 %collective-permute-start.3 = (bf16[4,64,256]{2,1,0:T(8,128)(2,1)S(1)}, bf16[4,64,256]{2,1,0:T(8,128)(2,1)S(1)}, u32[]{:S(2)}, u32[]{:S(2)}) collective-permute-start(bf16[4,64,256]{2,1,0:T(8,128)(2,1)S(1)} %get-tuple-element.38), channel_id=1, source_target_pairs={{0,2},{1,3},{2,0},{3,1},{4,6},{5,7},{6,4},{7,5},{8,10},{9,11},{10,... | collective-permute-start | bytes 393224 | tf_op jit(solution)/shard_map/ppermute | solution.py:501
  22.3 0.7 %collective-permute-start.4 = (bf16[4,64,256]{2,1,0:T(8,128)(2,1)S(1)}, bf16[4,64,256]{2,1,0:T(8,128)(2,1)S(1)}, u32[]{:S(2)}, u32[]{:S(2)}) collective-permute-start(bf16[4,64,256]{2,1,0:T(8,128)(2,1)S(1)} %get-tuple-element.39), channel_id=1, source_target_pairs={{0,3},{1,2},{2,1},{3,0},{4,7},{5,6},{6,5},{7,4},{8,11},{9,10},{10,... | collective-permute-start | bytes 393224 | tf_op jit(solution)/shard_map/ppermute | solution.py:501
  22.9 0.0 copy-start.1
  22.9 0.0 copy-start.2
  22.9 0.0 copy-start.3
  22.9 0.0 copy-start.5
  22.9 0.0 copy-start.6
  22.9 0.0 copy-start.7
  23.0 3.7 %shard_map.123._.own = bf16[4,64,256]{2,1,0:T(8,128)(2,1)S(1)} custom-call(s32[16,16]{1,0:T(8,128)S(1)} %copy-done.4, bf16[48,128,256]{2,1,0:T(8,128)(2,1)S(1)} %get-tuple-element.35.far, bf16[48,64,256]{2,1,0:T(8,128)(2,1)S(1)} %get-tuple-element.36.vectors, bf16[17,256,128]{2,1,0:T(8,128)(2,1)S(1)} %get-tuple-element.33.near), custom_call_target="tpu_custom_call" | custom-call | flops 805306368 | bytes 5833728 | tf_op jit(solution)/shard_map/pallas_call | solution.py:211
  26.7 0.0 copy-done.1
  26.7 0.0 copy-done.2
  26.7 0.0 copy-done.3
  26.7 0.0 copy-done.5
  26.7 0.0 copy-done.6
  26.7 0.0 copy-done.7
  26.7 0.5 shard_map.124
  27.2 0.0 collective-permute-done.2.refs_0_
  27.2 2.7 %collective-permute-done.3.refs_1_ = bf16[4,64,256]{2,1,0:T(8,128)(2,1)S(1)} collective-permute-done((bf16[4,64,256]{2,1,0:T(8,128)(2,1)S(1)}, bf16[4,64,256]{2,1,0:T(8,128)(2,1)S(1)}, u32[]{:S(2)}, u32[]{:S(2)}) %collective-permute-start.3) | collective-permute-done | bytes 131104 | tf_op jit(solution)/shard_map/ppermute | solution.py:501
  29.9 0.0 collective-permute-done.4.refs_2_
  29.9 2.0 %shard_map.125 = (f32[352,256]{1,0:T(8,128)S(1)}, f32[64,256]{1,0:T(8,128)S(1)}) custom-call(bf16[4,64,256]{2,1,0:T(8,128)(2,1)S(1)} %shard_map.123._.own, bf16[4,64,256]{2,1,0:T(8,128)(2,1)S(1)} %collective-permute-done.2.refs_0_, bf16[4,64,256]{2,1,0:T(8,128)(2,1)S(1)} %collective-permute-done.3.refs_1_, ...), custom_call_target="tpu_custom_call" | custom-call | bytes 884736 | tf_op jit(solution)/shard_map/pallas_call | solution.py:452
  31.9 1.9 %collective-permute-start.7 = (f32[64,256]{1,0:T(8,128)S(1)}, f32[64,256]{1,0:T(8,128)S(1)}, u32[]{:S(2)}, u32[]{:S(2)}) collective-permute-start(f32[64,256]{1,0:T(8,128)S(1)} %get-tuple-element.42.own), channel_id=1, source_target_pairs={{0,3},{1,2},{2,1},{3,0},{4,7},{5,6},{6,5},{7,4},{8,11},{9,10},{10,... | collective-permute-start | bytes 196616 | tf_op jit(solution)/shard_map/ppermute | solution.py:501
  33.9 0.5 collective-permute-start.6
  34.3 1.2 %collective-permute-start.5 = (f32[64,256]{1,0:T(8,128)S(1)}, f32[64,256]{1,0:T(8,128)S(1)}, u32[]{:S(2)}, u32[]{:S(2)}) collective-permute-start(f32[64,256]{1,0:T(8,128)S(1)} %get-tuple-element.42.own), channel_id=1, source_target_pairs={{0,1},{1,0},{2,3},{3,2},{4,5},{5,4},{6,7},{7,6},{8,9},{9,8},{10,11... | collective-permute-start | bytes 196616 | tf_op jit(solution)/shard_map/ppermute | solution.py:501
  35.5 1.4 %collective-permute-start.12 = (f32[352,256]{1,0:T(8,128)S(1)}, f32[352,256]{1,0:T(8,128)S(1)}, u32[]{:S(2)}, u32[]{:S(2)}) collective-permute-start(f32[352,256]{1,0:T(8,128)S(1)} %get-tuple-element.50.refs_0_), channel_id=1, source_target_pairs={{0,2},{1,3},{2,0},{3,1},{4,6},{5,7},{6,4},{7,5},{8,10},{9,11},{10,... | collective-permute-start | bytes 1081352 | tf_op jit(solution)/shard_map/ppermute | solution.py:501
  36.9 1.0 %collective-permute-start.11 = (f32[352,256]{1,0:T(8,128)S(1)}, f32[352,256]{1,0:T(8,128)S(1)}, u32[]{:S(2)}, u32[]{:S(2)}) collective-permute-start(f32[352,256]{1,0:T(8,128)S(1)} %get-tuple-element.50.refs_0_), channel_id=1, source_target_pairs={{0,1},{1,0},{2,3},{3,2},{4,5},{5,4},{6,7},{7,6},{8,9},{9,8},{10,11... | collective-permute-start | bytes 1081352 | tf_op jit(solution)/shard_map/ppermute | solution.py:501
  37.9 0.0 collective-permute-done.7.refs_2_
  37.9 0.9 %collective-permute-done.6.refs_1_ = f32[64,256]{1,0:T(8,128)S(1)} collective-permute-done((f32[64,256]{1,0:T(8,128)S(1)}, f32[64,256]{1,0:T(8,128)S(1)}, u32[]{:S(2)}, u32[]{:S(2)}) %collective-permute-start.6) | collective-permute-done | bytes 65568 | tf_op jit(solution)/shard_map/ppermute | solution.py:501
  38.9 0.0 collective-permute-done.5.refs_0_
  38.9 1.2 %shard_map.126 = (f32[192,128]{1,0:T(8,128)S(1)}, f32[64,256]{1,0:T(8,128)S(1)}) custom-call(f32[64,256]{1,0:T(8,128)S(1)} %get-tuple-element.42.own, f32[64,256]{1,0:T(8,128)S(1)} %collective-permute-done.5.refs_0_, f32[64,256]{1,0:T(8,128)S(1)} %collective-permute-done.6.refs_1_, f32[64,256]{1,0:T(8,128)S(1)} %collective-permute-done.7.refs_2_, ...), custom_call_target="tpu_custom_call" | custom-call | bytes 360448 | tf_op jit(solution)/shard_map/pallas_call | solution.py:452
  40.1 0.1 collective-permute-start.8
  40.2 1.2 %collective-permute-done.8.arrived = f32[64,256]{1,0:T(8,128)S(1)} collective-permute-done((f32[64,256]{1,0:T(8,128)S(1)}, f32[64,256]{1,0:T(8,128)S(1)}, u32[]{:S(2)}, u32[]{:S(2)}) %collective-permute-start.8) | collective-permute-done | bytes 65568 | tf_op jit(solution)/shard_map/ppermute | solution.py:580
  41.4 0.5 shard_map.127
  41.9 3.3 %collective-permute-start.9 = (f32[64,256]{1,0:T(8,128)S(1)}, f32[64,256]{1,0:T(8,128)S(1)}, u32[]{:S(2)}, u32[]{:S(2)}) collective-permute-start(f32[64,256]{1,0:T(8,128)S(1)} %get-tuple-element.46.own), channel_id=1, source_target_pairs={{0,8},{4,12},{8,0},{12,4},{16,24},{20,28},{24,16},{28,20},{1,9},{5... | collective-permute-start | bytes 196616 | tf_op jit(solution)/shard_map/ppermute | solution.py:580
  45.2 2.4 %collective-permute-done.9.arrived = f32[64,256]{1,0:T(8,128)S(1)} collective-permute-done((f32[64,256]{1,0:T(8,128)S(1)}, f32[64,256]{1,0:T(8,128)S(1)}, u32[]{:S(2)}, u32[]{:S(2)}) %collective-permute-start.9) | collective-permute-done | bytes 65568 | tf_op jit(solution)/shard_map/ppermute | solution.py:580
  47.6 0.5 shard_map.128
  48.1 0.0 collective-permute-done.12.there.refs_2_
  48.1 0.0 collective-permute-done.11.here.refs_1_
  48.1 0.9 %collective-permute-start.13 = (f32[192,256]{1,0:T(8,128)S(1)}, f32[192,256]{1,0:T(8,128)S(1)}, u32[]{:S(2)}, u32[]{:S(2)}) collective-permute-start(f32[192,256]{1,0:T(8,128)S(1)} %get-tuple-element.51), channel_id=1, source_target_pairs={{0,2},{1,3},{2,0},{3,1},{4,6},{5,7},{6,4},{7,5},{8,10},{9,11},{10,... | collective-permute-start | bytes 589832 | tf_op jit(solution)/shard_map/ppermute | solution.py:501
  49.0 1.5 %collective-permute-start.14 = (f32[160,256]{1,0:T(8,128)S(1)}, f32[160,256]{1,0:T(8,128)S(1)}, u32[]{:S(2)}, u32[]{:S(2)}) collective-permute-start(f32[160,256]{1,0:T(8,128)S(1)} %get-tuple-element.52), channel_id=1, source_target_pairs={{0,1},{1,0},{2,3},{3,2},{4,5},{5,4},{6,7},{7,6},{8,9},{9,8},{10,11... | collective-permute-start | bytes 491528 | tf_op jit(solution)/shard_map/ppermute | solution.py:501
  50.6 2.7 %collective-permute-start.10 = (f32[64,256]{1,0:T(8,128)S(1)}, f32[64,256]{1,0:T(8,128)S(1)}, u32[]{:S(2)}, u32[]{:S(2)}) collective-permute-start(f32[64,256]{1,0:T(8,128)S(1)} %get-tuple-element.47._.own), channel_id=1, source_target_pairs={{0,16},{4,20},{8,24},{12,28},{16,0},{20,4},{24,8},{28,12},{1,17},{... | collective-permute-start | bytes 196616 | tf_op jit(solution)/shard_map/ppermute | solution.py:580
  53.3 1.1 %shard_map.130 = (f32[1024,256]{1,0:T(8,128)}, f32[960,128]{1,0:T(8,128)}) custom-call(f32[352,256]{1,0:T(8,128)S(1)} %get-tuple-element.50.refs_0_, f32[352,256]{1,0:T(8,128)S(1)} %collective-permute-done.11.here.refs_1_, f32[352,256]{1,0:T(8,128)S(1)} %collective-permute-done.12.there.refs_2_, f32[192,128]{1,0:T(8,128)S(1)} %get-tuple-element.53.refs_3_), custom_call_target="tpu_custom_call" | custom-call | flops 950000000 | bytes 1179648 | tf_op jit(solution)/shard_map/pallas_call | solution.py:452
  54.4 1.3 %collective-permute-done.10.arrived = f32[64,256]{1,0:T(8,128)S(1)} collective-permute-done((f32[64,256]{1,0:T(8,128)S(1)}, f32[64,256]{1,0:T(8,128)S(1)}, u32[]{:S(2)}, u32[]{:S(2)}) %collective-permute-start.10) | collective-permute-done | bytes 65568 | tf_op jit(solution)/shard_map/ppermute | solution.py:580
  55.7 0.0 collective-permute-done.14.refs_3_
  55.7 0.0 collective-permute-done.13.refs_2_
  55.7 1.7 %shard_map.131 = (f32[3,64,128]{2,1,0:T(8,128)}, f32[64,64]{1,0:T(8,128)}, f32[1024,256]{1,0:T(8,128)}, f32[960,128]{1,0:T(8,128)}) custom-call(f32[64,256]{1,0:T(8,128)S(1)} %get-tuple-element.47._.own, f32[64,256]{1,0:T(8,128)S(1)} %collective-permute-done.10.arrived, ...), custom_call_target="tpu_custom_call", output_to_operand_aliasing={{2}: (7, {}), {3}: (8, {})} | custom-call | flops 950000000 | bytes 2195456 | tf_op jit(solution)/shard_map/pallas_call | solution.py:452
  (2 shorter events, 0.1 us)
Async XLA Ops:
  1.4 1.0 %copy-start = (bf16[16,64,256]{2,1,0:T(8,128)(2,1)S(1)}, bf16[16,64,256]{2,1,0:T(8,128)(2,1)}, u32[]{:S(2)}) copy-start(bf16[16,64,256]{2,1,0:T(8,128)(2,1)} %probe.1) | copy-start | bytes 1572868
  2.5 11.9 %collective-permute-start.1 = (bf16[1072,256]{1,0:T(8,128)(2,1)S(1)}, bf16[1072,256]{1,0:T(8,128)(2,1)S(1)}, u32[]{:S(2)}, u32[]{:S(2)}) collective-permute-start(bf16[1072,256]{1,0:T(8,128)(2,1)S(1)} %shard_map.120.joined), channel_id=1, source_target_pairs={{4,8},{12,16},{20,24},{8,4},{16,12},{24,20},{5,9},{13,17},{21,25},... | collective-permute-start | bytes 1646600 | tf_op jit(solution)/shard_map/ppermute | solution.py:497
  3.2 11.2 %collective-permute-start = (bf16[1072,256]{1,0:T(8,128)(2,1)S(1)}, bf16[1072,256]{1,0:T(8,128)(2,1)S(1)}, u32[]{:S(2)}, u32[]{:S(2)}) collective-permute-start(bf16[1072,256]{1,0:T(8,128)(2,1)S(1)} %shard_map.120.joined), channel_id=1, source_target_pairs={{0,4},{8,12},{16,20},{24,28},{4,0},{12,8},{20,16},{28,24},{1,5},{9... | collective-permute-start | bytes 1646600 | tf_op jit(solution)/shard_map/ppermute | solution.py:497
  7.6 0.7 %copy-start.4 = (s32[16,16]{1,0:T(8,128)S(1)}, s32[16,16]{1,0:T(8,128)}, u32[]{:S(2)}) copy-start(s32[16,16]{1,0:T(8,128)} %nb_ref.5) | copy-start | bytes 3076
  19.4 7.8 %collective-permute-start.2 = (bf16[4,64,256]{2,1,0:T(8,128)(2,1)S(1)}, bf16[4,64,256]{2,1,0:T(8,128)(2,1)S(1)}, u32[]{:S(2)}, u32[]{:S(2)}) collective-permute-start(bf16[4,64,256]{2,1,0:T(8,128)(2,1)S(1)} %get-tuple-element.37), channel_id=1, source_target_pairs={{0,1},{1,0},{2,3},{3,2},{4,5},{5,4},{6,7},{7,6},{8,9},{9,8},{10,11... | collective-permute-start | bytes 393224 | tf_op jit(solution)/shard_map/ppermute | solution.py:501
  20.9 9.0 %collective-permute-start.3 = (bf16[4,64,256]{2,1,0:T(8,128)(2,1)S(1)}, bf16[4,64,256]{2,1,0:T(8,128)(2,1)S(1)}, u32[]{:S(2)}, u32[]{:S(2)}) collective-permute-start(bf16[4,64,256]{2,1,0:T(8,128)(2,1)S(1)} %get-tuple-element.38), channel_id=1, source_target_pairs={{0,2},{1,3},{2,0},{3,1},{4,6},{5,7},{6,4},{7,5},{8,10},{9,11},{10,... | collective-permute-start | bytes 393224 | tf_op jit(solution)/shard_map/ppermute | solution.py:501
  22.3 7.6 %collective-permute-start.4 = (bf16[4,64,256]{2,1,0:T(8,128)(2,1)S(1)}, bf16[4,64,256]{2,1,0:T(8,128)(2,1)S(1)}, u32[]{:S(2)}, u32[]{:S(2)}) collective-permute-start(bf16[4,64,256]{2,1,0:T(8,128)(2,1)S(1)} %get-tuple-element.39), channel_id=1, source_target_pairs={{0,3},{1,2},{2,1},{3,0},{4,7},{5,6},{6,5},{7,4},{8,11},{9,10},{10,... | collective-permute-start | bytes 393224 | tf_op jit(solution)/shard_map/ppermute | solution.py:501
  22.9 3.7 %copy-start.1 = (f32[16,64,64]{2,1,0:T(8,128)S(1)}, f32[16,64,64]{2,1,0:T(8,128)}, u32[]{:S(2)}) copy-start(f32[16,64,64]{2,1,0:T(8,128)} %leaf_inverse.1) | copy-start | bytes 786436
  22.9 3.8 %copy-start.2 = (f32[15,64,64]{2,1,0:T(8,128)S(1)}, f32[15,64,64]{2,1,0:T(8,128)}, u32[]{:S(2)}) copy-start(f32[15,64,64]{2,1,0:T(8,128)} %local_inverse.1) | copy-start | bytes 737284
  22.9 3.8 %copy-start.3 = (f32[7,64,64]{2,1,0:T(8,128)S(1)}, f32[7,64,64]{2,1,0:T(8,128)}, u32[]{:S(2)}) copy-start(f32[7,64,64]{2,1,0:T(8,128)} %upper_inverse.1) | copy-start | bytes 344068
  22.9 3.8 %copy-start.5 = (s32[16,64]{1,0:T(8,128)S(1)}, s32[16,64]{1,0:T(8,128)}, u32[]{:S(2)}) copy-start(s32[16,64]{1,0:T(8,128)} %leaf_pivots.1) | copy-start | bytes 12292
  22.9 3.8 %copy-start.6 = (s32[15,64]{1,0:T(8,128)S(1)}, s32[15,64]{1,0:T(8,128)}, u32[]{:S(2)}) copy-start(s32[15,64]{1,0:T(8,128)} %local_pivots.1) | copy-start | bytes 11524
  22.9 3.8 %copy-start.7 = (s32[7,64]{1,0:T(8,128)S(1)}, s32[7,64]{1,0:T(8,128)}, u32[]{:S(2)}) copy-start(s32[7,64]{1,0:T(8,128)} %upper_pivots.1) | copy-start | bytes 5380
  31.9 6.0 %collective-permute-start.7 = (f32[64,256]{1,0:T(8,128)S(1)}, f32[64,256]{1,0:T(8,128)S(1)}, u32[]{:S(2)}, u32[]{:S(2)}) collective-permute-start(f32[64,256]{1,0:T(8,128)S(1)} %get-tuple-element.42.own), channel_id=1, source_target_pairs={{0,3},{1,2},{2,1},{3,0},{4,7},{5,6},{6,5},{7,4},{8,11},{9,10},{10,... | collective-permute-start | bytes 196616 | tf_op jit(solution)/shard_map/ppermute | solution.py:501
  33.9 5.0 %collective-permute-start.6 = (f32[64,256]{1,0:T(8,128)S(1)}, f32[64,256]{1,0:T(8,128)S(1)}, u32[]{:S(2)}, u32[]{:S(2)}) collective-permute-start(f32[64,256]{1,0:T(8,128)S(1)} %get-tuple-element.42.own), channel_id=1, source_target_pairs={{0,2},{1,3},{2,0},{3,1},{4,6},{5,7},{6,4},{7,5},{8,10},{9,11},{10,... | collective-permute-start | bytes 196616 | tf_op jit(solution)/shard_map/ppermute | solution.py:501
  34.3 4.6 %collective-permute-start.5 = (f32[64,256]{1,0:T(8,128)S(1)}, f32[64,256]{1,0:T(8,128)S(1)}, u32[]{:S(2)}, u32[]{:S(2)}) collective-permute-start(f32[64,256]{1,0:T(8,128)S(1)} %get-tuple-element.42.own), channel_id=1, source_target_pairs={{0,1},{1,0},{2,3},{3,2},{4,5},{5,4},{6,7},{7,6},{8,9},{9,8},{10,11... | collective-permute-start | bytes 196616 | tf_op jit(solution)/shard_map/ppermute | solution.py:501
  35.5 12.6 %collective-permute-start.12 = (f32[352,256]{1,0:T(8,128)S(1)}, f32[352,256]{1,0:T(8,128)S(1)}, u32[]{:S(2)}, u32[]{:S(2)}) collective-permute-start(f32[352,256]{1,0:T(8,128)S(1)} %get-tuple-element.50.refs_0_), channel_id=1, source_target_pairs={{0,2},{1,3},{2,0},{3,1},{4,6},{5,7},{6,4},{7,5},{8,10},{9,11},{10,... | collective-permute-start | bytes 1081352 | tf_op jit(solution)/shard_map/ppermute | solution.py:501
  36.9 11.2 %collective-permute-start.11 = (f32[352,256]{1,0:T(8,128)S(1)}, f32[352,256]{1,0:T(8,128)S(1)}, u32[]{:S(2)}, u32[]{:S(2)}) collective-permute-start(f32[352,256]{1,0:T(8,128)S(1)} %get-tuple-element.50.refs_0_), channel_id=1, source_target_pairs={{0,1},{1,0},{2,3},{3,2},{4,5},{5,4},{6,7},{7,6},{8,9},{9,8},{10,11... | collective-permute-start | bytes 1081352 | tf_op jit(solution)/shard_map/ppermute | solution.py:501
  40.1 1.3 %collective-permute-start.8 = (f32[64,256]{1,0:T(8,128)S(1)}, f32[64,256]{1,0:T(8,128)S(1)}, u32[]{:S(2)}, u32[]{:S(2)}) collective-permute-start(f32[64,256]{1,0:T(8,128)S(1)} %get-tuple-element.44.own), channel_id=1, source_target_pairs={{0,4},{4,0},{8,12},{12,8},{16,20},{20,16},{24,28},{28,24},{1,5},{5... | collective-permute-start | bytes 196616 | tf_op jit(solution)/shard_map/ppermute | solution.py:580
  41.9 5.7 %collective-permute-start.9 = (f32[64,256]{1,0:T(8,128)S(1)}, f32[64,256]{1,0:T(8,128)S(1)}, u32[]{:S(2)}, u32[]{:S(2)}) collective-permute-start(f32[64,256]{1,0:T(8,128)S(1)} %get-tuple-element.46.own), channel_id=1, source_target_pairs={{0,8},{4,12},{8,0},{12,4},{16,24},{20,28},{24,16},{28,20},{1,9},{5... | collective-permute-start | bytes 196616 | tf_op jit(solution)/shard_map/ppermute | solution.py:580
  48.1 7.6 %collective-permute-start.13 = (f32[192,256]{1,0:T(8,128)S(1)}, f32[192,256]{1,0:T(8,128)S(1)}, u32[]{:S(2)}, u32[]{:S(2)}) collective-permute-start(f32[192,256]{1,0:T(8,128)S(1)} %get-tuple-element.51), channel_id=1, source_target_pairs={{0,2},{1,3},{2,0},{3,1},{4,6},{5,7},{6,4},{7,5},{8,10},{9,11},{10,... | collective-permute-start | bytes 589832 | tf_op jit(solution)/shard_map/ppermute | solution.py:501
  49.0 6.7 %collective-permute-start.14 = (f32[160,256]{1,0:T(8,128)S(1)}, f32[160,256]{1,0:T(8,128)S(1)}, u32[]{:S(2)}, u32[]{:S(2)}) collective-permute-start(f32[160,256]{1,0:T(8,128)S(1)} %get-tuple-element.52), channel_id=1, source_target_pairs={{0,1},{1,0},{2,3},{3,2},{4,5},{5,4},{6,7},{7,6},{8,9},{9,8},{10,11... | collective-permute-start | bytes 491528 | tf_op jit(solution)/shard_map/ppermute | solution.py:501
  50.6 5.2 %collective-permute-start.10 = (f32[64,256]{1,0:T(8,128)S(1)}, f32[64,256]{1,0:T(8,128)S(1)}, u32[]{:S(2)}, u32[]{:S(2)}) collective-permute-start(f32[64,256]{1,0:T(8,128)S(1)} %get-tuple-element.47._.own), channel_id=1, source_target_pairs={{0,16},{4,20},{8,24},{12,28},{16,0},{20,4},{24,8},{28,12},{1,17},{... | collective-permute-start | bytes 196616 | tf_op jit(solution)/shard_map/ppermute | solution.py:580

commit v5 on v4

--- a/solution.py
+++ b/solution.py
@@ -11,7 +11,7 @@
 
 SOFTEN = 0.0009
 EPSILON = 1e-06
-FLIGHT = 8
+FLIGHT = 4
 DEPTH = 128
 CHUNK = 256
 ROUND_FLOPS = 950_000_000
@@ -115,7 +115,7 @@
 
     steps = (filled - 1) // flight
     done = jnp.int32(0)
-    for width in (4, 2, 1):
+    for width in (8, 4, 2, 1):
         rounds = (steps - done) // width
 
         def several(index, carry, width=width, done=done):

time: 57.7 us -> 57.2 us (level)
  starting transfers between devices: 23.1 us -> 21.6 us
  Pallas kernels: 22.3 us -> 23.3 us
    ppermute x3, starting transfers between devices: 6.06 us -> 4.58 us  [on_device(): lax.ppermute(own_up, 'leaf', [(i, i ^ 1 << tier) for i in range(leaf_tota...]
    pallas_call x3, Pallas kernels: 14.7 us -> 15.8 us  [near_call(): pl.pallas_call(body, out_shape=outs, in_specs=[pl.BlockSpec(memory_space=...]
  transfers between devices with their start and end apart: 15 -> 15, of which waited for: 5 -> 8; matrix products, arithmetic and copies ran while one was open for 0% -> 0% of each run, Pallas kernels for 24% -> 25%
where the time goes in v5:
time: 57.2 us; the launch traced here: 56.9 us
  Pallas kernels  23.3 us (41%)
  starting transfers between devices  21.6 us (38%)
  waiting for transfers between devices  8.47 us (15%)
  local copies, waits for them, and re-layouts  2.52 us (4%)
  between operations  1.01 us (2%)
    pallas_call x3, Pallas kernels, near_call(): pl.pallas_call(body, out_shape=outs, in_specs=[pl.BlockSpec(memory_space=...  15.8 us
    ppermute x10, starting transfers between devices, vec_send(): return lax.ppermute(array, 'vec', [(i, i ^ tier) for i in range(parts)])  11.9 us
    pallas_call x9, Pallas kernels, call(): pl.pallas_call(body, out_shape=outs, in_specs=[fixed] * (len(operands) -...  7.56 us
    ppermute x2, starting transfers between devices, on_device(): lax.ppermute(joined, 'leaf', pairs + [(j, i) for i, j in pairs])  5.11 us
    ppermute x3, waiting for transfers between devices, on_device(): lax.ppermute(own_up, 'leaf', [(i, i ^ 1 << tier) for i in range(leaf_tota...  5.09 us
    ppermute x3, starting transfers between devices, on_device(): lax.ppermute(own_up, 'leaf', [(i, i ^ 1 << tier) for i in range(leaf_tota...  4.58 us
    ppermute x10, waiting for transfers between devices, vec_send(): return lax.ppermute(array, 'vec', [(i, i ^ tier) for i in range(parts)])  3.38 us
    unnamed x17, local copies, waits for them, and re-layouts  2.52 us
  transfers between devices with their start and end apart: 15, of which 8 were waited for; matrix products, arithmetic and copies ran while one was open for 0% of the time, Pallas kernels for 25%

profile of v5, /device:TPU:0, one launch (start us, length us, event | category | flops | bytes accessed | tf_op | source)
XLA Modules:
  0.0 56.9 jit_solution(16338126339623221012)
XLA Ops:
  0.6 0.8 %copy.15.points = bf16[16,3,256]{2,1,0:T(4,128)(2,1)S(1)} copy(bf16[16,3,256]{2,0,1:T(8,128)(2,1)} %param.9) | data formatting | bytes 49152 | tf_op args[0]
  1.4 0.0 copy-start
  1.4 1.0 %copy-done = bf16[16,64,256]{2,1,0:T(8,128)(2,1)S(1)} copy-done((bf16[16,64,256]{2,1,0:T(8,128)(2,1)S(1)}, bf16[16,64,256]{2,1,0:T(8,128)(2,1)}, u32[]{:S(2)}) %copy-start) | copy-done | bytes 524312
  2.5 0.7 %collective-permute-start.1 = (bf16[1072,256]{1,0:T(8,128)(2,1)S(1)}, bf16[1072,256]{1,0:T(8,128)(2,1)S(1)}, u32[]{:S(2)}, u32[]{:S(2)}) collective-permute-start(bf16[1072,256]{1,0:T(8,128)(2,1)S(1)} %shard_map.120.joined), channel_id=1, source_target_pairs={{4,8},{12,16},{20,24},{8,4},{16,12},{24,20},{5,9},{13,17},{21,25},... | collective-permute-start | bytes 1646600 | tf_op jit(solution)/shard_map/ppermute | solution.py:497
  3.2 4.4 %collective-permute-start = (bf16[1072,256]{1,0:T(8,128)(2,1)S(1)}, bf16[1072,256]{1,0:T(8,128)(2,1)S(1)}, u32[]{:S(2)}, u32[]{:S(2)}) collective-permute-start(bf16[1072,256]{1,0:T(8,128)(2,1)S(1)} %shard_map.120.joined), channel_id=1, source_target_pairs={{0,4},{8,12},{16,20},{24,28},{4,0},{12,8},{20,16},{28,24},{1,5},{9... | collective-permute-start | bytes 1646600 | tf_op jit(solution)/shard_map/ppermute | solution.py:497
  7.6 0.0 copy-start.4
  7.6 0.7 %copy-done.4 = s32[16,16]{1,0:T(8,128)S(1)} copy-done((s32[16,16]{1,0:T(8,128)S(1)}, s32[16,16]{1,0:T(8,128)}, u32[]{:S(2)}) %copy-start.4) | copy-done | bytes 1048
  8.3 6.5 %shard_map.121 = (f32[17,64,256]{2,1,0:T(8,128)S(1)}, bf16[16,128,256]{2,1,0:T(8,128)(2,1)S(1)}, bf16[17,256,128]{2,1,0:T(8,128)(2,1)S(1)}) custom-call(s32[16,16]{1,0:T(8,128)S(1)} %copy-done.4, bf16[1072,256]{1,0:T(8,128)(2,1)S(1)} %shard_map.120.joined), custom_call_target="tpu_custom_call" | custom-call | flops 1207959552 | bytes 549888 | tf_op jit(solution)/shard_map/pallas_call | solution.py:211
  14.8 0.0 collective-permute-done.1.outer
  14.8 0.0 collective-permute-done.inner
  14.8 5.4 %shard_map.122 = (bf16[4,64,256]{2,1,0:T(8,128)(2,1)S(1)}, bf16[4,64,256]{2,1,0:T(8,128)(2,1)S(1)}, bf16[4,64,256]{2,1,0:T(8,128)(2,1)S(1)}, bf16[48,128,256]{2,1,0:T(8,128)(2,1)S(1)}, bf16[48,64,256]{2,1,0:T(8,128)(2,1)S(1)}) custom-call(s32[16,16]{1,0:T(8,128)S(1)} %copy-done.4, bf16[1072,256]{1,0:T(8,128)(2,1)S(1)} %shard_map.120.joined, ...), custom_call_target="tpu_custom_call" | custom-call | flops 1207959552 | bytes 4924416 | tf_op jit(solution)/shard_map/pallas_call | solution.py:211
  20.3 1.2 %collective-permute-start.2 = (bf16[4,64,256]{2,1,0:T(8,128)(2,1)S(1)}, bf16[4,64,256]{2,1,0:T(8,128)(2,1)S(1)}, u32[]{:S(2)}, u32[]{:S(2)}) collective-permute-start(bf16[4,64,256]{2,1,0:T(8,128)(2,1)S(1)} %get-tuple-element.37), channel_id=1, source_target_pairs={{0,1},{1,0},{2,3},{3,2},{4,5},{5,4},{6,7},{7,6},{8,9},{9,8},{10,11... | collective-permute-start | bytes 393224 | tf_op jit(solution)/shard_map/ppermute | solution.py:501
  21.4 2.2 %collective-permute-start.3 = (bf16[4,64,256]{2,1,0:T(8,128)(2,1)S(1)}, bf16[4,64,256]{2,1,0:T(8,128)(2,1)S(1)}, u32[]{:S(2)}, u32[]{:S(2)}) collective-permute-start(bf16[4,64,256]{2,1,0:T(8,128)(2,1)S(1)} %get-tuple-element.38), channel_id=1, source_target_pairs={{0,2},{1,3},{2,0},{3,1},{4,6},{5,7},{6,4},{7,5},{8,10},{9,11},{10,... | collective-permute-start | bytes 393224 | tf_op jit(solution)/shard_map/ppermute | solution.py:501
  23.7 0.1 collective-permute-start.4
  23.8 0.0 copy-start.1
  23.8 0.0 copy-start.2
  23.8 0.0 copy-start.3
  23.8 0.0 copy-start.5
  23.8 0.0 copy-start.6
  23.8 0.0 copy-start.7
  23.8 3.9 %shard_map.123._.own = bf16[4,64,256]{2,1,0:T(8,128)(2,1)S(1)} custom-call(s32[16,16]{1,0:T(8,128)S(1)} %copy-done.4, bf16[48,128,256]{2,1,0:T(8,128)(2,1)S(1)} %get-tuple-element.35.far, bf16[48,64,256]{2,1,0:T(8,128)(2,1)S(1)} %get-tuple-element.36.vectors, bf16[17,256,128]{2,1,0:T(8,128)(2,1)S(1)} %get-tuple-element.33.near), custom_call_target="tpu_custom_call" | custom-call | flops 805306368 | bytes 5833728 | tf_op jit(solution)/shard_map/pallas_call | solution.py:211
  27.7 0.0 copy-done.1
  27.7 0.0 copy-done.2
  27.7 0.0 copy-done.3
  27.8 0.0 copy-done.5
  27.8 0.0 copy-done.6
  27.8 0.0 copy-done.7
  27.8 0.5 shard_map.124
  28.2 0.0 collective-permute-done.2.refs_0_
  28.3 0.6 %collective-permute-done.3.refs_1_ = bf16[4,64,256]{2,1,0:T(8,128)(2,1)S(1)} collective-permute-done((bf16[4,64,256]{2,1,0:T(8,128)(2,1)S(1)}, bf16[4,64,256]{2,1,0:T(8,128)(2,1)S(1)}, u32[]{:S(2)}, u32[]{:S(2)}) %collective-permute-start.3) | collective-permute-done | bytes 131104 | tf_op jit(solution)/shard_map/ppermute | solution.py:501
  28.8 0.7 %collective-permute-done.4.refs_2_ = bf16[4,64,256]{2,1,0:T(8,128)(2,1)S(1)} collective-permute-done((bf16[4,64,256]{2,1,0:T(8,128)(2,1)S(1)}, bf16[4,64,256]{2,1,0:T(8,128)(2,1)S(1)}, u32[]{:S(2)}, u32[]{:S(2)}) %collective-permute-start.4) | collective-permute-done | bytes 131104 | tf_op jit(solution)/shard_map/ppermute | solution.py:501
  29.6 2.0 %shard_map.125 = (f32[352,256]{1,0:T(8,128)S(1)}, f32[64,256]{1,0:T(8,128)S(1)}) custom-call(bf16[4,64,256]{2,1,0:T(8,128)(2,1)S(1)} %shard_map.123._.own, bf16[4,64,256]{2,1,0:T(8,128)(2,1)S(1)} %collective-permute-done.2.refs_0_, bf16[4,64,256]{2,1,0:T(8,128)(2,1)S(1)} %collective-permute-done.3.refs_1_, ...), custom_call_target="tpu_custom_call" | custom-call | bytes 884736 | tf_op jit(solution)/shard_map/pallas_call | solution.py:452
  31.6 1.7 %collective-permute-start.7 = (f32[64,256]{1,0:T(8,128)S(1)}, f32[64,256]{1,0:T(8,128)S(1)}, u32[]{:S(2)}, u32[]{:S(2)}) collective-permute-start(f32[64,256]{1,0:T(8,128)S(1)} %get-tuple-element.42.own), channel_id=1, source_target_pairs={{0,3},{1,2},{2,1},{3,0},{4,7},{5,6},{6,5},{7,4},{8,11},{9,10},{10,... | collective-permute-start | bytes 196616 | tf_op jit(solution)/shard_map/ppermute | solution.py:501
  33.3 1.1 %collective-permute-start.6 = (f32[64,256]{1,0:T(8,128)S(1)}, f32[64,256]{1,0:T(8,128)S(1)}, u32[]{:S(2)}, u32[]{:S(2)}) collective-permute-start(f32[64,256]{1,0:T(8,128)S(1)} %get-tuple-element.42.own), channel_id=1, source_target_pairs={{0,2},{1,3},{2,0},{3,1},{4,6},{5,7},{6,4},{7,5},{8,10},{9,11},{10,... | collective-permute-start | bytes 196616 | tf_op jit(solution)/shard_map/ppermute | solution.py:501
  34.5 0.7 %collective-permute-start.5 = (f32[64,256]{1,0:T(8,128)S(1)}, f32[64,256]{1,0:T(8,128)S(1)}, u32[]{:S(2)}, u32[]{:S(2)}) collective-permute-start(f32[64,256]{1,0:T(8,128)S(1)} %get-tuple-element.42.own), channel_id=1, source_target_pairs={{0,1},{1,0},{2,3},{3,2},{4,5},{5,4},{6,7},{7,6},{8,9},{9,8},{10,11... | collective-permute-start | bytes 196616 | tf_op jit(solution)/shard_map/ppermute | solution.py:501
  35.2 1.8 %collective-permute-start.12 = (f32[352,256]{1,0:T(8,128)S(1)}, f32[352,256]{1,0:T(8,128)S(1)}, u32[]{:S(2)}, u32[]{:S(2)}) collective-permute-start(f32[352,256]{1,0:T(8,128)S(1)} %get-tuple-element.50.refs_0_), channel_id=1, source_target_pairs={{0,2},{1,3},{2,0},{3,1},{4,6},{5,7},{6,4},{7,5},{8,10},{9,11},{10,... | collective-permute-start | bytes 1081352 | tf_op jit(solution)/shard_map/ppermute | solution.py:501
  36.9 0.5 collective-permute-start.11
  37.4 0.1 collective-permute-done.7.refs_2_
  37.5 1.2 %collective-permute-done.6.refs_1_ = f32[64,256]{1,0:T(8,128)S(1)} collective-permute-done((f32[64,256]{1,0:T(8,128)S(1)}, f32[64,256]{1,0:T(8,128)S(1)}, u32[]{:S(2)}, u32[]{:S(2)}) %collective-permute-start.6) | collective-permute-done | bytes 65568 | tf_op jit(solution)/shard_map/ppermute | solution.py:501
  38.6 0.8 %collective-permute-done.5.refs_0_ = f32[64,256]{1,0:T(8,128)S(1)} collective-permute-done((f32[64,256]{1,0:T(8,128)S(1)}, f32[64,256]{1,0:T(8,128)S(1)}, u32[]{:S(2)}, u32[]{:S(2)}) %collective-permute-start.5) | collective-permute-done | bytes 65568 | tf_op jit(solution)/shard_map/ppermute | solution.py:501
  39.5 1.2 %shard_map.126 = (f32[192,128]{1,0:T(8,128)S(1)}, f32[64,256]{1,0:T(8,128)S(1)}) custom-call(f32[64,256]{1,0:T(8,128)S(1)} %get-tuple-element.42.own, f32[64,256]{1,0:T(8,128)S(1)} %collective-permute-done.5.refs_0_, f32[64,256]{1,0:T(8,128)S(1)} %collective-permute-done.6.refs_1_, f32[64,256]{1,0:T(8,128)S(1)} %collective-permute-done.7.refs_2_, ...), custom_call_target="tpu_custom_call" | custom-call | bytes 360448 | tf_op jit(solution)/shard_map/pallas_call | solution.py:452
  40.7 0.1 collective-permute-start.8
  40.8 1.2 %collective-permute-done.8.arrived = f32[64,256]{1,0:T(8,128)S(1)} collective-permute-done((f32[64,256]{1,0:T(8,128)S(1)}, f32[64,256]{1,0:T(8,128)S(1)}, u32[]{:S(2)}, u32[]{:S(2)}) %collective-permute-start.8) | collective-permute-done | bytes 65568 | tf_op jit(solution)/shard_map/ppermute | solution.py:580
  42.0 0.5 shard_map.127
  42.5 1.8 %collective-permute-start.9 = (f32[64,256]{1,0:T(8,128)S(1)}, f32[64,256]{1,0:T(8,128)S(1)}, u32[]{:S(2)}, u32[]{:S(2)}) collective-permute-start(f32[64,256]{1,0:T(8,128)S(1)} %get-tuple-element.46.own), channel_id=1, source_target_pairs={{0,8},{4,12},{8,0},{12,4},{16,24},{20,28},{24,16},{28,20},{1,9},{5... | collective-permute-start | bytes 196616 | tf_op jit(solution)/shard_map/ppermute | solution.py:580
  44.3 2.5 %collective-permute-done.9.arrived = f32[64,256]{1,0:T(8,128)S(1)} collective-permute-done((f32[64,256]{1,0:T(8,128)S(1)}, f32[64,256]{1,0:T(8,128)S(1)}, u32[]{:S(2)}, u32[]{:S(2)}) %collective-permute-start.9) | collective-permute-done | bytes 65568 | tf_op jit(solution)/shard_map/ppermute | solution.py:580
  46.8 0.5 shard_map.128
  47.3 0.0 collective-permute-done.12.there.refs_2_
  47.3 0.0 collective-permute-done.11.here.refs_1_
  47.3 1.6 %collective-permute-start.13 = (f32[192,256]{1,0:T(8,128)S(1)}, f32[192,256]{1,0:T(8,128)S(1)}, u32[]{:S(2)}, u32[]{:S(2)}) collective-permute-start(f32[192,256]{1,0:T(8,128)S(1)} %get-tuple-element.51), channel_id=1, source_target_pairs={{0,2},{1,3},{2,0},{3,1},{4,6},{5,7},{6,4},{7,5},{8,10},{9,11},{10,... | collective-permute-start | bytes 589832 | tf_op jit(solution)/shard_map/ppermute | solution.py:501
  48.9 1.0 %collective-permute-start.14 = (f32[160,256]{1,0:T(8,128)S(1)}, f32[160,256]{1,0:T(8,128)S(1)}, u32[]{:S(2)}, u32[]{:S(2)}) collective-permute-start(f32[160,256]{1,0:T(8,128)S(1)} %get-tuple-element.52), channel_id=1, source_target_pairs={{0,1},{1,0},{2,3},{3,2},{4,5},{5,4},{6,7},{7,6},{8,9},{9,8},{10,11... | collective-permute-start | bytes 491528 | tf_op jit(solution)/shard_map/ppermute | solution.py:501
  49.9 2.7 %collective-permute-start.10 = (f32[64,256]{1,0:T(8,128)S(1)}, f32[64,256]{1,0:T(8,128)S(1)}, u32[]{:S(2)}, u32[]{:S(2)}) collective-permute-start(f32[64,256]{1,0:T(8,128)S(1)} %get-tuple-element.47._.own), channel_id=1, source_target_pairs={{0,16},{4,20},{8,24},{12,28},{16,0},{20,4},{24,8},{28,12},{1,17},{... | collective-permute-start | bytes 196616 | tf_op jit(solution)/shard_map/ppermute | solution.py:580
  52.6 1.1 %shard_map.130 = (f32[1024,256]{1,0:T(8,128)}, f32[960,128]{1,0:T(8,128)}) custom-call(f32[352,256]{1,0:T(8,128)S(1)} %get-tuple-element.50.refs_0_, f32[352,256]{1,0:T(8,128)S(1)} %collective-permute-done.11.here.refs_1_, f32[352,256]{1,0:T(8,128)S(1)} %collective-permute-done.12.there.refs_2_, f32[192,128]{1,0:T(8,128)S(1)} %get-tuple-element.53.refs_3_), custom_call_target="tpu_custom_call" | custom-call | flops 950000000 | bytes 1179648 | tf_op jit(solution)/shard_map/pallas_call | solution.py:452
  53.7 1.4 %collective-permute-done.10.arrived = f32[64,256]{1,0:T(8,128)S(1)} collective-permute-done((f32[64,256]{1,0:T(8,128)S(1)}, f32[64,256]{1,0:T(8,128)S(1)}, u32[]{:S(2)}, u32[]{:S(2)}) %collective-permute-start.10) | collective-permute-done | bytes 65568 | tf_op jit(solution)/shard_map/ppermute | solution.py:580
  55.1 0.0 collective-permute-done.14.refs_3_
  55.1 0.0 collective-permute-done.13.refs_2_
  55.1 1.7 %shard_map.131 = (f32[3,64,128]{2,1,0:T(8,128)}, f32[64,64]{1,0:T(8,128)}, f32[1024,256]{1,0:T(8,128)}, f32[960,128]{1,0:T(8,128)}) custom-call(f32[64,256]{1,0:T(8,128)S(1)} %get-tuple-element.47._.own, f32[64,256]{1,0:T(8,128)S(1)} %collective-permute-done.10.arrived, ...), custom_call_target="tpu_custom_call", output_to_operand_aliasing={{2}: (7, {}), {3}: (8, {})} | custom-call | flops 950000000 | bytes 2195456 | tf_op jit(solution)/shard_map/pallas_call | solution.py:452
  (2 shorter events, 0.1 us)
Async XLA Ops:
  1.4 1.0 %copy-start = (bf16[16,64,256]{2,1,0:T(8,128)(2,1)S(1)}, bf16[16,64,256]{2,1,0:T(8,128)(2,1)}, u32[]{:S(2)}) copy-start(bf16[16,64,256]{2,1,0:T(8,128)(2,1)} %probe.1) | copy-start | bytes 1572868
  2.5 12.3 %collective-permute-start.1 = (bf16[1072,256]{1,0:T(8,128)(2,1)S(1)}, bf16[1072,256]{1,0:T(8,128)(2,1)S(1)}, u32[]{:S(2)}, u32[]{:S(2)}) collective-permute-start(bf16[1072,256]{1,0:T(8,128)(2,1)S(1)} %shard_map.120.joined), channel_id=1, source_target_pairs={{4,8},{12,16},{20,24},{8,4},{16,12},{24,20},{5,9},{13,17},{21,25},... | collective-permute-start | bytes 1646600 | tf_op jit(solution)/shard_map/ppermute | solution.py:497
  3.2 11.6 %collective-permute-start = (bf16[1072,256]{1,0:T(8,128)(2,1)S(1)}, bf16[1072,256]{1,0:T(8,128)(2,1)S(1)}, u32[]{:S(2)}, u32[]{:S(2)}) collective-permute-start(bf16[1072,256]{1,0:T(8,128)(2,1)S(1)} %shard_map.120.joined), channel_id=1, source_target_pairs={{0,4},{8,12},{16,20},{24,28},{4,0},{12,8},{20,16},{28,24},{1,5},{9... | collective-permute-start | bytes 1646600 | tf_op jit(solution)/shard_map/ppermute | solution.py:497
  7.6 0.7 %copy-start.4 = (s32[16,16]{1,0:T(8,128)S(1)}, s32[16,16]{1,0:T(8,128)}, u32[]{:S(2)}) copy-start(s32[16,16]{1,0:T(8,128)} %nb_ref.5) | copy-start | bytes 3076
  20.3 8.0 %collective-permute-start.2 = (bf16[4,64,256]{2,1,0:T(8,128)(2,1)S(1)}, bf16[4,64,256]{2,1,0:T(8,128)(2,1)S(1)}, u32[]{:S(2)}, u32[]{:S(2)}) collective-permute-start(bf16[4,64,256]{2,1,0:T(8,128)(2,1)S(1)} %get-tuple-element.37), channel_id=1, source_target_pairs={{0,1},{1,0},{2,3},{3,2},{4,5},{5,4},{6,7},{7,6},{8,9},{9,8},{10,11... | collective-permute-start | bytes 393224 | tf_op jit(solution)/shard_map/ppermute | solution.py:501
  21.4 7.4 %collective-permute-start.3 = (bf16[4,64,256]{2,1,0:T(8,128)(2,1)S(1)}, bf16[4,64,256]{2,1,0:T(8,128)(2,1)S(1)}, u32[]{:S(2)}, u32[]{:S(2)}) collective-permute-start(bf16[4,64,256]{2,1,0:T(8,128)(2,1)S(1)} %get-tuple-element.38), channel_id=1, source_target_pairs={{0,2},{1,3},{2,0},{3,1},{4,6},{5,7},{6,4},{7,5},{8,10},{9,11},{10,... | collective-permute-start | bytes 393224 | tf_op jit(solution)/shard_map/ppermute | solution.py:501
  23.7 5.9 %collective-permute-start.4 = (bf16[4,64,256]{2,1,0:T(8,128)(2,1)S(1)}, bf16[4,64,256]{2,1,0:T(8,128)(2,1)S(1)}, u32[]{:S(2)}, u32[]{:S(2)}) collective-permute-start(bf16[4,64,256]{2,1,0:T(8,128)(2,1)S(1)} %get-tuple-element.39), channel_id=1, source_target_pairs={{0,3},{1,2},{2,1},{3,0},{4,7},{5,6},{6,5},{7,4},{8,11},{9,10},{10,... | collective-permute-start | bytes 393224 | tf_op jit(solution)/shard_map/ppermute | solution.py:501
  23.8 3.9 %copy-start.1 = (f32[16,64,64]{2,1,0:T(8,128)S(1)}, f32[16,64,64]{2,1,0:T(8,128)}, u32[]{:S(2)}) copy-start(f32[16,64,64]{2,1,0:T(8,128)} %leaf_inverse.1) | copy-start | bytes 786436
  23.8 3.9 %copy-start.2 = (f32[15,64,64]{2,1,0:T(8,128)S(1)}, f32[15,64,64]{2,1,0:T(8,128)}, u32[]{:S(2)}) copy-start(f32[15,64,64]{2,1,0:T(8,128)} %local_inverse.1) | copy-start | bytes 737284
  23.8 3.9 %copy-start.3 = (f32[7,64,64]{2,1,0:T(8,128)S(1)}, f32[7,64,64]{2,1,0:T(8,128)}, u32[]{:S(2)}) copy-start(f32[7,64,64]{2,1,0:T(8,128)} %upper_inverse.1) | copy-start | bytes 344068
  23.8 3.9 %copy-start.5 = (s32[16,64]{1,0:T(8,128)S(1)}, s32[16,64]{1,0:T(8,128)}, u32[]{:S(2)}) copy-start(s32[16,64]{1,0:T(8,128)} %leaf_pivots.1) | copy-start | bytes 12292
  23.8 3.9 %copy-start.6 = (s32[15,64]{1,0:T(8,128)S(1)}, s32[15,64]{1,0:T(8,128)}, u32[]{:S(2)}) copy-start(s32[15,64]{1,0:T(8,128)} %local_pivots.1) | copy-start | bytes 11524
  23.8 3.9 %copy-start.7 = (s32[7,64]{1,0:T(8,128)S(1)}, s32[7,64]{1,0:T(8,128)}, u32[]{:S(2)}) copy-start(s32[7,64]{1,0:T(8,128)} %upper_pivots.1) | copy-start | bytes 5380
  31.6 5.8 %collective-permute-start.7 = (f32[64,256]{1,0:T(8,128)S(1)}, f32[64,256]{1,0:T(8,128)S(1)}, u32[]{:S(2)}, u32[]{:S(2)}) collective-permute-start(f32[64,256]{1,0:T(8,128)S(1)} %get-tuple-element.42.own), channel_id=1, source_target_pairs={{0,3},{1,2},{2,1},{3,0},{4,7},{5,6},{6,5},{7,4},{8,11},{9,10},{10,... | collective-permute-start | bytes 196616 | tf_op jit(solution)/shard_map/ppermute | solution.py:501
  33.3 5.3 %collective-permute-start.6 = (f32[64,256]{1,0:T(8,128)S(1)}, f32[64,256]{1,0:T(8,128)S(1)}, u32[]{:S(2)}, u32[]{:S(2)}) collective-permute-start(f32[64,256]{1,0:T(8,128)S(1)} %get-tuple-element.42.own), channel_id=1, source_target_pairs={{0,2},{1,3},{2,0},{3,1},{4,6},{5,7},{6,4},{7,5},{8,10},{9,11},{10,... | collective-permute-start | bytes 196616 | tf_op jit(solution)/shard_map/ppermute | solution.py:501
  34.5 5.0 %collective-permute-start.5 = (f32[64,256]{1,0:T(8,128)S(1)}, f32[64,256]{1,0:T(8,128)S(1)}, u32[]{:S(2)}, u32[]{:S(2)}) collective-permute-start(f32[64,256]{1,0:T(8,128)S(1)} %get-tuple-element.42.own), channel_id=1, source_target_pairs={{0,1},{1,0},{2,3},{3,2},{4,5},{5,4},{6,7},{7,6},{8,9},{9,8},{10,11... | collective-permute-start | bytes 196616 | tf_op jit(solution)/shard_map/ppermute | solution.py:501
  35.2 12.1 %collective-permute-start.12 = (f32[352,256]{1,0:T(8,128)S(1)}, f32[352,256]{1,0:T(8,128)S(1)}, u32[]{:S(2)}, u32[]{:S(2)}) collective-permute-start(f32[352,256]{1,0:T(8,128)S(1)} %get-tuple-element.50.refs_0_), channel_id=1, source_target_pairs={{0,2},{1,3},{2,0},{3,1},{4,6},{5,7},{6,4},{7,5},{8,10},{9,11},{10,... | collective-permute-start | bytes 1081352 | tf_op jit(solution)/shard_map/ppermute | solution.py:501
  36.9 10.4 %collective-permute-start.11 = (f32[352,256]{1,0:T(8,128)S(1)}, f32[352,256]{1,0:T(8,128)S(1)}, u32[]{:S(2)}, u32[]{:S(2)}) collective-permute-start(f32[352,256]{1,0:T(8,128)S(1)} %get-tuple-element.50.refs_0_), channel_id=1, source_target_pairs={{0,1},{1,0},{2,3},{3,2},{4,5},{5,4},{6,7},{7,6},{8,9},{9,8},{10,11... | collective-permute-start | bytes 1081352 | tf_op jit(solution)/shard_map/ppermute | solution.py:501
  40.7 1.3 %collective-permute-start.8 = (f32[64,256]{1,0:T(8,128)S(1)}, f32[64,256]{1,0:T(8,128)S(1)}, u32[]{:S(2)}, u32[]{:S(2)}) collective-permute-start(f32[64,256]{1,0:T(8,128)S(1)} %get-tuple-element.44.own), channel_id=1, source_target_pairs={{0,4},{4,0},{8,12},{12,8},{16,20},{20,16},{24,28},{28,24},{1,5},{5... | collective-permute-start | bytes 196616 | tf_op jit(solution)/shard_map/ppermute | solution.py:580
  42.5 4.3 %collective-permute-start.9 = (f32[64,256]{1,0:T(8,128)S(1)}, f32[64,256]{1,0:T(8,128)S(1)}, u32[]{:S(2)}, u32[]{:S(2)}) collective-permute-start(f32[64,256]{1,0:T(8,128)S(1)} %get-tuple-element.46.own), channel_id=1, source_target_pairs={{0,8},{4,12},{8,0},{12,4},{16,24},{20,28},{24,16},{28,20},{1,9},{5... | collective-permute-start | bytes 196616 | tf_op jit(solution)/shard_map/ppermute | solution.py:580
  47.3 7.7 %collective-permute-start.13 = (f32[192,256]{1,0:T(8,128)S(1)}, f32[192,256]{1,0:T(8,128)S(1)}, u32[]{:S(2)}, u32[]{:S(2)}) collective-permute-start(f32[192,256]{1,0:T(8,128)S(1)} %get-tuple-element.51), channel_id=1, source_target_pairs={{0,2},{1,3},{2,0},{3,1},{4,6},{5,7},{6,4},{7,5},{8,10},{9,11},{10,... | collective-permute-start | bytes 589832 | tf_op jit(solution)/shard_map/ppermute | solution.py:501
  48.9 6.2 %collective-permute-start.14 = (f32[160,256]{1,0:T(8,128)S(1)}, f32[160,256]{1,0:T(8,128)S(1)}, u32[]{:S(2)}, u32[]{:S(2)}) collective-permute-start(f32[160,256]{1,0:T(8,128)S(1)} %get-tuple-element.52), channel_id=1, source_target_pairs={{0,1},{1,0},{2,3},{3,2},{4,5},{5,4},{6,7},{7,6},{8,9},{9,8},{10,11... | collective-permute-start | bytes 491528 | tf_op jit(solution)/shard_map/ppermute | solution.py:501
  49.9 5.2 %collective-permute-start.10 = (f32[64,256]{1,0:T(8,128)S(1)}, f32[64,256]{1,0:T(8,128)S(1)}, u32[]{:S(2)}, u32[]{:S(2)}) collective-permute-start(f32[64,256]{1,0:T(8,128)S(1)} %get-tuple-element.47._.own), channel_id=1, source_target_pairs={{0,16},{4,20},{8,24},{12,28},{16,0},{20,4},{24,8},{28,12},{1,17},{... | collective-permute-start | bytes 196616 | tf_op jit(solution)/shard_map/ppermute | solution.py:580

commit v6 on v5

--- a/solution.py
+++ b/solution.py
@@ -94,7 +94,6 @@
                 filled += wanted(listed, first, count).astype(jnp.int32)
     for way in range(flight):
         codes[filled + way] = idle
-    tiles[...] = jnp.zeros(tiles.shape, tiles.dtype)
 
     def multiply(code, tile):
         row = code // 64

time: 57.2 us -> 57.2 us (level)
  starting transfers between devices: 21.6 us -> 22.6 us
  transfers between devices with their start and end apart: 15 -> 15, of which waited for: 8 -> 7; matrix products, arithmetic and copies ran while one was open for 0% -> 0% of each run, Pallas kernels for 25% -> 24%
where the time goes in v6:
time: 57.2 us; the launch traced here: 57.3 us
  Pallas kernels  22.8 us (40%)
  starting transfers between devices  22.6 us (40%)
  waiting for transfers between devices  8.33 us (15%)
  local copies, waits for them, and re-layouts  2.52 us (4%)
  between operations  1.01 us (2%)
    pallas_call x3, Pallas kernels, near_call(): pl.pallas_call(body, out_shape=outs, in_specs=[pl.BlockSpec(memory_space=...  15.2 us
    ppermute x10, starting transfers between devices, vec_send(): return lax.ppermute(array, 'vec', [(i, i ^ tier) for i in range(parts)])  12.4 us
    pallas_call x9, Pallas kernels, call(): pl.pallas_call(body, out_shape=outs, in_specs=[fixed] * (len(operands) -...  7.57 us
    ppermute x2, starting transfers between devices, on_device(): lax.ppermute(joined, 'leaf', pairs + [(j, i) for i, j in pairs])  5.11 us
    ppermute x3, starting transfers between devices, on_device(): lax.ppermute(own_up, 'leaf', [(i, i ^ 1 << tier) for i in range(leaf_tota...  5.07 us
    ppermute x3, waiting for transfers between devices, on_device(): lax.ppermute(own_up, 'leaf', [(i, i ^ 1 << tier) for i in range(leaf_tota...  4.8 us
    ppermute x10, waiting for transfers between devices, vec_send(): return lax.ppermute(array, 'vec', [(i, i ^ tier) for i in range(parts)])  3.52 us
    unnamed x17, local copies, waits for them, and re-layouts  2.52 us
  transfers between devices with their start and end apart: 15, of which 7 were waited for; matrix products, arithmetic and copies ran while one was open for 0% of the time, Pallas kernels for 24%

profile of v6, /device:TPU:0, one launch (start us, length us, event | category | flops | bytes accessed | tf_op | source)
XLA Modules:
  0.0 57.3 jit_solution(16857677953610064759)
XLA Ops:
  0.6 0.8 %copy.15.points = bf16[16,3,256]{2,1,0:T(4,128)(2,1)S(1)} copy(bf16[16,3,256]{2,0,1:T(8,128)(2,1)} %param.9) | data formatting | bytes 49152 | tf_op args[0]
  1.4 0.0 copy-start
  1.4 1.0 %copy-done = bf16[16,64,256]{2,1,0:T(8,128)(2,1)S(1)} copy-done((bf16[16,64,256]{2,1,0:T(8,128)(2,1)S(1)}, bf16[16,64,256]{2,1,0:T(8,128)(2,1)}, u32[]{:S(2)}) %copy-start) | copy-done | bytes 524312
  2.5 0.7 %collective-permute-start.1 = (bf16[1072,256]{1,0:T(8,128)(2,1)S(1)}, bf16[1072,256]{1,0:T(8,128)(2,1)S(1)}, u32[]{:S(2)}, u32[]{:S(2)}) collective-permute-start(bf16[1072,256]{1,0:T(8,128)(2,1)S(1)} %shard_map.120.joined), channel_id=1, source_target_pairs={{4,8},{12,16},{20,24},{8,4},{16,12},{24,20},{5,9},{13,17},{21,25},... | collective-permute-start | bytes 1646600 | tf_op jit(solution)/shard_map/ppermute | solution.py:496
  3.2 4.4 %collective-permute-start = (bf16[1072,256]{1,0:T(8,128)(2,1)S(1)}, bf16[1072,256]{1,0:T(8,128)(2,1)S(1)}, u32[]{:S(2)}, u32[]{:S(2)}) collective-permute-start(bf16[1072,256]{1,0:T(8,128)(2,1)S(1)} %shard_map.120.joined), channel_id=1, source_target_pairs={{0,4},{8,12},{16,20},{24,28},{4,0},{12,8},{20,16},{28,24},{1,5},{9... | collective-permute-start | bytes 1646600 | tf_op jit(solution)/shard_map/ppermute | solution.py:496
  7.6 0.0 copy-start.4
  7.6 0.7 %copy-done.4 = s32[16,16]{1,0:T(8,128)S(1)} copy-done((s32[16,16]{1,0:T(8,128)S(1)}, s32[16,16]{1,0:T(8,128)}, u32[]{:S(2)}) %copy-start.4) | copy-done | bytes 1048
  8.3 6.0 %shard_map.121 = (f32[17,64,256]{2,1,0:T(8,128)S(1)}, bf16[16,128,256]{2,1,0:T(8,128)(2,1)S(1)}, bf16[17,256,128]{2,1,0:T(8,128)(2,1)S(1)}) custom-call(s32[16,16]{1,0:T(8,128)S(1)} %copy-done.4, bf16[1072,256]{1,0:T(8,128)(2,1)S(1)} %shard_map.120.joined), custom_call_target="tpu_custom_call" | custom-call | flops 1207959552 | bytes 549888 | tf_op jit(solution)/shard_map/pallas_call | solution.py:210
  14.3 0.0 collective-permute-done.1.outer
  14.3 0.0 collective-permute-done.inner
  14.3 5.0 %shard_map.122 = (bf16[4,64,256]{2,1,0:T(8,128)(2,1)S(1)}, bf16[4,64,256]{2,1,0:T(8,128)(2,1)S(1)}, bf16[4,64,256]{2,1,0:T(8,128)(2,1)S(1)}, bf16[48,128,256]{2,1,0:T(8,128)(2,1)S(1)}, bf16[48,64,256]{2,1,0:T(8,128)(2,1)S(1)}) custom-call(s32[16,16]{1,0:T(8,128)S(1)} %copy-done.4, bf16[1072,256]{1,0:T(8,128)(2,1)S(1)} %shard_map.120.joined, ...), custom_call_target="tpu_custom_call" | custom-call | flops 1207959552 | bytes 4924416 | tf_op jit(solution)/shard_map/pallas_call | solution.py:210
  19.3 2.1 %collective-permute-start.2 = (bf16[4,64,256]{2,1,0:T(8,128)(2,1)S(1)}, bf16[4,64,256]{2,1,0:T(8,128)(2,1)S(1)}, u32[]{:S(2)}, u32[]{:S(2)}) collective-permute-start(bf16[4,64,256]{2,1,0:T(8,128)(2,1)S(1)} %get-tuple-element.37), channel_id=1, source_target_pairs={{0,1},{1,0},{2,3},{3,2},{4,5},{5,4},{6,7},{7,6},{8,9},{9,8},{10,11... | collective-permute-start | bytes 393224 | tf_op jit(solution)/shard_map/ppermute | solution.py:500
  21.4 1.2 %collective-permute-start.3 = (bf16[4,64,256]{2,1,0:T(8,128)(2,1)S(1)}, bf16[4,64,256]{2,1,0:T(8,128)(2,1)S(1)}, u32[]{:S(2)}, u32[]{:S(2)}) collective-permute-start(bf16[4,64,256]{2,1,0:T(8,128)(2,1)S(1)} %get-tuple-element.38), channel_id=1, source_target_pairs={{0,2},{1,3},{2,0},{3,1},{4,6},{5,7},{6,4},{7,5},{8,10},{9,11},{10,... | collective-permute-start | bytes 393224 | tf_op jit(solution)/shard_map/ppermute | solution.py:500
  22.6 0.5 collective-permute-start.4
  23.1 0.0 copy-start.1
  23.1 0.0 copy-start.2
  23.1 0.0 copy-start.3
  23.1 0.0 copy-start.5
  23.1 0.0 copy-start.6
  23.1 0.0 copy-start.7
  23.1 4.2 %shard_map.123._.own = bf16[4,64,256]{2,1,0:T(8,128)(2,1)S(1)} custom-call(s32[16,16]{1,0:T(8,128)S(1)} %copy-done.4, bf16[48,128,256]{2,1,0:T(8,128)(2,1)S(1)} %get-tuple-element.35.far, bf16[48,64,256]{2,1,0:T(8,128)(2,1)S(1)} %get-tuple-element.36.vectors, bf16[17,256,128]{2,1,0:T(8,128)(2,1)S(1)} %get-tuple-element.33.near), custom_call_target="tpu_custom_call" | custom-call | flops 805306368 | bytes 5833728 | tf_op jit(solution)/shard_map/pallas_call | solution.py:210
  27.4 0.0 copy-done.1
  27.4 0.0 copy-done.2
  27.4 0.0 copy-done.3
  27.4 0.0 copy-done.5
  27.4 0.0 copy-done.6
  27.4 0.0 copy-done.7
  27.4 0.5 shard_map.124
  27.9 0.0 collective-permute-done.2.refs_0_
  27.9 1.2 %collective-permute-done.3.refs_1_ = bf16[4,64,256]{2,1,0:T(8,128)(2,1)S(1)} collective-permute-done((bf16[4,64,256]{2,1,0:T(8,128)(2,1)S(1)}, bf16[4,64,256]{2,1,0:T(8,128)(2,1)S(1)}, u32[]{:S(2)}, u32[]{:S(2)}) %collective-permute-start.3) | collective-permute-done | bytes 131104 | tf_op jit(solution)/shard_map/ppermute | solution.py:500
  29.1 1.1 %collective-permute-done.4.refs_2_ = bf16[4,64,256]{2,1,0:T(8,128)(2,1)S(1)} collective-permute-done((bf16[4,64,256]{2,1,0:T(8,128)(2,1)S(1)}, bf16[4,64,256]{2,1,0:T(8,128)(2,1)S(1)}, u32[]{:S(2)}, u32[]{:S(2)}) %collective-permute-start.4) | collective-permute-done | bytes 131104 | tf_op jit(solution)/shard_map/ppermute | solution.py:500
  30.2 2.0 %shard_map.125 = (f32[352,256]{1,0:T(8,128)S(1)}, f32[64,256]{1,0:T(8,128)S(1)}) custom-call(bf16[4,64,256]{2,1,0:T(8,128)(2,1)S(1)} %shard_map.123._.own, bf16[4,64,256]{2,1,0:T(8,128)(2,1)S(1)} %collective-permute-done.2.refs_0_, bf16[4,64,256]{2,1,0:T(8,128)(2,1)S(1)} %collective-permute-done.3.refs_1_, ...), custom_call_target="tpu_custom_call" | custom-call | bytes 884736 | tf_op jit(solution)/shard_map/pallas_call | solution.py:451
  32.2 1.8 %collective-permute-start.7 = (f32[64,256]{1,0:T(8,128)S(1)}, f32[64,256]{1,0:T(8,128)S(1)}, u32[]{:S(2)}, u32[]{:S(2)}) collective-permute-start(f32[64,256]{1,0:T(8,128)S(1)} %get-tuple-element.42.own), channel_id=1, source_target_pairs={{0,3},{1,2},{2,1},{3,0},{4,7},{5,6},{6,5},{7,4},{8,11},{9,10},{10,... | collective-permute-start | bytes 196616 | tf_op jit(solution)/shard_map/ppermute | solution.py:500
  34.0 0.7 %collective-permute-start.6 = (f32[64,256]{1,0:T(8,128)S(1)}, f32[64,256]{1,0:T(8,128)S(1)}, u32[]{:S(2)}, u32[]{:S(2)}) collective-permute-start(f32[64,256]{1,0:T(8,128)S(1)} %get-tuple-element.42.own), channel_id=1, source_target_pairs={{0,2},{1,3},{2,0},{3,1},{4,6},{5,7},{6,4},{7,5},{8,10},{9,11},{10,... | collective-permute-start | bytes 196616 | tf_op jit(solution)/shard_map/ppermute | solution.py:500
  34.7 1.1 %collective-permute-start.5 = (f32[64,256]{1,0:T(8,128)S(1)}, f32[64,256]{1,0:T(8,128)S(1)}, u32[]{:S(2)}, u32[]{:S(2)}) collective-permute-start(f32[64,256]{1,0:T(8,128)S(1)} %get-tuple-element.42.own), channel_id=1, source_target_pairs={{0,1},{1,0},{2,3},{3,2},{4,5},{5,4},{6,7},{7,6},{8,9},{9,8},{10,11... | collective-permute-start | bytes 196616 | tf_op jit(solution)/shard_map/ppermute | solution.py:500
  35.8 1.4 %collective-permute-start.12 = (f32[352,256]{1,0:T(8,128)S(1)}, f32[352,256]{1,0:T(8,128)S(1)}, u32[]{:S(2)}, u32[]{:S(2)}) collective-permute-start(f32[352,256]{1,0:T(8,128)S(1)} %get-tuple-element.50.refs_0_), channel_id=1, source_target_pairs={{0,2},{1,3},{2,0},{3,1},{4,6},{5,7},{6,4},{7,5},{8,10},{9,11},{10,... | collective-permute-start | bytes 1081352 | tf_op jit(solution)/shard_map/ppermute | solution.py:500
  37.2 0.9 %collective-permute-start.11 = (f32[352,256]{1,0:T(8,128)S(1)}, f32[352,256]{1,0:T(8,128)S(1)}, u32[]{:S(2)}, u32[]{:S(2)}) collective-permute-start(f32[352,256]{1,0:T(8,128)S(1)} %get-tuple-element.50.refs_0_), channel_id=1, source_target_pairs={{0,1},{1,0},{2,3},{3,2},{4,5},{5,4},{6,7},{7,6},{8,9},{9,8},{10,11... | collective-permute-start | bytes 1081352 | tf_op jit(solution)/shard_map/ppermute | solution.py:500
  38.1 0.0 collective-permute-done.7.refs_2_
  38.1 1.0 %collective-permute-done.6.refs_1_ = f32[64,256]{1,0:T(8,128)S(1)} collective-permute-done((f32[64,256]{1,0:T(8,128)S(1)}, f32[64,256]{1,0:T(8,128)S(1)}, u32[]{:S(2)}, u32[]{:S(2)}) %collective-permute-start.6) | collective-permute-done | bytes 65568 | tf_op jit(solution)/shard_map/ppermute | solution.py:500
  39.0 0.3 collective-permute-done.5.refs_0_
  39.3 1.2 %shard_map.126 = (f32[192,128]{1,0:T(8,128)S(1)}, f32[64,256]{1,0:T(8,128)S(1)}) custom-call(f32[64,256]{1,0:T(8,128)S(1)} %get-tuple-element.42.own, f32[64,256]{1,0:T(8,128)S(1)} %collective-permute-done.5.refs_0_, f32[64,256]{1,0:T(8,128)S(1)} %collective-permute-done.6.refs_1_, f32[64,256]{1,0:T(8,128)S(1)} %collective-permute-done.7.refs_2_, ...), custom_call_target="tpu_custom_call" | custom-call | bytes 360448 | tf_op jit(solution)/shard_map/pallas_call | solution.py:451
  40.6 0.1 collective-permute-start.8
  40.6 1.2 %collective-permute-done.8.arrived = f32[64,256]{1,0:T(8,128)S(1)} collective-permute-done((f32[64,256]{1,0:T(8,128)S(1)}, f32[64,256]{1,0:T(8,128)S(1)}, u32[]{:S(2)}, u32[]{:S(2)}) %collective-permute-start.8) | collective-permute-done | bytes 65568 | tf_op jit(solution)/shard_map/ppermute | solution.py:579
  41.9 0.5 shard_map.127
  42.4 1.9 %collective-permute-start.9 = (f32[64,256]{1,0:T(8,128)S(1)}, f32[64,256]{1,0:T(8,128)S(1)}, u32[]{:S(2)}, u32[]{:S(2)}) collective-permute-start(f32[64,256]{1,0:T(8,128)S(1)} %get-tuple-element.46.own), channel_id=1, source_target_pairs={{0,8},{4,12},{8,0},{12,4},{16,24},{20,28},{24,16},{28,20},{1,9},{5... | collective-permute-start | bytes 196616 | tf_op jit(solution)/shard_map/ppermute | solution.py:579
  44.2 2.4 %collective-permute-done.9.arrived = f32[64,256]{1,0:T(8,128)S(1)} collective-permute-done((f32[64,256]{1,0:T(8,128)S(1)}, f32[64,256]{1,0:T(8,128)S(1)}, u32[]{:S(2)}, u32[]{:S(2)}) %collective-permute-start.9) | collective-permute-done | bytes 65568 | tf_op jit(solution)/shard_map/ppermute | solution.py:579
  46.7 0.5 shard_map.128
  47.2 0.0 collective-permute-done.12.there.refs_2_
  47.2 0.0 collective-permute-done.11.here.refs_1_
  47.2 1.7 %collective-permute-start.13 = (f32[192,256]{1,0:T(8,128)S(1)}, f32[192,256]{1,0:T(8,128)S(1)}, u32[]{:S(2)}, u32[]{:S(2)}) collective-permute-start(f32[192,256]{1,0:T(8,128)S(1)} %get-tuple-element.51), channel_id=1, source_target_pairs={{0,2},{1,3},{2,0},{3,1},{4,6},{5,7},{6,4},{7,5},{8,10},{9,11},{10,... | collective-permute-start | bytes 589832 | tf_op jit(solution)/shard_map/ppermute | solution.py:500
  49.0 1.1 %collective-permute-start.14 = (f32[160,256]{1,0:T(8,128)S(1)}, f32[160,256]{1,0:T(8,128)S(1)}, u32[]{:S(2)}, u32[]{:S(2)}) collective-permute-start(f32[160,256]{1,0:T(8,128)S(1)} %get-tuple-element.52), channel_id=1, source_target_pairs={{0,1},{1,0},{2,3},{3,2},{4,5},{5,4},{6,7},{7,6},{8,9},{9,8},{10,11... | collective-permute-start | bytes 491528 | tf_op jit(solution)/shard_map/ppermute | solution.py:500
  50.0 3.1 %collective-permute-start.10 = (f32[64,256]{1,0:T(8,128)S(1)}, f32[64,256]{1,0:T(8,128)S(1)}, u32[]{:S(2)}, u32[]{:S(2)}) collective-permute-start(f32[64,256]{1,0:T(8,128)S(1)} %get-tuple-element.47._.own), channel_id=1, source_target_pairs={{0,16},{4,20},{8,24},{12,28},{16,0},{20,4},{24,8},{28,12},{1,17},{... | collective-permute-start | bytes 196616 | tf_op jit(solution)/shard_map/ppermute | solution.py:579
  53.1 1.1 %shard_map.130 = (f32[1024,256]{1,0:T(8,128)}, f32[960,128]{1,0:T(8,128)}) custom-call(f32[352,256]{1,0:T(8,128)S(1)} %get-tuple-element.50.refs_0_, f32[352,256]{1,0:T(8,128)S(1)} %collective-permute-done.11.here.refs_1_, f32[352,256]{1,0:T(8,128)S(1)} %collective-permute-done.12.there.refs_2_, f32[192,128]{1,0:T(8,128)S(1)} %get-tuple-element.53.refs_3_), custom_call_target="tpu_custom_call" | custom-call | flops 950000000 | bytes 1179648 | tf_op jit(solution)/shard_map/pallas_call | solution.py:451
  54.3 1.1 %collective-permute-done.10.arrived = f32[64,256]{1,0:T(8,128)S(1)} collective-permute-done((f32[64,256]{1,0:T(8,128)S(1)}, f32[64,256]{1,0:T(8,128)S(1)}, u32[]{:S(2)}, u32[]{:S(2)}) %collective-permute-start.10) | collective-permute-done | bytes 65568 | tf_op jit(solution)/shard_map/ppermute | solution.py:579
  55.4 0.0 collective-permute-done.14.refs_3_
  55.4 0.0 collective-permute-done.13.refs_2_
  55.4 1.7 %shard_map.131 = (f32[3,64,128]{2,1,0:T(8,128)}, f32[64,64]{1,0:T(8,128)}, f32[1024,256]{1,0:T(8,128)}, f32[960,128]{1,0:T(8,128)}) custom-call(f32[64,256]{1,0:T(8,128)S(1)} %get-tuple-element.47._.own, f32[64,256]{1,0:T(8,128)S(1)} %collective-permute-done.10.arrived, ...), custom_call_target="tpu_custom_call", output_to_operand_aliasing={{2}: (7, {}), {3}: (8, {})} | custom-call | flops 950000000 | bytes 2195456 | tf_op jit(solution)/shard_map/pallas_call | solution.py:451
  (2 shorter events, 0.1 us)
Async XLA Ops:
  1.4 1.0 %copy-start = (bf16[16,64,256]{2,1,0:T(8,128)(2,1)S(1)}, bf16[16,64,256]{2,1,0:T(8,128)(2,1)}, u32[]{:S(2)}) copy-start(bf16[16,64,256]{2,1,0:T(8,128)(2,1)} %probe.1) | copy-start | bytes 1572868
  2.5 11.8 %collective-permute-start.1 = (bf16[1072,256]{1,0:T(8,128)(2,1)S(1)}, bf16[1072,256]{1,0:T(8,128)(2,1)S(1)}, u32[]{:S(2)}, u32[]{:S(2)}) collective-permute-start(bf16[1072,256]{1,0:T(8,128)(2,1)S(1)} %shard_map.120.joined), channel_id=1, source_target_pairs={{4,8},{12,16},{20,24},{8,4},{16,12},{24,20},{5,9},{13,17},{21,25},... | collective-permute-start | bytes 1646600 | tf_op jit(solution)/shard_map/ppermute | solution.py:496
  3.2 11.1 %collective-permute-start = (bf16[1072,256]{1,0:T(8,128)(2,1)S(1)}, bf16[1072,256]{1,0:T(8,128)(2,1)S(1)}, u32[]{:S(2)}, u32[]{:S(2)}) collective-permute-start(bf16[1072,256]{1,0:T(8,128)(2,1)S(1)} %shard_map.120.joined), channel_id=1, source_target_pairs={{0,4},{8,12},{16,20},{24,28},{4,0},{12,8},{20,16},{28,24},{1,5},{9... | collective-permute-start | bytes 1646600 | tf_op jit(solution)/shard_map/ppermute | solution.py:496
  7.6 0.7 %copy-start.4 = (s32[16,16]{1,0:T(8,128)S(1)}, s32[16,16]{1,0:T(8,128)}, u32[]{:S(2)}) copy-start(s32[16,16]{1,0:T(8,128)} %nb_ref.5) | copy-start | bytes 3076
  19.3 8.6 %collective-permute-start.2 = (bf16[4,64,256]{2,1,0:T(8,128)(2,1)S(1)}, bf16[4,64,256]{2,1,0:T(8,128)(2,1)S(1)}, u32[]{:S(2)}, u32[]{:S(2)}) collective-permute-start(bf16[4,64,256]{2,1,0:T(8,128)(2,1)S(1)} %get-tuple-element.37), channel_id=1, source_target_pairs={{0,1},{1,0},{2,3},{3,2},{4,5},{5,4},{6,7},{7,6},{8,9},{9,8},{10,11... | collective-permute-start | bytes 393224 | tf_op jit(solution)/shard_map/ppermute | solution.py:500
  21.4 7.7 %collective-permute-start.3 = (bf16[4,64,256]{2,1,0:T(8,128)(2,1)S(1)}, bf16[4,64,256]{2,1,0:T(8,128)(2,1)S(1)}, u32[]{:S(2)}, u32[]{:S(2)}) collective-permute-start(bf16[4,64,256]{2,1,0:T(8,128)(2,1)S(1)} %get-tuple-element.38), channel_id=1, source_target_pairs={{0,2},{1,3},{2,0},{3,1},{4,6},{5,7},{6,4},{7,5},{8,10},{9,11},{10,... | collective-permute-start | bytes 393224 | tf_op jit(solution)/shard_map/ppermute | solution.py:500
  22.6 7.6 %collective-permute-start.4 = (bf16[4,64,256]{2,1,0:T(8,128)(2,1)S(1)}, bf16[4,64,256]{2,1,0:T(8,128)(2,1)S(1)}, u32[]{:S(2)}, u32[]{:S(2)}) collective-permute-start(bf16[4,64,256]{2,1,0:T(8,128)(2,1)S(1)} %get-tuple-element.39), channel_id=1, source_target_pairs={{0,3},{1,2},{2,1},{3,0},{4,7},{5,6},{6,5},{7,4},{8,11},{9,10},{10,... | collective-permute-start | bytes 393224 | tf_op jit(solution)/shard_map/ppermute | solution.py:500
  23.1 4.3 %copy-start.1 = (f32[16,64,64]{2,1,0:T(8,128)S(1)}, f32[16,64,64]{2,1,0:T(8,128)}, u32[]{:S(2)}) copy-start(f32[16,64,64]{2,1,0:T(8,128)} %leaf_inverse.1) | copy-start | bytes 786436
  23.1 4.3 %copy-start.2 = (f32[15,64,64]{2,1,0:T(8,128)S(1)}, f32[15,64,64]{2,1,0:T(8,128)}, u32[]{:S(2)}) copy-start(f32[15,64,64]{2,1,0:T(8,128)} %local_inverse.1) | copy-start | bytes 737284
  23.1 4.3 %copy-start.3 = (f32[7,64,64]{2,1,0:T(8,128)S(1)}, f32[7,64,64]{2,1,0:T(8,128)}, u32[]{:S(2)}) copy-start(f32[7,64,64]{2,1,0:T(8,128)} %upper_inverse.1) | copy-start | bytes 344068
  23.1 4.3 %copy-start.5 = (s32[16,64]{1,0:T(8,128)S(1)}, s32[16,64]{1,0:T(8,128)}, u32[]{:S(2)}) copy-start(s32[16,64]{1,0:T(8,128)} %leaf_pivots.1) | copy-start | bytes 12292
  23.1 4.3 %copy-start.6 = (s32[15,64]{1,0:T(8,128)S(1)}, s32[15,64]{1,0:T(8,128)}, u32[]{:S(2)}) copy-start(s32[15,64]{1,0:T(8,128)} %local_pivots.1) | copy-start | bytes 11524
  23.1 4.3 %copy-start.7 = (s32[7,64]{1,0:T(8,128)S(1)}, s32[7,64]{1,0:T(8,128)}, u32[]{:S(2)}) copy-start(s32[7,64]{1,0:T(8,128)} %upper_pivots.1) | copy-start | bytes 5380
  32.2 5.9 %collective-permute-start.7 = (f32[64,256]{1,0:T(8,128)S(1)}, f32[64,256]{1,0:T(8,128)S(1)}, u32[]{:S(2)}, u32[]{:S(2)}) collective-permute-start(f32[64,256]{1,0:T(8,128)S(1)} %get-tuple-element.42.own), channel_id=1, source_target_pairs={{0,3},{1,2},{2,1},{3,0},{4,7},{5,6},{6,5},{7,4},{8,11},{9,10},{10,... | collective-permute-start | bytes 196616 | tf_op jit(solution)/shard_map/ppermute | solution.py:500
  34.0 5.0 %collective-permute-start.6 = (f32[64,256]{1,0:T(8,128)S(1)}, f32[64,256]{1,0:T(8,128)S(1)}, u32[]{:S(2)}, u32[]{:S(2)}) collective-permute-start(f32[64,256]{1,0:T(8,128)S(1)} %get-tuple-element.42.own), channel_id=1, source_target_pairs={{0,2},{1,3},{2,0},{3,1},{4,6},{5,7},{6,4},{7,5},{8,10},{9,11},{10,... | collective-permute-start | bytes 196616 | tf_op jit(solution)/shard_map/ppermute | solution.py:500
  34.7 4.6 %collective-permute-start.5 = (f32[64,256]{1,0:T(8,128)S(1)}, f32[64,256]{1,0:T(8,128)S(1)}, u32[]{:S(2)}, u32[]{:S(2)}) collective-permute-start(f32[64,256]{1,0:T(8,128)S(1)} %get-tuple-element.42.own), channel_id=1, source_target_pairs={{0,1},{1,0},{2,3},{3,2},{4,5},{5,4},{6,7},{7,6},{8,9},{9,8},{10,11... | collective-permute-start | bytes 196616 | tf_op jit(solution)/shard_map/ppermute | solution.py:500
  35.8 11.4 %collective-permute-start.12 = (f32[352,256]{1,0:T(8,128)S(1)}, f32[352,256]{1,0:T(8,128)S(1)}, u32[]{:S(2)}, u32[]{:S(2)}) collective-permute-start(f32[352,256]{1,0:T(8,128)S(1)} %get-tuple-element.50.refs_0_), channel_id=1, source_target_pairs={{0,2},{1,3},{2,0},{3,1},{4,6},{5,7},{6,4},{7,5},{8,10},{9,11},{10,... | collective-permute-start | bytes 1081352 | tf_op jit(solution)/shard_map/ppermute | solution.py:500
  37.2 10.0 %collective-permute-start.11 = (f32[352,256]{1,0:T(8,128)S(1)}, f32[352,256]{1,0:T(8,128)S(1)}, u32[]{:S(2)}, u32[]{:S(2)}) collective-permute-start(f32[352,256]{1,0:T(8,128)S(1)} %get-tuple-element.50.refs_0_), channel_id=1, source_target_pairs={{0,1},{1,0},{2,3},{3,2},{4,5},{5,4},{6,7},{7,6},{8,9},{9,8},{10,11... | collective-permute-start | bytes 1081352 | tf_op jit(solution)/shard_map/ppermute | solution.py:500
  40.6 1.3 %collective-permute-start.8 = (f32[64,256]{1,0:T(8,128)S(1)}, f32[64,256]{1,0:T(8,128)S(1)}, u32[]{:S(2)}, u32[]{:S(2)}) collective-permute-start(f32[64,256]{1,0:T(8,128)S(1)} %get-tuple-element.44.own), channel_id=1, source_target_pairs={{0,4},{4,0},{8,12},{12,8},{16,20},{20,16},{24,28},{28,24},{1,5},{5... | collective-permute-start | bytes 196616 | tf_op jit(solution)/shard_map/ppermute | solution.py:579
  42.4 4.3 %collective-permute-start.9 = (f32[64,256]{1,0:T(8,128)S(1)}, f32[64,256]{1,0:T(8,128)S(1)}, u32[]{:S(2)}, u32[]{:S(2)}) collective-permute-start(f32[64,256]{1,0:T(8,128)S(1)} %get-tuple-element.46.own), channel_id=1, source_target_pairs={{0,8},{4,12},{8,0},{12,4},{16,24},{20,28},{24,16},{28,20},{1,9},{5... | collective-permute-start | bytes 196616 | tf_op jit(solution)/shard_map/ppermute | solution.py:579
  47.2 8.2 %collective-permute-start.13 = (f32[192,256]{1,0:T(8,128)S(1)}, f32[192,256]{1,0:T(8,128)S(1)}, u32[]{:S(2)}, u32[]{:S(2)}) collective-permute-start(f32[192,256]{1,0:T(8,128)S(1)} %get-tuple-element.51), channel_id=1, source_target_pairs={{0,2},{1,3},{2,0},{3,1},{4,6},{5,7},{6,4},{7,5},{8,10},{9,11},{10,... | collective-permute-start | bytes 589832 | tf_op jit(solution)/shard_map/ppermute | solution.py:500
  49.0 6.4 %collective-permute-start.14 = (f32[160,256]{1,0:T(8,128)S(1)}, f32[160,256]{1,0:T(8,128)S(1)}, u32[]{:S(2)}, u32[]{:S(2)}) collective-permute-start(f32[160,256]{1,0:T(8,128)S(1)} %get-tuple-element.52), channel_id=1, source_target_pairs={{0,1},{1,0},{2,3},{3,2},{4,5},{5,4},{6,7},{7,6},{8,9},{9,8},{10,11... | collective-permute-start | bytes 491528 | tf_op jit(solution)/shard_map/ppermute | solution.py:500
  50.0 5.4 %collective-permute-start.10 = (f32[64,256]{1,0:T(8,128)S(1)}, f32[64,256]{1,0:T(8,128)S(1)}, u32[]{:S(2)}, u32[]{:S(2)}) collective-permute-start(f32[64,256]{1,0:T(8,128)S(1)} %get-tuple-element.47._.own), channel_id=1, source_target_pairs={{0,16},{4,20},{8,24},{12,28},{16,0},{20,4},{24,8},{28,12},{1,17},{... | collective-permute-start | bytes 196616 | tf_op jit(solution)/shard_map/ppermute | solution.py:579
